TPU v7x, 128 devices: a whole 4x4x4 slice. The times are simulated.
128 devices in a mesh: dp: 2 (over core), member: 4 (over x), space: 16 (over y, z).
Axes of the slice: x: 4, y: 4, z: 4, core: 2. Of those that a mesh axis runs over, the one named last changes fastest.
Arguments:
- latents: bfloat16 [2, 8, 32768, 512], P('dp', 'member', 'space'), may hold values from -6 to 6
- edge_weight: bfloat16 [128, 4, 128, 128], P('space'), may hold values from -0.25 to 0.25
- block_ids: int32 [128, 4], P('space'), may hold values from 0 to 19, as said below
- block_count: int32 [128], P('space'), may hold values from 1 to 4, as said below
- w_in: bfloat16 [512, 512], replicated, may hold values from -0.25 to 0.25
- w_out: bfloat16 [83, 512], replicated, may hold values from -0.25 to 0.25
- targets: bfloat16 [2, 83, 16384], P('dp', None, 'space'), may hold values from -6 to 6
- area: float32 [16384], P('space'), may hold values from 0.2 to 2
- var_weight: float32 [83], replicated, may hold values from 0.2 to 2
Outputs:
- grad_latent: float32 [2, 8, 32768, 512], P('dp', 'member', 'space')
- grad_w_in: float32 [512, 512], P(('dp', 'member', 'space'))
- grad_w_out: float32 [83, 512], P(None, ('dp', 'member', 'space'))
Inputs may be any that keep to these rules, and one draw needn't show every extreme that they name: Slots k >= block_count[t] of a tile are padding; some tile has 4 live slots. `block_ids`: block numbers are counted in the tile's own space index's blocks extended by 2 blocks on each side. On every space index, the first slot of its first tile reads a block below its own and the first slot of its last tile a block above its own.
All inputs are finite; a program needn't handle non-finite values.
Results may differ from a plain program's by a relative error of at most 0.02.
Values may be sent and summed in bfloat16 or wider, within the bound.
No kernel may reach another device: no remote copies, remote signals or barrier semaphores. Data moves between devices by JAX's collectives and lax.ppermute only.
A program may use at most 128 MiB of HBM per device.

v0:
```python
import jax
import jax.numpy as jnp
from jax import lax
from jax.sharding import PartitionSpec as P

HALO_BLK = 2


smooth_width = 0.1


def with_halo(block, sides, width):
    for axis, dim in sides:
        count = lax.axis_size(axis)
        forward = [(i, i + 1) for i in range(count - 1)]
        backward = [(target, source) for source, target in forward]
        low = lax.ppermute(
            lax.slice_in_dim(block, block.shape[dim] - width, None, axis=dim), axis, forward
        )
        high = lax.ppermute(lax.slice_in_dim(block, 0, width, axis=dim), axis, backward)
        block = jnp.concatenate([low, block, high], axis=dim)
    return block


def passed_along(block, axis, distance):
    devices = range(lax.axis_size(axis))
    route = [(i - distance, i) for i in devices if i - distance in devices]
    return lax.ppermute(block, axis, route)


def crps_cotangent(own_fields, all_fields, target_part, cell_weight):
    ensemble_size = all_fields.shape[0]
    to_truth = own_fields - target_part[None]
    truth_term = (
        to_truth / jnp.sqrt(to_truth * to_truth + smooth_width * smooth_width) / ensemble_size
    )

    def add_pair(summed, member_field):
        spread_diff = own_fields - member_field[None]
        return (
            summed
            + spread_diff / jnp.sqrt(spread_diff * spread_diff + smooth_width * smooth_width),
            None,
        )

    spread_sum, _ = lax.scan(add_pair, jnp.zeros_like(own_fields), all_fields)
    result = cell_weight[None] * (truth_term - spread_sum / (ensemble_size * (ensemble_size - 1)))
    return result.astype(jnp.bfloat16)


def over_slots(slot_step, initial, slot_count):
    running = initial
    for slot_index in range(slot_count):
        running = slot_step(slot_index, running)
    return running


def local(latents, edge_weight, block_ids, block_count, w_in, w_out, targets, area, var_weight):
    members_here = latents.shape[1]
    feature_width = latents.shape[3]
    tile_count, slot_count, tile_cells, block_nodes = edge_weight.shape
    cell_count = tile_count * tile_cells
    live_slots = lax.broadcasted_iota(jnp.int32, (tile_count, slot_count), 1) < block_count[:, None]
    masked = edge_weight * live_slots[:, :, None, None].astype(jnp.bfloat16)
    own_blocks = latents[0].reshape(members_here, -1, block_nodes, feature_width)
    extended = with_halo(own_blocks, (("space", 1),), HALO_BLK)

    def forward_slot(slot_index, running):
        picked = jnp.take(extended, block_ids[:, slot_index], axis=1)
        weights_slot = masked[:, slot_index]
        return running + jnp.einsum(
            "tgj,mtjc->mtgc", weights_slot, picked, preferred_element_type=jnp.float32
        )

    start_latent = jnp.zeros((members_here, tile_count, tile_cells, feature_width), jnp.float32)
    grid_latent = over_slots(forward_slot, start_latent, slot_count).astype(jnp.bfloat16)
    grid_latent = grid_latent.reshape(members_here, cell_count, feature_width)
    pre_act = jnp.einsum("mnc,hc->mnh", grid_latent, w_in, preferred_element_type=jnp.float32)
    activated = jax.nn.gelu(pre_act).astype(jnp.bfloat16)
    fields = jnp.einsum("vh,mnh->mvn", w_out, activated, preferred_element_type=jnp.float32).astype(
        jnp.bfloat16
    )
    state_total = targets.shape[0] * lax.axis_size("dp")
    cell_weight = area[None, :] * var_weight[:, None] / state_total
    target_local = targets[0].astype(jnp.float32)
    all_members = lax.all_gather(fields, "member", axis=0, tiled=True).astype(jnp.float32)
    cotangent = crps_cotangent(fields.astype(jnp.float32), all_members, target_local, cell_weight)
    grad_act = jnp.einsum("mvn,vh->mnh", cotangent, w_out, preferred_element_type=jnp.float32)
    grad_pre = jax.vjp(jax.nn.gelu, pre_act)[1](grad_act)[0].astype(jnp.bfloat16)
    grad_out_local = jnp.einsum(
        "mvn,mnh->vh", cotangent, activated, preferred_element_type=jnp.float32
    )
    grad_in_local = jnp.einsum(
        "mnh,mnc->hc", grad_pre, grid_latent, preferred_element_type=jnp.float32
    )
    grad_grid = jnp.einsum(
        "mnh,hc->mnc", grad_pre, w_in, preferred_element_type=jnp.float32
    ).astype(jnp.bfloat16)
    grad_grid = grad_grid.reshape(members_here, tile_count, tile_cells, feature_width)

    def backward_slot(slot_index, running):
        weights_slot = masked[:, slot_index]
        contrib = jnp.einsum(
            "tgj,mtgc->mtjc", weights_slot, grad_grid, preferred_element_type=jnp.float32
        )
        return running.at[:, block_ids[:, slot_index]].add(contrib)

    start_grad = jnp.zeros(extended.shape, jnp.float32)
    block_grad = over_slots(backward_slot, start_grad, slot_count)
    lower_rim = block_grad[:, :HALO_BLK]
    upper_rim = block_grad[:, block_grad.shape[1] - HALO_BLK :]
    owned_grad = block_grad[:, HALO_BLK : block_grad.shape[1] - HALO_BLK]
    from_above = passed_along(lower_rim.astype(jnp.bfloat16), "space", -1).astype(lower_rim.dtype)
    from_below = passed_along(upper_rim.astype(jnp.bfloat16), "space", 1).astype(upper_rim.dtype)
    owned_grad = owned_grad.at[:, :HALO_BLK].add(from_below)
    owned_grad = owned_grad.at[:, owned_grad.shape[1] - HALO_BLK :].add(from_above)
    grad_latent = owned_grad.reshape(1, members_here, -1, feature_width)
    grad_w_in, grad_w_out = (
        lax.psum_scatter(grad_in_local, ("dp", "member", "space"), scatter_dimension=0, tiled=True),
        lax.psum_scatter(
            grad_out_local, ("dp", "member", "space"), scatter_dimension=1, tiled=True
        ),
    )
    return (grad_latent, grad_w_in, grad_w_out)


def solution(mesh):
    placed = (
        P("dp", "member", "space", None),
        P("space", None, None, None),
        P("space", None),
        P("space"),
        P(),
        P(),
        P("dp", None, "space"),
        P("space"),
        P(),
    )
    return jax.shard_map(
        local,
        mesh=mesh,
        in_specs=placed,
        out_specs=(
            P("dp", "member", "space", None),
            P(("dp", "member", "space"), None),
            P(None, ("dp", "member", "space")),
        ),
        check_vma=False,
    )
```

profile of v0, /device:TPU:0, one launch (start us, length us, event | category | flops | bytes accessed | tf_op | source)
XLA Modules:
  0.0 363.5 jit_solution(4544462700578452838)
XLA Ops:
  7.2 1.5 fusion.51
  8.7 4.1 %collective-permute-start = (bf16[2,2,128,512]{3,2,1,0:T(8,128)(2,1)S(1)}, bf16[2,2,128,512]{3,2,1,0:T(8,128)(2,1)S(1)}, u32[]{:S(2)}, u32[]{:S(2)}) collective-permute-start(bf16[2,2,128,512]{3,2,1,0:T(8,128)(2,1)S(1)} %get-tuple-element.86), channel_id=1, source_target_pairs={{0,1},{1,2},{2,3},{3,4},{4,5},{5,6},{6,7},{7,8},{8,9},{9,10},{10,1... | collective-permute-start | bytes 1572872 | tf_op jit(solution)/shard_map/ppermute | solution.py:17
  12.8 1.3 collective-permute-start.1
  14.1 0.8 compare_and_fusion.2
  15.0 0.7 fusion.41
  15.6 1.4 copy_multiply_fusion
  17.0 6.9 %collective-permute-done = bf16[2,2,128,512]{3,2,1,0:T(8,128)(2,1)S(1)} collective-permute-done((bf16[2,2,128,512]{3,2,1,0:T(8,128)(2,1)S(1)}, bf16[2,2,128,512]{3,2,1,0:T(8,128)(2,1)S(1)}, u32[]{:S(2)}, u32[]{:S(2)}) %collective-permute-start) | collective-permute-done | bytes 524320 | tf_op jit(solution)/shard_map/ppermute | solution.py:17
  23.9 4.3 %collective-permute-done.1 = bf16[2,2,128,512]{3,2,1,0:T(8,128)(2,1)S(1)} collective-permute-done((bf16[2,2,128,512]{3,2,1,0:T(8,128)(2,1)S(1)}, bf16[2,2,128,512]{3,2,1,0:T(8,128)(2,1)S(1)}, u32[]{:S(2)}, u32[]{:S(2)}) %collective-permute-start.1) | collective-permute-done | bytes 524320 | tf_op jit(solution)/shard_map/ppermute | solution.py:20
  28.2 3.0 pad_maximum_fusion
  31.2 4.5 %gather_fusion.1 = bf16[8,2,128,512]{3,2,1,0:T(8,128)(2,1)} fusion(bf16[2,20,128,512]{3,2,1,0:T(8,128)(2,1)} %pad_maximum_fusion, s32[1024]{0:T(1024)S(1)} %get-tuple-element.104), kind=kCustom, calls=%fused_computation.1.clone | custom fusion | bytes 4194336 | tf_op jit(solution)/shard_map/jit(_take)/gather | solution.py:69
  35.8 4.5 %gather_fusion = bf16[8,2,128,512]{3,2,1,0:T(8,128)(2,1)} fusion(bf16[2,20,128,512]{3,2,1,0:T(8,128)(2,1)} %pad_maximum_fusion, s32[1024]{0:T(1024)S(1)} %get-tuple-element.105), kind=kCustom, calls=%fused_computation.clone | custom fusion | bytes 4194336 | tf_op jit(solution)/shard_map/jit(_take)/gather | solution.py:69
  40.3 4.5 %gather_fusion.2 = bf16[8,2,128,512]{3,2,1,0:T(8,128)(2,1)} fusion(bf16[2,20,128,512]{3,2,1,0:T(8,128)(2,1)} %pad_maximum_fusion, s32[1024]{0:T(1024)S(1)} %get-tuple-element.103), kind=kCustom, calls=%fused_computation.2.clone | custom fusion | bytes 4194336 | tf_op jit(solution)/shard_map/jit(_take)/gather | solution.py:69
  44.7 4.5 %gather_fusion.3 = bf16[8,2,128,512]{3,2,1,0:T(8,128)(2,1)} fusion(bf16[2,20,128,512]{3,2,1,0:T(8,128)(2,1)} %pad_maximum_fusion, s32[1024]{0:T(1024)S(1)} %get-tuple-element.102), kind=kCustom, calls=%fused_computation.3.clone | custom fusion | bytes 4194336 | tf_op jit(solution)/shard_map/jit(_take)/gather | solution.py:69
  49.2 2.5 fusion.10
  51.8 0.8 fusion.12
  52.5 0.8 copy-done.7
  53.3 0.8 fusion.8
  54.3 1.3 fusion.22
  55.9 4.0 %multiply_convert_fusion = (bf16[2,1024,512]{2,1,0:T(8,128)(2,1)S(1)}, f32[2,1024,512]{2,1,0:T(8,128)}) fusion(bf16[2,1024,512]{2,1,0:T(8,128)(2,1)S(1)} %bitcast.115, bf16[512,512]{1,0:T(8,128)(2,1)S(1)} %copy-done), kind=kOutput, calls=%fused_computation.20 | convolution fusion | flops 1083179008 | bytes 8912896 | tf_op jit(solution)/shard_map/mnc,hc->mnh/dot_general | solution.py:78
  59.9 1.4 copy-done.5
  61.3 1.5 fusion.52
  63.0 0.9 multiply_multiply_fusion.2
  63.8 0.8 bitcast_convert_fusion
  64.6 26.5 %all-gather.2.cloned.1.call-done = bf16[8,83,1024]{2,1,0:T(8,128)(2,1)} async-done(((bf16[2,83,1024]{2,1,0:T(8,128)(2,1)}), bf16[8,83,1024]{2,1,0:T(8,128)(2,1)}) %all-gather.2.cloned.1.call-update) | async-done | bytes 1359888 | tf_op jit(solution)/shard_map/all_gather | solution.py:86
  91.1 3.3 convert_element_type.55
  94.4 11.8 %while.13 = (s32[]{:T(128)}, f32[2,83,1024]{2,1,0:T(8,128)S(1)}, f32[8,83,1024]{2,1,0:T(8,128)}, f32[2,83,1024]{2,1,0:T(8,128)S(1)}, s32[]{:T(128)}, /*index=5*/s32[]{:T(128)}) while((s32[]{:T(128)}, f32[2,83,1024]{2,1,0:T(8,128)S(1)}, f32[8,83,1024]{2,1,0:T(8,128)}, f32[2,83,1024]{2,1,0:T(8,128)S(1)}, s32[]{:T(128)}, ...), condition=%wide.region_1.3_spmd.clone, body=%wide.region_0.0_spmd.clone.sunk | while | flops 1019907 | bytes 3059795 | solution.py:46
  94.4 1.0 dynamic-slice_bitcast_fusion.2
  95.4 0.4 select_add_fusion.2
  95.9 1.0 dynamic-slice_bitcast_fusion.2
  96.9 0.4 select_add_fusion.2
  97.3 1.0 dynamic-slice_bitcast_fusion.2
  98.8 1.0 dynamic-slice_bitcast_fusion.2
  100.3 1.0 dynamic-slice_bitcast_fusion.2
  101.8 1.0 dynamic-slice_bitcast_fusion.2
  103.2 1.0 dynamic-slice_bitcast_fusion.2
  104.7 1.0 dynamic-slice_bitcast_fusion.2
  106.2 1.5 multiply_convert_fusion.1
  107.6 4.8 %fusion.6 = bf16[2,1024,512]{2,1,0:T(8,128)(2,1)S(1)} fusion(f32[2,1024,512]{2,1,0:T(8,128)} %get-tuple-element.99, bf16[2,83,1024]{2,1,0:T(8,128)(2,1)S(1)} %multiply_convert_fusion.1, bf16[83,512]{1,0:T(8,128)(2,1)S(1)} %copy-done.13), kind=kOutput, calls=%fused_computation.19 | convolution fusion | flops 195035136 | bytes 6716416 | tf_op jit(solution)/shard_map/mvn,vh->mnh/dot_general | solution.py:88
  112.4 1.3 copy-done.10
  113.8 1.2 convolution_convert_fusion
  115.0 2.8 convolution_bitcast_fusion.3
  117.9 2.8 convolution_bitcast_fusion.2
  120.7 2.8 convolution_bitcast_fusion.1
  123.5 2.8 convolution_bitcast_fusion
  126.3 5.4 %copy.34 = f32[8,2,128,512]{3,2,1,0:T(8,128)} copy(f32[8,2,128,512]{2,3,1,0:T(8,128)} %convolution_bitcast_fusion.3) | data formatting | bytes 8388608 | tf_op jit(solution)/shard_map/tgj,mtgc->mtjc/transpose | solution.py:103
  131.6 5.3 %copy.36 = f32[8,2,128,512]{3,2,1,0:T(8,128)} copy(f32[8,2,128,512]{2,3,1,0:T(8,128)} %convolution_bitcast_fusion.2) | data formatting | bytes 8388608 | tf_op jit(solution)/shard_map/tgj,mtgc->mtjc/transpose | solution.py:103
  137.0 5.3 %copy.38 = f32[8,2,128,512]{3,2,1,0:T(8,128)} copy(f32[8,2,128,512]{2,3,1,0:T(8,128)} %convolution_bitcast_fusion.1) | data formatting | bytes 8388608 | tf_op jit(solution)/shard_map/tgj,mtgc->mtjc/transpose | solution.py:103
  142.3 5.4 %copy.40 = f32[8,2,128,512]{3,2,1,0:T(8,128)} copy(f32[8,2,128,512]{2,3,1,0:T(8,128)} %convolution_bitcast_fusion) | data formatting | bytes 8388608 | tf_op jit(solution)/shard_map/tgj,mtgc->mtjc/transpose | solution.py:103
  147.7 5.4 %broadcast_in_dim.13 = f32[2,20,128,512]{3,2,1,0:T(8,128)} broadcast(f32[]{:T(128)} %constant.90.clone.1), dimensions={} | broadcast | bytes 10485764 | tf_op jit(solution)/shard_map/broadcast_in_dim | solution.py:108
  153.0 9.4 %scatter_fusion = f32[2,20,128,512]{3,2,1,0:T(8,128)} fusion(f32[2,20,128,512]{3,2,1,0:T(8,128)} %broadcast_in_dim.13, s32[8]{0:T(128)S(1)} %get-tuple-element.89, f32[8,2,128,512]{3,2,1,0:T(8,128)} %copy.34), kind=kCustom, calls=%fused_computation.4 | custom fusion | flops 1048576 | bytes 12582944 | tf_op jit(solution)/shard_map/scatter-add | solution.py:106
  162.5 9.5 %scatter_fusion.1 = f32[2,20,128,512]{3,2,1,0:T(8,128)} fusion(f32[2,20,128,512]{3,2,1,0:T(8,128)} %scatter_fusion, s32[8]{0:T(128)S(1)} %get-tuple-element.90, f32[8,2,128,512]{3,2,1,0:T(8,128)} %copy.36), kind=kCustom, calls=%fused_computation.5 | custom fusion | flops 1048576 | bytes 12582944 | tf_op jit(solution)/shard_map/scatter-add | solution.py:106
  172.0 9.4 %scatter_fusion.2 = f32[2,20,128,512]{3,2,1,0:T(8,128)} fusion(f32[2,20,128,512]{3,2,1,0:T(8,128)} %scatter_fusion.1, s32[8]{0:T(128)S(1)} %get-tuple-element.91, f32[8,2,128,512]{3,2,1,0:T(8,128)} %copy.38), kind=kCustom, calls=%fused_computation.6 | custom fusion | flops 1048576 | bytes 12582944 | tf_op jit(solution)/shard_map/scatter-add | solution.py:106
  181.4 9.5 %scatter_fusion.3 = f32[2,20,128,512]{3,2,1,0:T(8,128)} fusion(f32[2,20,128,512]{3,2,1,0:T(8,128)} %scatter_fusion.2, s32[8]{0:T(128)S(1)} %get-tuple-element.88, f32[8,2,128,512]{3,2,1,0:T(8,128)} %copy.40), kind=kCustom, calls=%fused_computation.7 | custom fusion | flops 1048576 | bytes 12582944 | tf_op jit(solution)/shard_map/scatter-add | solution.py:106
  190.9 4.9 %convert.5 = bf16[2,20,128,512]{3,2,1,0:T(8,128)(2,1)S(1)} convert(f32[2,20,128,512]{3,2,1,0:T(8,128)} %scatter_fusion.3) | non-fusion elementwise | flops 2621440 | bytes 15728640 | tf_op jit(solution)/shard_map/convert.2
  196.0 3.1 collective-permute-start.2
  199.0 1.3 collective-permute-start.3
  200.4 2.3 convolution_bitcast_fusion.4
  202.6 1.7 convolution_bitcast_fusion.5
  204.3 8.4 %slice.137 = f32[2,16,128,512]{3,2,1,0:T(8,128)} slice(f32[2,20,128,512]{3,2,1,0:T(8,128)} %scatter_fusion.3), slice={[0:2], [2:18], [0:128], [0:512]} | slice | bytes 16777216 | tf_op jit(solution)/shard_map/slice | solution.py:112
  212.8 2.4 fusion.31
  215.2 2.4 fusion.30
  217.5 136.6 %all-reduce.5.cloned.1.call-done = (f32[512,512]{1,0:T(8,128)}, f32[83,512]{0,1:T(8,128)}) async-done(((f32[512,512]{1,0:T(8,128)}, f32[83,512]{0,1:T(8,128)}), (f32[512,512]{1,0:T(8,128)}, f32[83,512]{0,1:T(8,128)})) %all-reduce.5.cloned.1.call-update) | async-done | bytes 1218576
  354.1 1.3 constant_dynamic-slice_fusion.1
  355.4 1.3 constant_dynamic-slice_fusion
  (49 shorter events, 3.2 us)
Async XLA Ops:
  7.2 48.7 %copy-start = (bf16[512,512]{1,0:T(8,128)(2,1)S(1)}, bf16[512,512]{1,0:T(8,128)(2,1)}, u32[]{:S(2)}) copy-start(bf16[512,512]{1,0:T(8,128)(2,1)} %param.21) | copy-start | bytes 1572868
  7.2 83.9 %all-gather.2.cloned.1.call-start = ((), (), s32[]{:S(2)}) async-start(), calls=%async_computation | async-start | bytes 1802240 | tf_op jit(solution)/shard_map/all_gather | solution.py:86
  7.2 21.0 %copy-start.9 = (bf16[1,2,2048,512]{3,2,1,0:T(8,128)(2,1)S(1)}, bf16[1,2,2048,512]{3,2,1,0:T(8,128)(2,1)}, u32[]{:S(2)}) copy-start(bf16[1,2,2048,512]{3,2,1,0:T(8,128)(2,1)} %param.17) | copy-start | bytes 12582916
  8.7 15.2 %collective-permute-start = (bf16[2,2,128,512]{3,2,1,0:T(8,128)(2,1)S(1)}, bf16[2,2,128,512]{3,2,1,0:T(8,128)(2,1)S(1)}, u32[]{:S(2)}, u32[]{:S(2)}) collective-permute-start(bf16[2,2,128,512]{3,2,1,0:T(8,128)(2,1)S(1)} %get-tuple-element.86), channel_id=1, source_target_pairs={{0,1},{1,2},{2,3},{3,4},{4,5},{5,6},{6,7},{7,8},{8,9},{9,10},{10,1... | collective-permute-start | bytes 1572872 | tf_op jit(solution)/shard_map/ppermute | solution.py:17
  12.8 15.4 %collective-permute-start.1 = (bf16[2,2,128,512]{3,2,1,0:T(8,128)(2,1)S(1)}, bf16[2,2,128,512]{3,2,1,0:T(8,128)(2,1)S(1)}, u32[]{:S(2)}, u32[]{:S(2)}) collective-permute-start(bf16[2,2,128,512]{3,2,1,0:T(8,128)(2,1)S(1)} %get-tuple-element.87), channel_id=1, source_target_pairs={{1,0},{2,1},{3,2},{4,3},{5,4},{6,5},{7,6},{8,7},{9,8},{10,9},{11,1... | collective-permute-start | bytes 1572872 | tf_op jit(solution)/shard_map/ppermute | solution.py:20
  49.2 2.5 copy-start.8
  51.7 1.6 copy-start.7
  52.5 1.7 copy-start.2
  55.8 4.1 %copy-start.3 = (bf16[2,8,128,512]{3,2,1,0:T(8,128)(2,1)}, bf16[2,8,128,512]{3,2,1,0:T(8,128)(2,1)S(1)}, u32[]{:S(2)}) copy-start(bf16[2,8,128,512]{3,2,1,0:T(8,128)(2,1)S(1)} %copy.32) | copy-start | bytes 6291460
  55.8 5.5 %copy-start.13 = (bf16[83,512]{1,0:T(8,128)(2,1)S(1)}, bf16[83,512]{1,0:T(8,128)(2,1)}, u32[]{:S(2)}) copy-start(bf16[83,512]{1,0:T(8,128)(2,1)} %param.22) | copy-start | bytes 254980
  55.8 7.1 %copy-start.14 = (s32[8,4]{0,1:T(4,128)S(1)}, s32[8,4]{0,1:T(4,128)}, u32[]{:S(2)}) copy-start(s32[8,4]{0,1:T(4,128)} %param.19) | copy-start | bytes 388
  55.9 7.1 %copy-start.15 = (f32[1024]{0:T(1024)S(1)}, f32[1024]{0:T(1024)}, u32[]{:S(2)}) copy-start(f32[1024]{0:T(1024)} %param.24) | copy-start | bytes 12292
  55.9 7.1 %copy-start.16 = (f32[83]{0:T(128)S(1)}, f32[83]{0:T(128)}, u32[]{:S(2)}) copy-start(f32[83]{0:T(128)} %param.25) | copy-start | bytes 1000
  55.9 7.9 %copy-start.12 = (bf16[1,83,1024]{2,1,0:T(8,128)(2,1)S(1)}, bf16[1,83,1024]{2,1,0:T(8,128)(2,1)}, u32[]{:S(2)}) copy-start(bf16[1,83,1024]{2,1,0:T(8,128)(2,1)} %param.23) | copy-start | bytes 509956
  59.9 1.4 copy-start.5
  62.8 291.3 %all-reduce.5.cloned.1.call-start = ((), (), s32[]{:S(2)}) async-start(), calls=%async_computation.1 | async-start | bytes 2621440
  112.4 1.3 copy-start.10
  190.9 9.4 %copy-start.4 = (bf16[2,8,128,512]{3,2,1,0:T(8,128)(2,1)S(1)}, bf16[2,8,128,512]{3,2,1,0:T(8,128)(2,1)}, u32[]{:S(2)}) copy-start(bf16[2,8,128,512]{3,2,1,0:T(8,128)(2,1)} %copy-done.3) | copy-start | bytes 6291460
  190.9 9.5 %copy-start.11 = (bf16[2,1024,512]{2,1,0:T(8,128)(2,1)S(1)}, bf16[2,1024,512]{2,1,0:T(8,128)(2,1)}, u32[]{:S(2)}) copy-start(bf16[2,1024,512]{2,1,0:T(8,128)(2,1)} %copy-done.10) | copy-start | bytes 6291460
  195.9 6.8 %copy-start.6 = (bf16[2,1024,512]{2,1,0:T(8,128)(2,1)S(1)}, bf16[2,1024,512]{2,1,0:T(8,128)(2,1)}, u32[]{:S(2)}) copy-start(bf16[2,1024,512]{2,1,0:T(8,128)(2,1)} %copy-done.5) | copy-start | bytes 6291460
  196.0 16.8 %collective-permute-start.2 = (bf16[2,2,128,512]{3,2,1,0:T(8,128)(2,1)S(1)}, bf16[2,2,128,512]{3,2,1,0:T(8,128)(2,1)S(1)}, u32[]{:S(2)}, u32[]{:S(2)}) collective-permute-start(bf16[2,2,128,512]{3,2,1,0:T(8,128)(2,1)S(1)} %get-tuple-element.85), channel_id=1, source_target_pairs={{0,1},{1,2},{2,3},{3,4},{4,5},{5,6},{6,7},{7,8},{8,9},{9,10},{10,1... | collective-permute-start | bytes 1572872 | tf_op jit(solution)/shard_map/ppermute | solution.py:28
  199.0 16.1 %collective-permute-start.3 = (bf16[2,2,128,512]{3,2,1,0:T(8,128)(2,1)S(1)}, bf16[2,2,128,512]{3,2,1,0:T(8,128)(2,1)S(1)}, u32[]{:S(2)}, u32[]{:S(2)}) collective-permute-start(bf16[2,2,128,512]{3,2,1,0:T(8,128)(2,1)S(1)} %get-tuple-element.84), channel_id=1, source_target_pairs={{1,0},{2,1},{3,2},{4,3},{5,4},{6,5},{7,6},{8,7},{9,8},{10,9},{11,1... | collective-permute-start | bytes 1572872 | tf_op jit(solution)/shard_map/ppermute | solution.py:28
  204.3 152.4 %copy-start.1 = (bf16[512,512]{1,0:T(8,128)(2,1)S(1)}, bf16[512,512]{1,0:T(8,128)(2,1)}, u32[]{:S(2)}) copy-start(bf16[512,512]{1,0:T(8,128)(2,1)} %param.21) | copy-start | bytes 1572868
Sparse Core Ops, SparseCore 0:
  63.0 28.0 all-gather.1
  204.4 149.6 all-reduce.4
where the time goes:
time: 366 us; the launch traced here: 364 us
  waiting for transfers between devices  174 us (48%)
  local copies, waits for them, and re-layouts  69.3 us (19%)
  other arithmetic  63.3 us (17%)
  matrix products  32.2 us (9%)
  between operations  14.4 us (4%)
  starting transfers between devices  9.82 us (3%)
    unnamed x3, waiting for transfers between devices  137 us
    scatter-add x4, other arithmetic, backward_slot(): return running.at[:, block_ids[:, slot_index]].add(contrib)  37.9 us
    all_gather x1, waiting for transfers between devices, local(): lax.all_gather(fields, 'member', axis=0, tiled=True).astype(jnp.float32)  26.5 us
    transpose x4, local copies, waits for them, and re-layouts, backward_slot(): jnp.einsum('tgj,mtgc->mtjc', weights_slot, grad_grid, preferred_element_t...  21.4 us
    gather x4, local copies, waits for them, and re-layouts, forward_slot(): picked = jnp.take(extended, block_ids[:, slot_index], axis=1)  18 us
    dot_general x4, matrix products, backward_slot(): jnp.einsum('tgj,mtgc->mtjc', weights_slot, grad_grid, preferred_element_t...  11.3 us
    slice x1, local copies, waits for them, and re-layouts, local(): owned_grad = block_grad[:, HALO_BLK:block_grad.shape[1] - HALO_BLK]  8.43 us
    sub x8, local copies, waits for them, and re-layouts, add_pair(): spread_diff = own_fields - member_field[None]  8.1 us
  transfers between devices with their start and end apart: 6, of which 4 were waited for; matrix products, arithmetic and copies ran while one was open for 6% of the time, Pallas kernels for 0%

commit v1 on v0

v1 whole, which is shorter than its diff:
```python
import functools

import jax
import jax.numpy as jnp
from jax import lax
from jax.experimental import pallas as pl
from jax.experimental.pallas import tpu as pltpu
from jax.sharding import PartitionSpec as P

HALO = 2
lat_blocks = 16
smooth_square = 0.1 * 0.1
MIB = 1 << 20
f32 = jnp.float32
bf16 = jnp.bfloat16

NN = (((1,), (0,)), ((), ()))
NT = (((1,), (1,)), ((), ()))


def dot(a, b, dims=NN):
    return lax.dot_general(a, b, dims, preferred_element_type=f32)


def whole(memory_space=pltpu.VMEM):
    return pl.BlockSpec(memory_space=memory_space)


def smem():
    return pl.BlockSpec(memory_space=pltpu.SMEM)


def cost(flops, moved, transcendentals=0):
    return pl.CostEstimate(flops=flops, bytes_accessed=moved, transcendentals=transcendentals)


def params(mib):
    return pltpu.CompilerParams(vmem_limit_bytes=mib * MIB)


def shape(dims, dtype):
    return jax.ShapeDtypeStruct(dims, dtype)


def own_part_kernel(ids, count, lat, weight, w_in, w_out, acc, weight_t, w_in_t, w_out_t):
    members, blocks = lat.shape[0], lat.shape[1]
    tiles, slots = weight.shape[0], weight.shape[1]

    def tile(t, carry):
        parts, at = [], []
        for k in range(slots):
            e = ids[t, k]
            mine = (k < count[t]) & (e >= HALO) & (e < HALO + blocks)
            w = weight[t, k]
            weight_t[t, k] = w.T
            parts.append(jnp.where(mine, w, jnp.zeros_like(w)))
            at.append(jnp.clip(e - HALO, 0, blocks - 1))
        lhs = jnp.concatenate(parts, axis=1)
        for m in range(members):
            rhs = jnp.concatenate([lat[m, a] for a in at], axis=0)
            acc[m, t] = dot(lhs, rhs)
        return carry

    lax.fori_loop(0, tiles, tile, 0)
    w_in_t[...] = w_in[...].T
    w_out_t[...] = w_out[...].T


def gelu_parts(x):
    scale = 0.7978845608028654
    square = x * x
    half = 0.5 + 0.5 * jnp.tanh(x * (scale + (scale * 0.044715) * square))
    return square, half


def fields_kernel(ids, count, acc, low, high, weight, w_in, w_out, lat_out, fields, total):
    t = pl.program_id(0)
    members, slots = acc.shape[0], weight.shape[1]
    total[...] = acc[:, 0]
    for k in range(slots):
        e = ids[t, k]
        live = k < count[t]

        @pl.when(live & (e < HALO))
        def _():
            w = weight[0, k]
            for m in range(members):
                total[m] += dot(w, low[m, e])

        upper = e - (HALO + lat_blocks)

        @pl.when(live & (upper >= 0))
        def _():
            w = weight[0, k]
            for m in range(members):
                total[m] += dot(w, high[m, upper])

    rounded = total[...].astype(bf16)
    lat_out[...] = rounded
    cells = rounded.shape[1]
    pre = dot(w_in[...], rounded.reshape(members * cells, -1), NT)
    _, half = gelu_parts(pre)
    out = dot(w_out[...], (pre * half).astype(bf16))
    for m in range(members):
        fields[m] = out[:, m * cells : (m + 1) * cells].astype(bf16)


def slopes_kernel(lat, w_in, act_t, slope_t):
    members, cells = lat.shape[0], lat.shape[1]
    x = dot(w_in[...], lat[...].reshape(members * cells, -1), NT)
    square, half = gelu_parts(x)
    scale = 0.7978845608028654
    act = (x * half).astype(bf16)
    inner = x * (2.0 * scale + (6.0 * scale * 0.044715) * square)
    slope = (half + half * (1.0 - half) * inner).astype(bf16)
    for m in range(members):
        act_t[m] = act[:, m * cells : (m + 1) * cells]
        slope_t[m] = slope[:, m * cells : (m + 1) * cells]


def smooth_sign(u):
    return u * lax.rsqrt(u * u + smooth_square)


def weights_kernel(
    place, own, other1, other2, other3, target, area, var_weight, act_t, slope_t, lat, w_out_t,
    grad_pre, keep, send, total_in, total_out, *, ensemble, states,
):
    step = pl.program_id(0)
    members = own.shape[0]
    truth = target[...].astype(f32)
    mine = [own[m].astype(f32) for m in range(members)]
    spread = [jnp.zeros_like(truth) for _ in mine]
    for a in range(members):
        for b in range(a + 1, members):
            d = smooth_sign(mine[a] - mine[b])
            spread[a] += d
            spread[b] -= d
    for other in (other1, other2, other3):
        for b in range(members):
            theirs = other[b].astype(f32)
            for a in range(members):
                spread[a] += smooth_sign(mine[a] - theirs)
    cell_weight = area[...] * var_weight[...] * (1.0 / states)
    cots = []
    for m in range(members):
        value = smooth_sign(mine[m] - truth) * (1.0 / ensemble)
        value = value - spread[m] * (1.0 / (ensemble * (ensemble - 1)))
        cots.append((cell_weight * value).astype(bf16))
    cot = jnp.concatenate(cots, axis=1)
    width = cots[0].shape[1]
    grad_act = dot(w_out_t[...], cot)
    act = jnp.concatenate([act_t[m] for m in range(members)], axis=1)
    slope = jnp.concatenate([slope_t[m] for m in range(members)], axis=1)
    pre = (grad_act * slope.astype(f32)).astype(bf16)
    for m in range(members):
        grad_pre[m] = pre[:, m * width : (m + 1) * width]
    part_in = dot(pre, lat[...].reshape(members * width, -1))
    part_out = dot(act, cot, NT)

    @pl.when(step == 0)
    def _():
        total_in[...] = part_in
        total_out[:, : part_out.shape[1]] = part_out
        total_out[:, part_out.shape[1] :] = jnp.zeros(
            (part_out.shape[0], total_out.shape[1] - part_out.shape[1]), f32
        )

    @pl.when(step > 0)
    def _():
        total_in[...] += part_in
        total_out[:, : part_out.shape[1]] += part_out

    @pl.when(step == pl.num_programs(0) - 1)
    def _():
        rows = keep.shape[0]
        wide = total_in.shape[1]
        stay = pl.multiple_of(place[0] * rows, rows)
        leave = pl.multiple_of((1 - place[0]) * rows, rows)
        keep[:, :wide] = total_in[pl.ds(stay, rows)]
        keep[:, wide:] = total_out[pl.ds(stay, rows)]
        send[:, :wide] = total_in[pl.ds(leave, rows)].astype(bf16)
        send[:, wide:] = total_out[pl.ds(leave, rows)].astype(bf16)


def rim_kernel(ids, count, grad_pre, weight_t, w_in_t, grad_grid, low, high, total):
    t = pl.program_id(0)
    members, cells = grad_pre.shape[0], grad_pre.shape[2]
    slots = weight_t.shape[1]

    @pl.when(t == 0)
    def _():
        total[...] = jnp.zeros_like(total)

    both = jnp.concatenate([grad_pre[m] for m in range(members)], axis=1)
    grid = dot(w_in_t[...], both).astype(bf16)
    for m in range(members):
        grad_grid[m] = grid[:, m * cells : (m + 1) * cells]
    for k in range(slots):
        e = ids[t, k]
        outside = (e < HALO) | (e >= HALO + lat_blocks)
        slot = jnp.where(e < HALO, e, e - lat_blocks)

        @pl.when((k < count[t]) & outside)
        def _():
            w = weight_t[0, k]
            for m in range(members):
                total[slot, m] += dot(w, grad_grid[m], NT)

    @pl.when(t == pl.num_programs(0) - 1)
    def _():
        for m in range(members):
            for e in range(HALO):
                low[m, e] = total[e, m].astype(bf16)
                high[m, e] = total[HALO + e, m].astype(bf16)


def owned_kernel(ids, count, grad_grid, weight_t, out):
    members, tiles = out.shape[0], weight_t.shape[0]
    slots, cells = weight_t.shape[1], weight_t.shape[3]
    blocks = out.shape[1]

    def clear(b, carry):
        for m in range(members):
            out[m, b] = jnp.zeros(out.shape[2:], f32)
        return carry

    lax.fori_loop(0, blocks, clear, 0)

    def tile(t, carry):
        at = pl.ds(pl.multiple_of(t * cells, cells), cells)
        for k in range(slots):
            e = ids[t, k] - HALO

            @pl.when((k < count[t]) & (e >= 0) & (e < blocks))
            def _():
                w = weight_t[t, k]
                for m in range(members):
                    out[m, e] += dot(w, grad_grid[m, :, at], NT)

        return carry

    lax.fori_loop(0, tiles, tile, 0)


def add_rim_kernel(base, below, above, out):
    side = pl.program_id(0)

    @pl.when(side == 0)
    def _():
        out[...] = base[...] + below[...].astype(f32)

    @pl.when(side == 1)
    def _():
        out[...] = base[...] + above[...].astype(f32)


def split_kernel(place, kept, *refs, which, received):
    got, outs = refs[:received], refs[received : received + 4]
    total = refs[received + 4]
    value = kept[...]
    for r in got:
        value = value + r[...].astype(f32)
    parts = total.shape[0]
    rows = total.shape[1]
    for p in range(parts):
        total[p] = value[p * rows : (p + 1) * rows]
    here = place[which]
    for d in range(parts):
        outs[d][...] = total[lax.rem(here + d, parts)].astype(outs[d].dtype)


def split(place, which, kept, got, dtype):
    parts = 4
    rows, wide = kept.shape[0] // parts, kept.shape[1]
    return pl.pallas_call(
        functools.partial(split_kernel, which=which, received=len(got)),
        in_specs=[smem()] + [whole()] * (1 + len(got)),
        out_specs=[whole()] * parts,
        out_shape=[shape((rows, wide), f32)] + [shape((rows, wide), dtype)] * (parts - 1),
        scratch_shapes=[pltpu.VMEM((parts, rows, wide), f32)],
        compiler_params=params(8),
        cost_estimate=cost(kept.size, kept.size * 8),
    )(place, kept, *got)


def finish_kernel(kept, got1, got2, got3, grad_in, grad_out):
    value = kept[...] + got1[...] + got2[...] + got3[...]
    wide = grad_in.shape[1]
    grad_in[...] = value[:, :wide]
    turned = value[:, wide:].T
    grad_out[...] = turned[: grad_out.shape[0]]


def shift(count, distance):
    return [(i, (i + distance) % count) for i in range(count)]


def shift_y(side_y, side_z, distance):
    return [
        (y * side_z + z, (y + distance) % side_y * side_z + z)
        for y in range(side_y)
        for z in range(side_z)
    ]


def shift_z(side_y, side_z, distance):
    return [
        (y * side_z + z, y * side_z + (z + distance) % side_z)
        for y in range(side_y)
        for z in range(side_z)
    ]


def local(latents, edge_weight, block_ids, block_count, w_in, w_out, targets, area, var_weight):
    members = latents.shape[1]
    feature = latents.shape[3]
    hidden = w_in.shape[0]
    variables = w_out.shape[0]
    rows_v = (variables + 7) // 8 * 8
    tiles, slots, cells, nodes = edge_weight.shape
    count_cells = tiles * cells
    lat = latents[0].reshape(members, -1, nodes, feature)
    blocks = lat.shape[1]
    space = lax.axis_size("space")
    side = 4
    at_space = lax.axis_index("space")
    place = jnp.stack(
        [lax.axis_index("dp"), lax.axis_index("member"), at_space // side, at_space % side]
    ).astype(jnp.int32)

    up = [(i, i + 1) for i in range(space - 1)]
    down = [(i + 1, i) for i in range(space - 1)]
    low = lax.ppermute(lat[:, blocks - HALO :], "space", up)
    high = lax.ppermute(lat[:, :HALO], "space", down)

    w_out_pad = jnp.pad(w_out, ((0, rows_v - variables), (0, 0)))
    target = jnp.pad(targets[0], ((0, rows_v - variables), (0, 0)))
    scale_v = jnp.pad(var_weight, (0, rows_v - variables))[:, None]
    scale_n = area[None, :]

    acc, weight_t, w_in_t, w_out_t = pl.pallas_call(
        own_part_kernel,
        in_specs=[smem(), smem()] + [whole()] * 4,
        out_specs=[whole()] * 4,
        out_shape=[
            shape((members, tiles, cells, feature), f32),
            shape((tiles, slots, nodes, cells), bf16),
            shape((feature, hidden), bf16),
            shape((hidden, rows_v), bf16),
        ],
        compiler_params=params(24),
        cost_estimate=cost(2 * tiles * slots * cells * nodes * feature * members, 10 * MIB),
    )(block_ids, block_count, lat, edge_weight, w_in, w_out_pad)

    lat_spec = pl.BlockSpec((members, cells, feature), lambda t: (0, t, 0))
    col_spec = pl.BlockSpec((members, hidden, cells), lambda t: (0, 0, t))
    grid_latent, fields = pl.pallas_call(
        fields_kernel,
        grid=(tiles,),
        in_specs=[
            smem(),
            smem(),
            pl.BlockSpec((members, 1, cells, feature), lambda t: (0, t, 0, 0)),
            whole(),
            whole(),
            pl.BlockSpec((1, slots, cells, nodes), lambda t: (t, 0, 0, 0)),
            whole(),
            whole(),
        ],
        out_specs=[lat_spec, pl.BlockSpec((members, rows_v, cells), lambda t: (0, 0, t))],
        out_shape=[
            shape((members, count_cells, feature), bf16),
            shape((members, rows_v, count_cells), bf16),
        ],
        scratch_shapes=[pltpu.VMEM((members, cells, feature), f32)],
        compiler_params=params(16),
        cost_estimate=cost(2 * members * count_cells * feature * hidden, 8 * MIB),
    )(block_ids, block_count, acc, low, high, edge_weight, w_in, w_out_pad)

    ring = lax.axis_size("member")
    others = [lax.ppermute(fields, "member", shift(ring, d)) for d in (1, 3, 2)]

    act_t, slope_t = pl.pallas_call(
        slopes_kernel,
        grid=(tiles,),
        in_specs=[lat_spec, whole()],
        out_specs=[col_spec, col_spec],
        out_shape=[shape((members, hidden, count_cells), bf16)] * 2,
        compiler_params=params(16),
        cost_estimate=cost(2 * members * count_cells * feature * hidden, 8 * MIB),
    )(grid_latent, w_in)

    width = 2 * cells
    wide = feature + 128
    field_spec = pl.BlockSpec((members, rows_v, width), lambda t: (0, 0, t))
    wide_spec = pl.BlockSpec((members, hidden, width), lambda t: (0, 0, t))
    half_rows = hidden // 2
    grad_pre, keep, send = pl.pallas_call(
        functools.partial(
            weights_kernel, ensemble=members * ring, states=targets.shape[0] * lax.axis_size("dp")
        ),
        grid=(count_cells // width,),
        in_specs=[
            smem(),
            field_spec,
            field_spec,
            field_spec,
            field_spec,
            pl.BlockSpec((rows_v, width), lambda t: (0, t)),
            pl.BlockSpec((1, width), lambda t: (0, t)),
            whole(),
            wide_spec,
            wide_spec,
            pl.BlockSpec((members, width, feature), lambda t: (0, t, 0)),
            whole(),
        ],
        out_specs=[wide_spec, whole(), whole()],
        out_shape=[
            shape((members, hidden, count_cells), bf16),
            shape((half_rows, wide), f32),
            shape((half_rows, wide), bf16),
        ],
        scratch_shapes=[pltpu.VMEM((hidden, feature), f32), pltpu.VMEM((hidden, 128), f32)],
        compiler_params=params(24),
        cost_estimate=cost(2 * members * count_cells * feature * hidden, 8 * MIB),
    )(place, fields, *others, target, scale_n, scale_v, act_t, slope_t, grid_latent, w_out_t)

    swapped = lax.ppermute(send, "dp", [(0, 1), (1, 0)])

    grad_grid, rim_low, rim_high = pl.pallas_call(
        rim_kernel,
        grid=(tiles,),
        in_specs=[
            smem(),
            smem(),
            col_spec,
            pl.BlockSpec((1, slots, nodes, cells), lambda t: (t, 0, 0, 0)),
            whole(),
        ],
        out_specs=[col_spec, whole(), whole()],
        out_shape=[
            shape((members, feature, count_cells), bf16),
            shape((members, HALO, nodes, feature), bf16),
            shape((members, HALO, nodes, feature), bf16),
        ],
        scratch_shapes=[pltpu.VMEM((2 * HALO, members, nodes, feature), f32)],
        compiler_params=params(16),
        cost_estimate=cost(2 * members * count_cells * feature * hidden, 6 * MIB),
    )(block_ids, block_count, grad_pre, weight_t, w_in_t)

    from_below = lax.ppermute(rim_high, "space", up)
    from_above = lax.ppermute(rim_low, "space", down)

    owned = pl.pallas_call(
        owned_kernel,
        in_specs=[smem(), smem(), whole(), whole()],
        out_specs=whole(),
        out_shape=shape((members, blocks, nodes, feature), f32),
        compiler_params=params(24),
        cost_estimate=cost(2 * tiles * slots * cells * nodes * feature * members, 12 * MIB),
    )(block_ids, block_count, grad_grid, weight_t)

    kept, *sends = split(place, 1, keep, [swapped], bf16)
    got = [
        lax.ppermute(s, "member", shift(ring, d)) for d, s in zip((1, 2, 3), sends)
    ]
    kept, *sends = split(place, 2, kept, got, f32)
    got = [lax.ppermute(s, "space", shift_y(side, side, d)) for d, s in zip((1, 2, 3), sends)]
    kept, *sends = split(place, 3, kept, got, f32)
    got = [lax.ppermute(s, "space", shift_z(side, side, d)) for d, s in zip((1, 2, 3), sends)]
    grad_w_in, grad_w_out = pl.pallas_call(
        finish_kernel,
        in_specs=[whole()] * 4,
        out_specs=[whole()] * 2,
        out_shape=[
            shape((kept.shape[0], feature), f32),
            shape((variables, kept.shape[0]), f32),
        ],
        compiler_params=params(8),
    )(kept, *got)

    rim_spec = pl.BlockSpec((1, HALO, nodes, feature), lambda s, m: (m, 0, 0, 0))
    last = blocks // HALO - 1
    edge_spec = pl.BlockSpec((1, HALO, nodes, feature), lambda s, m: (m, s * last, 0, 0))
    grad_latent = pl.pallas_call(
        add_rim_kernel,
        grid=(2, members),
        in_specs=[edge_spec, rim_spec, rim_spec],
        out_specs=edge_spec,
        out_shape=shape(owned.shape, f32),
        input_output_aliases={0: 0},
        compiler_params=params(16),
    )(owned, from_below, from_above)
    return (
        grad_latent.reshape(1, members, blocks * nodes, feature),
        grad_w_in,
        grad_w_out,
    )


def solution(mesh):
    placed = (
        P("dp", "member", "space", None),
        P("space", None, None, None),
        P("space", None),
        P("space"),
        P(),
        P(),
        P("dp", None, "space"),
        P("space"),
        P(),
    )
    return jax.shard_map(
        local,
        mesh=mesh,
        in_specs=placed,
        out_specs=(
            P("dp", "member", "space", None),
            P(("dp", "member", "space"), None),
            P(None, ("dp", "member", "space")),
        ),
        check_vma=False,
    )
```

time: 366 us -> 112 us (0.31)
  waiting for transfers between devices: 174 us -> 14.8 us
  other arithmetic: 63.3 us -> 0.08 us
  local copies, waits for them, and re-layouts: 69.3 us -> 13.9 us
  Pallas kernels: 0 us -> 45.9 us
  matrix products: 32.2 us -> 0 us
  starting transfers between devices: 9.82 us -> 36.6 us
  between operations: 14.4 us -> 0.88 us
    unnamed x3 -> x0, waiting for transfers between devices: 137 us -> none
    pallas_call x0 -> x11, Pallas kernels: none -> 45.9 us  [the longest x1 9.62 us: local(): pl.pallas_call(owned_kernel, in_specs=[smem(), smem(), whole(), whole()],...]
    scatter-add x6 -> x0, other arithmetic: 42.6 us -> none  [the longest x4 37.9 us: backward_slot(): return running.at[:, block_ids[:, slot_index]].add(contrib)]
    dot_general x14 -> x0, matrix products: 32.2 us -> none  [the longest x4 11.3 us: backward_slot(): jnp.einsum('tgj,mtgc->mtjc', weights_slot, grad_grid, preferred_element_t...]
    ppermute x4 -> x17, starting transfers between devices: 9.74 us -> 36.6 us  [the longest x3 12.3 us: local(): lax.ppermute(s, 'space', shift_y(side, side, d))]
    all_gather x1 -> x0, waiting for transfers between devices: 26.5 us -> none  [local(): lax.all_gather(fields, 'member', axis=0, tiled=True).astype(jnp.float32)]
    transpose x4 -> x0, local copies, waits for them, and re-layouts: 21.4 us -> none  [backward_slot(): jnp.einsum('tgj,mtgc->mtjc', weights_slot, grad_grid, preferred_element_t...]
    gather x4 -> x0, local copies, waits for them, and re-layouts: 18 us -> none  [forward_slot(): picked = jnp.take(extended, block_ids[:, slot_index], axis=1)]
  transfers between devices with their start and end apart: 6 -> 17, of which waited for: 4 -> 8; matrix products, arithmetic and copies ran while one was open for 6% -> 3% of each run, Pallas kernels for 0% -> 24%
where the time goes in v1:
time: 112 us
  Pallas kernels  45.9 us (41%)
  starting transfers between devices  36.6 us (33%)
  waiting for transfers between devices  14.8 us (13%)
  local copies, waits for them, and re-layouts  13.9 us (12%)
    ppermute x3, starting transfers between devices, local(): lax.ppermute(s, 'space', shift_y(side, side, d))  12.3 us
    unnamed x34, local copies, waits for them, and re-layouts  9.84 us
    pallas_call x1, Pallas kernels, local(): pl.pallas_call(owned_kernel, in_specs=[smem(), smem(), whole(), whole()],...  9.62 us
    pallas_call x1, Pallas kernels, local(): pl.pallas_call(fields_kernel, grid=(tiles,), in_specs=[smem(), smem(), pl...  8.37 us
    ppermute x3, waiting for transfers between devices, local(): others = [lax.ppermute(fields, 'member', shift(ring, d)) for d in (1, 3, 2)]  7.72 us
    pallas_call x1, Pallas kernels, local(): pl.pallas_call(rim_kernel, grid=(tiles,), in_specs=[smem(), smem(), col_s...  6.75 us
    pallas_call x1, Pallas kernels, local(): pl.pallas_call(functools.partial(weights_kernel, ensemble=members * ring,...  6.39 us
    ppermute x3, starting transfers between devices, local(): lax.ppermute(s, 'member', shift(ring, d))  5.57 us
  transfers between devices with their start and end apart: 17, of which 8 were waited for; matrix products, arithmetic and copies ran while one was open for 3% of the time, Pallas kernels for 24%

profile of v1, /device:TPU:0, one launch (start us, length us, event | category | flops | bytes accessed | tf_op | source)
XLA Modules:
  0.0 112.1 jit_solution(4198026682100083069)
XLA Ops:
  0.6 2.1 %fusion = (bf16[2,2,128,512]{3,2,1,0:T(8,128)(2,1)}, bf16[2,2,128,512]{3,2,1,0:T(8,128)(2,1)S(1)}) fusion(bf16[2,16,128,512]{3,2,1,0:T(8,128)(2,1)} %bitcast.10), kind=kLoop, calls=%fused_computation.2 | loop fusion | bytes 2097152 | tf_op jit(solution)/shard_map/slice | solution.py:335
  2.8 1.3 %collective-permute-start.1 = (bf16[2,2,128,512]{3,2,1,0:T(8,128)(2,1)}, bf16[2,2,128,512]{3,2,1,0:T(8,128)(2,1)S(1)}, u32[]{:S(2)}, u32[]{:S(2)}) collective-permute-start(bf16[2,2,128,512]{3,2,1,0:T(8,128)(2,1)} %get-tuple-element.62), channel_id=1, source_target_pairs={{1,0},{2,1},{3,2},{4,3},{5,4},{6,5},{7,6},{8,7},{9,8},{10,9},{11,1... | collective-permute-start | bytes 1572872 | tf_op jit(solution)/shard_map/ppermute | solution.py:335
  4.1 4.6 %collective-permute-start = (bf16[2,2,128,512]{3,2,1,0:T(8,128)(2,1)S(1)}, bf16[2,2,128,512]{3,2,1,0:T(8,128)(2,1)S(1)}, u32[]{:S(2)}, u32[]{:S(2)}) collective-permute-start(bf16[2,2,128,512]{3,2,1,0:T(8,128)(2,1)S(1)} %get-tuple-element.63), channel_id=1, source_target_pairs={{0,1},{1,2},{2,3},{3,4},{4,5},{5,6},{6,7},{7,8},{8,9},{9,10},{10,1... | collective-permute-start | bytes 1572872 | tf_op jit(solution)/shard_map/ppermute | solution.py:334
  8.6 0.8 copy.17.ids
  9.4 0.9 pad.12.w_out
  10.3 2.2 %copy-done = bf16[1,2,2048,512]{3,2,1,0:T(8,128)(2,1)S(1)} copy-done((bf16[1,2,2048,512]{3,2,1,0:T(8,128)(2,1)S(1)}, bf16[1,2,2048,512]{3,2,1,0:T(8,128)(2,1)}, u32[]{:S(2)}) %copy-start) | copy-done | bytes 4194328
  12.5 1.2 %copy-done.1 = bf16[8,4,128,128]{3,2,1,0:T(8,128)(2,1)S(1)} copy-done((bf16[8,4,128,128]{3,2,1,0:T(8,128)(2,1)S(1)}, bf16[8,4,128,128]{3,2,1,0:T(8,128)(2,1)}, u32[]{:S(2)}) %copy-start.1) | copy-done | bytes 1048600
  13.7 1.0 copy-done.2
  14.8 0.7 copy-done.10
  15.4 3.3 %shard_map.112 = (f32[2,8,128,512]{3,2,1,0:T(8,128)S(1)}, bf16[8,4,128,128]{3,2,1,0:T(8,128)(2,1)S(1)}, bf16[512,512]{1,0:T(8,128)(2,1)S(1)}, bf16[512,88]{1,0:T(8,128)(2,1)S(1)}) custom-call(s32[8,4]{1,0:T(8,128)S(1)} %copy.17.ids, s32[8]{0:T(128)S(1)} %copy-done.10, bf16[2,16,128,512]{3,2,1,0:T(8,128)(2,1)S(1)} %bitcast.11, ...), custom_call_target="tpu_custom_call" | custom-call | flops 1073741824 | bytes 10485760 | tf_op jit(solution)/shard_map/pallas_call | solution.py:342
  18.7 0.6 copy-done.8
  19.4 0.8 copy-done.13
  20.1 0.0 collective-permute-done.1.high
  20.1 0.0 collective-permute-done.low
  20.2 0.8 copy-done.6
  21.0 1.0 copy-done.7
  22.0 8.4 %shard_map.113 = (bf16[2,1024,512]{2,1,0:T(8,128)(2,1)S(1)}, bf16[2,88,1024]{2,1,0:T(8,128)(2,1)S(1)}) custom-call(s32[8,4]{1,0:T(8,128)S(1)} %copy.17.ids, s32[8]{0:T(128)S(1)} %copy-done.10, f32[2,8,128,512]{3,2,1,0:T(8,128)S(1)} %get-tuple-element.31.acc, bf16[2,2,128,512]{3,2,1,0:T(8,128)(2,1)S(1)} %copy-done.7, ...), custom_call_target="tpu_custom_call" | custom-call | flops 1073741824 | bytes 8388608 | tf_op jit(solution)/shard_map/pallas_call | solution.py:358
  30.4 3.2 %collective-permute-start.4 = (bf16[2,88,1024]{2,1,0:T(8,128)(2,1)S(1)}, bf16[2,88,1024]{2,1,0:T(8,128)(2,1)}, u32[]{:S(2)}, u32[]{:S(2)}) collective-permute-start(bf16[2,88,1024]{2,1,0:T(8,128)(2,1)S(1)} %get-tuple-element.32.own), channel_id=1, source_target_pairs={{0,32},{16,48},{32,0},{48,16},{1,33},{17,49},{33,1},{49,17},{2,34}... | collective-permute-start | bytes 1081352 | tf_op jit(solution)/shard_map/ppermute | solution.py:382
  33.6 1.2 %collective-permute-start.3 = (bf16[2,88,1024]{2,1,0:T(8,128)(2,1)S(1)}, bf16[2,88,1024]{2,1,0:T(8,128)(2,1)}, u32[]{:S(2)}, u32[]{:S(2)}) collective-permute-start(bf16[2,88,1024]{2,1,0:T(8,128)(2,1)S(1)} %get-tuple-element.32.own), channel_id=1, source_target_pairs={{0,48},{16,0},{32,16},{48,32},{1,49},{17,1},{33,17},{49,33},{2,50}... | collective-permute-start | bytes 1081352 | tf_op jit(solution)/shard_map/ppermute | solution.py:382
  34.8 0.9 collective-permute-start.2
  35.6 0.1 copy.15.var_weight
  35.7 0.9 pad.13.target
  36.7 0.1 pad_add_fusion.place
  36.8 5.3 %shard_map.114 = (bf16[2,512,1024]{2,1,0:T(8,128)(2,1)S(1)}, bf16[2,512,1024]{2,1,0:T(8,128)(2,1)S(1)}) custom-call(bf16[2,1024,512]{2,1,0:T(8,128)(2,1)S(1)} %get-tuple-element.33.lat, bf16[512,512]{1,0:T(8,128)(2,1)S(1)} %copy-done.3), custom_call_target="tpu_custom_call" | custom-call | flops 1073741824 | bytes 8388608 | tf_op jit(solution)/shard_map/pallas_call | solution.py:384
  42.1 0.0 copy-start.5
  42.1 0.0 copy-start.11
  42.1 1.4 %collective-permute-done.4.other3 = bf16[2,88,1024]{2,1,0:T(8,128)(2,1)} collective-permute-done((bf16[2,88,1024]{2,1,0:T(8,128)(2,1)S(1)}, bf16[2,88,1024]{2,1,0:T(8,128)(2,1)}, u32[]{:S(2)}, u32[]{:S(2)}) %collective-permute-start.4) | collective-permute-done | bytes 360480 | tf_op jit(solution)/shard_map/ppermute | solution.py:382
  43.5 6.3 %collective-permute-done.3.other2 = bf16[2,88,1024]{2,1,0:T(8,128)(2,1)} collective-permute-done((bf16[2,88,1024]{2,1,0:T(8,128)(2,1)S(1)}, bf16[2,88,1024]{2,1,0:T(8,128)(2,1)}, u32[]{:S(2)}, u32[]{:S(2)}) %collective-permute-start.3) | collective-permute-done | bytes 360480 | tf_op jit(solution)/shard_map/ppermute | solution.py:382
  49.8 0.0 collective-permute-done.2.other1
  49.8 6.4 %shard_map.115 = (bf16[2,512,1024]{2,1,0:T(8,128)(2,1)S(1)}, f32[256,640]{1,0:T(8,128)S(1)}, bf16[256,640]{1,0:T(8,128)(2,1)S(1)}) custom-call(s32[4]{0:T(128)S(1)} %pad_add_fusion.place, bf16[2,88,1024]{2,1,0:T(8,128)(2,1)S(1)} %get-tuple-element.32.own, bf16[2,88,1024]{2,1,0:T(8,128)(2,1)} %collective-permute-done.2.other1, ...), custom_call_target="tpu_custom_call" | custom-call | flops 1073741824 | bytes 8388608 | tf_op jit(solution)/shard_map/pallas_call | solution.py:399
  56.2 0.1 collective-permute-start.7
  56.3 0.0 copy-done.5
  56.3 0.0 copy-done.11
  56.3 6.7 %shard_map.116 = (bf16[2,512,1024]{2,1,0:T(8,128)(2,1)S(1)}, bf16[2,2,128,512]{3,2,1,0:T(8,128)(2,1)S(1)}, bf16[2,2,128,512]{3,2,1,0:T(8,128)(2,1)S(1)}) custom-call(s32[8,4]{1,0:T(8,128)S(1)} %copy.17.ids, s32[8]{0:T(128)S(1)} %copy-done.11, bf16[2,512,1024]{2,1,0:T(8,128)(2,1)S(1)} %get-tuple-element.37.grad_pre, bf16[8,4,128,128]{3,2,1,0:T(8,128)(2,1)S(1)} %copy-done.5, ...), custom_call_target="tpu_custom_call" | custom-call | flops 1073741824 | bytes 6291456 | tf_op jit(solution)/shard_map/pallas_call | solution.py:431
  63.1 3.0 %collective-permute-start.5 = (bf16[2,2,128,512]{3,2,1,0:T(8,128)(2,1)S(1)}, bf16[2,2,128,512]{3,2,1,0:T(8,128)(2,1)S(1)}, u32[]{:S(2)}, u32[]{:S(2)}) collective-permute-start(bf16[2,2,128,512]{3,2,1,0:T(8,128)(2,1)S(1)} %get-tuple-element.41), channel_id=1, source_target_pairs={{0,1},{1,2},{2,3},{3,4},{4,5},{5,6},{6,7},{7,8},{8,9},{9,10},{10,1... | collective-permute-start | bytes 1572872 | tf_op jit(solution)/shard_map/ppermute | solution.py:452
  66.1 1.3 %collective-permute-start.6 = (bf16[2,2,128,512]{3,2,1,0:T(8,128)(2,1)S(1)}, bf16[2,2,128,512]{3,2,1,0:T(8,128)(2,1)S(1)}, u32[]{:S(2)}, u32[]{:S(2)}) collective-permute-start(bf16[2,2,128,512]{3,2,1,0:T(8,128)(2,1)S(1)} %get-tuple-element.42), channel_id=1, source_target_pairs={{1,0},{2,1},{3,2},{4,3},{5,4},{6,5},{7,6},{8,7},{9,8},{10,9},{11,1... | collective-permute-start | bytes 1572872 | tf_op jit(solution)/shard_map/ppermute | solution.py:453
  67.4 0.0 collective-permute-done.7.refs_0_
  67.4 0.7 shard_map.119
  68.1 1.5 %collective-permute-start.8 = (bf16[64,640]{1,0:T(8,128)(2,1)S(1)}, bf16[64,640]{1,0:T(8,128)(2,1)S(1)}, u32[]{:S(2)}, u32[]{:S(2)}) collective-permute-start(bf16[64,640]{1,0:T(8,128)(2,1)S(1)} %get-tuple-element.46), channel_id=1, source_target_pairs={{0,16},{16,32},{32,48},{48,0},{1,17},{17,33},{33,49},{49,1},{2,18}... | collective-permute-start | bytes 245768 | tf_op jit(solution)/shard_map/ppermute | solution.py:466
  69.6 2.7 %collective-permute-start.9 = (bf16[64,640]{1,0:T(8,128)(2,1)S(1)}, bf16[64,640]{1,0:T(8,128)(2,1)S(1)}, u32[]{:S(2)}, u32[]{:S(2)}) collective-permute-start(bf16[64,640]{1,0:T(8,128)(2,1)S(1)} %get-tuple-element.47), channel_id=1, source_target_pairs={{0,32},{16,48},{32,0},{48,16},{1,33},{17,49},{33,1},{49,17},{2,34}... | collective-permute-start | bytes 245768 | tf_op jit(solution)/shard_map/ppermute | solution.py:466
  72.2 1.4 %collective-permute-start.10 = (bf16[64,640]{1,0:T(8,128)(2,1)S(1)}, bf16[64,640]{1,0:T(8,128)(2,1)S(1)}, u32[]{:S(2)}, u32[]{:S(2)}) collective-permute-start(bf16[64,640]{1,0:T(8,128)(2,1)S(1)} %get-tuple-element.48), channel_id=1, source_target_pairs={{0,48},{16,0},{32,16},{48,32},{1,49},{17,1},{33,17},{49,33},{2,50}... | collective-permute-start | bytes 245768 | tf_op jit(solution)/shard_map/ppermute | solution.py:466
  73.7 0.2 collective-permute-done.8.refs_0_
  73.9 2.6 %collective-permute-done.9.refs_1_ = bf16[64,640]{1,0:T(8,128)(2,1)S(1)} collective-permute-done((bf16[64,640]{1,0:T(8,128)(2,1)S(1)}, bf16[64,640]{1,0:T(8,128)(2,1)S(1)}, u32[]{:S(2)}, u32[]{:S(2)}) %collective-permute-start.9) | collective-permute-done | bytes 81952 | tf_op jit(solution)/shard_map/ppermute | solution.py:466
  76.5 0.2 collective-permute-done.10.refs_2_
  76.7 0.6 shard_map.120
  77.3 8.2 %collective-permute-start.11 = (f32[16,640]{1,0:T(8,128)S(1)}, f32[16,640]{1,0:T(8,128)S(1)}, u32[]{:S(2)}, u32[]{:S(2)}) collective-permute-start(f32[16,640]{1,0:T(8,128)S(1)} %get-tuple-element.50), channel_id=1, source_target_pairs={{0,4},{1,5},{2,6},{3,7},{4,8},{5,9},{6,10},{7,11},{8,12},{9,13},{1... | collective-permute-start | bytes 122888 | tf_op jit(solution)/shard_map/ppermute | solution.py:469
  85.5 4.0 %collective-permute-start.12 = (f32[16,640]{1,0:T(8,128)S(1)}, f32[16,640]{1,0:T(8,128)S(1)}, u32[]{:S(2)}, u32[]{:S(2)}) collective-permute-start(f32[16,640]{1,0:T(8,128)S(1)} %get-tuple-element.51), channel_id=1, source_target_pairs={{0,8},{1,9},{2,10},{3,11},{4,12},{5,13},{6,14},{7,15},{8,0},{9,1},... | collective-permute-start | bytes 122888 | tf_op jit(solution)/shard_map/ppermute | solution.py:469
  89.5 0.0 collective-permute-start.13
  89.5 0.9 collective-permute-done.11.refs_0_
  90.4 1.6 %collective-permute-done.12.refs_1_ = f32[16,640]{1,0:T(8,128)S(1)} collective-permute-done((f32[16,640]{1,0:T(8,128)S(1)}, f32[16,640]{1,0:T(8,128)S(1)}, u32[]{:S(2)}, u32[]{:S(2)}) %collective-permute-start.12) | collective-permute-done | bytes 40992 | tf_op jit(solution)/shard_map/ppermute | solution.py:469
  92.0 1.6 %collective-permute-done.13.refs_2_ = f32[16,640]{1,0:T(8,128)S(1)} collective-permute-done((f32[16,640]{1,0:T(8,128)S(1)}, f32[16,640]{1,0:T(8,128)S(1)}, u32[]{:S(2)}, u32[]{:S(2)}) %collective-permute-start.13) | collective-permute-done | bytes 40992 | tf_op jit(solution)/shard_map/ppermute | solution.py:469
  93.5 0.6 shard_map.121
  94.1 0.1 collective-permute-start.14
  94.2 0.3 collective-permute-start.15
  94.5 2.9 %collective-permute-start.16 = (f32[4,640]{1,0:T(4,128)S(1)}, f32[4,640]{1,0:T(4,128)S(1)}, u32[]{:S(2)}, u32[]{:S(2)}) collective-permute-start(f32[4,640]{1,0:T(4,128)S(1)} %get-tuple-element.56), channel_id=1, source_target_pairs={{0,3},{1,0},{2,1},{3,2},{4,7},{5,4},{6,5},{7,6},{8,11},{9,8},{10,9... | collective-permute-start | bytes 30728 | tf_op jit(solution)/shard_map/ppermute | solution.py:471
  97.4 9.6 %shard_map.117.base = f32[2,16,128,512]{3,2,1,0:T(8,128)} custom-call(s32[8,4]{1,0:T(8,128)S(1)} %copy.17.ids, s32[8]{0:T(128)S(1)} %copy-done.11, bf16[2,512,1024]{2,1,0:T(8,128)(2,1)S(1)} %get-tuple-element.40.grad_grid, bf16[8,4,128,128]{3,2,1,0:T(8,128)(2,1)S(1)} %copy-done.5), custom_call_target="tpu_custom_call" | custom-call | flops 1073741824 | bytes 12582912 | tf_op jit(solution)/shard_map/pallas_call | solution.py:455
  107.0 0.0 collective-permute-done.14.got1
  107.0 0.0 collective-permute-done.15.got2
  107.0 0.0 collective-permute-done.16.got3
  107.0 0.6 shard_map.122
  107.7 0.7 copy.18
  108.3 0.0 collective-permute-done.5.below
  108.3 0.0 collective-permute-done.6.above
  108.3 3.8 %shard_map.118 = f32[2,16,128,512]{3,2,1,0:T(8,128)} custom-call(f32[2,16,128,512]{3,2,1,0:T(8,128)} %shard_map.117.base, bf16[2,2,128,512]{3,2,1,0:T(8,128)(2,1)S(1)} %collective-permute-done.5.below, bf16[2,2,128,512]{3,2,1,0:T(8,128)(2,1)S(1)} %collective-permute-done.6.above), custom_call_target="tpu_custom_call", output_to_operand_aliasing={{}: (0, {})} | custom-call | tf_op jit(solution)/shard_map/pallas_call | solution.py:486
  (21 shorter events, 0.0 us)
Async XLA Ops:
  2.8 17.4 %collective-permute-start.1 = (bf16[2,2,128,512]{3,2,1,0:T(8,128)(2,1)}, bf16[2,2,128,512]{3,2,1,0:T(8,128)(2,1)S(1)}, u32[]{:S(2)}, u32[]{:S(2)}) collective-permute-start(bf16[2,2,128,512]{3,2,1,0:T(8,128)(2,1)} %get-tuple-element.62), channel_id=1, source_target_pairs={{1,0},{2,1},{3,2},{4,3},{5,4},{6,5},{7,6},{8,7},{9,8},{10,9},{11,1... | collective-permute-start | bytes 1572872 | tf_op jit(solution)/shard_map/ppermute | solution.py:335
  4.1 16.1 %collective-permute-start = (bf16[2,2,128,512]{3,2,1,0:T(8,128)(2,1)S(1)}, bf16[2,2,128,512]{3,2,1,0:T(8,128)(2,1)S(1)}, u32[]{:S(2)}, u32[]{:S(2)}) collective-permute-start(bf16[2,2,128,512]{3,2,1,0:T(8,128)(2,1)S(1)} %get-tuple-element.63), channel_id=1, source_target_pairs={{0,1},{1,2},{2,3},{3,4},{4,5},{5,6},{6,7},{7,8},{8,9},{9,10},{10,1... | collective-permute-start | bytes 1572872 | tf_op jit(solution)/shard_map/ppermute | solution.py:334
  10.3 2.2 %copy-start = (bf16[1,2,2048,512]{3,2,1,0:T(8,128)(2,1)S(1)}, bf16[1,2,2048,512]{3,2,1,0:T(8,128)(2,1)}, u32[]{:S(2)}) copy-start(bf16[1,2,2048,512]{3,2,1,0:T(8,128)(2,1)} %param.9) | copy-start | bytes 12582916
  12.5 1.2 %copy-start.1 = (bf16[8,4,128,128]{3,2,1,0:T(8,128)(2,1)S(1)}, bf16[8,4,128,128]{3,2,1,0:T(8,128)(2,1)}, u32[]{:S(2)}) copy-start(bf16[8,4,128,128]{3,2,1,0:T(8,128)(2,1)} %weight.3) | copy-start | bytes 3145732
  13.7 1.0 copy-start.2
  14.8 0.7 copy-start.10
  15.4 20.2 %copy-start.15 = (f32[83]{0:T(128)S(1)}, f32[83]{0:T(128)}, u32[]{:S(2)}) copy-start(f32[83]{0:T(128)} %param.17) | copy-start | bytes 1000
  18.7 0.6 copy-start.8
  19.4 0.8 copy-start.13
  20.1 10.3 %copy-start.4 = (bf16[8,4,128,128]{3,2,1,0:T(8,128)(2,1)}, bf16[8,4,128,128]{3,2,1,0:T(8,128)(2,1)S(1)}, u32[]{:S(2)}) copy-start(bf16[8,4,128,128]{3,2,1,0:T(8,128)(2,1)S(1)} %get-tuple-element.38.weight_t) | copy-start | bytes 3145732
  20.1 16.6 %copy-start.3 = (bf16[512,512]{1,0:T(8,128)(2,1)S(1)}, bf16[512,512]{1,0:T(8,128)(2,1)}, u32[]{:S(2)}) copy-start(bf16[512,512]{1,0:T(8,128)(2,1)} %w_in.5) | copy-start | bytes 1572868
  20.2 0.8 copy-start.6
  21.0 1.0 copy-start.7
  22.0 27.8 %copy-start.12 = (f32[1024]{0:T(1024)S(1)}, f32[1024]{0:T(1024)}, u32[]{:S(2)}) copy-start(f32[1024]{0:T(1024)} %param.16) | copy-start | bytes 12292
  30.4 19.4 %copy-start.9 = (bf16[512,88]{1,0:T(8,128)(2,1)S(1)}, bf16[512,88]{1,0:T(8,128)(2,1)}, u32[]{:S(2)}) copy-start(bf16[512,88]{1,0:T(8,128)(2,1)} %copy-done.8) | copy-start | bytes 270340
  30.4 13.1 %collective-permute-start.4 = (bf16[2,88,1024]{2,1,0:T(8,128)(2,1)S(1)}, bf16[2,88,1024]{2,1,0:T(8,128)(2,1)}, u32[]{:S(2)}, u32[]{:S(2)}) collective-permute-start(bf16[2,88,1024]{2,1,0:T(8,128)(2,1)S(1)} %get-tuple-element.32.own), channel_id=1, source_target_pairs={{0,32},{16,48},{32,0},{48,16},{1,33},{17,49},{33,1},{49,17},{2,34}... | collective-permute-start | bytes 1081352 | tf_op jit(solution)/shard_map/ppermute | solution.py:382
  33.6 16.2 %collective-permute-start.3 = (bf16[2,88,1024]{2,1,0:T(8,128)(2,1)S(1)}, bf16[2,88,1024]{2,1,0:T(8,128)(2,1)}, u32[]{:S(2)}, u32[]{:S(2)}) collective-permute-start(bf16[2,88,1024]{2,1,0:T(8,128)(2,1)S(1)} %get-tuple-element.32.own), channel_id=1, source_target_pairs={{0,48},{16,0},{32,16},{48,32},{1,49},{17,1},{33,17},{49,33},{2,50}... | collective-permute-start | bytes 1081352 | tf_op jit(solution)/shard_map/ppermute | solution.py:382
  34.8 15.1 %collective-permute-start.2 = (bf16[2,88,1024]{2,1,0:T(8,128)(2,1)S(1)}, bf16[2,88,1024]{2,1,0:T(8,128)(2,1)}, u32[]{:S(2)}, u32[]{:S(2)}) collective-permute-start(bf16[2,88,1024]{2,1,0:T(8,128)(2,1)S(1)} %get-tuple-element.32.own), channel_id=1, source_target_pairs={{0,16},{16,32},{32,48},{48,0},{1,17},{17,33},{33,49},{49,1},{2,18}... | collective-permute-start | bytes 1081352 | tf_op jit(solution)/shard_map/ppermute | solution.py:382
  42.1 14.3 %copy-start.5 = (bf16[8,4,128,128]{3,2,1,0:T(8,128)(2,1)S(1)}, bf16[8,4,128,128]{3,2,1,0:T(8,128)(2,1)}, u32[]{:S(2)}) copy-start(bf16[8,4,128,128]{3,2,1,0:T(8,128)(2,1)} %copy-done.4) | copy-start | bytes 3145732
  42.1 14.3 %copy-start.11 = (s32[8]{0:T(128)S(1)}, s32[8]{0:T(128)}, u32[]{:S(2)}) copy-start(s32[8]{0:T(128)} %count.7) | copy-start | bytes 100
  42.1 14.2 %copy-start.14 = (bf16[512,512]{1,0:T(8,128)(2,1)S(1)}, bf16[512,512]{1,0:T(8,128)(2,1)}, u32[]{:S(2)}) copy-start(bf16[512,512]{1,0:T(8,128)(2,1)} %copy-done.13) | copy-start | bytes 1572868
  56.2 11.2 %collective-permute-start.7 = (bf16[256,640]{1,0:T(8,128)(2,1)S(1)}, bf16[256,640]{1,0:T(8,128)(2,1)S(1)}, u32[]{:S(2)}, u32[]{:S(2)}) collective-permute-start(bf16[256,640]{1,0:T(8,128)(2,1)S(1)} %get-tuple-element.44), channel_id=1, source_target_pairs={{0,64},{64,0},{1,65},{65,1},{2,66},{66,2},{3,67},{67,3},{4,68},{68... | collective-permute-start | bytes 983048 | tf_op jit(solution)/shard_map/ppermute | solution.py:429
  63.1 45.2 %collective-permute-start.5 = (bf16[2,2,128,512]{3,2,1,0:T(8,128)(2,1)S(1)}, bf16[2,2,128,512]{3,2,1,0:T(8,128)(2,1)S(1)}, u32[]{:S(2)}, u32[]{:S(2)}) collective-permute-start(bf16[2,2,128,512]{3,2,1,0:T(8,128)(2,1)S(1)} %get-tuple-element.41), channel_id=1, source_target_pairs={{0,1},{1,2},{2,3},{3,4},{4,5},{5,6},{6,7},{7,8},{8,9},{9,10},{10,1... | collective-permute-start | bytes 1572872 | tf_op jit(solution)/shard_map/ppermute | solution.py:452
  66.1 42.2 %collective-permute-start.6 = (bf16[2,2,128,512]{3,2,1,0:T(8,128)(2,1)S(1)}, bf16[2,2,128,512]{3,2,1,0:T(8,128)(2,1)S(1)}, u32[]{:S(2)}, u32[]{:S(2)}) collective-permute-start(bf16[2,2,128,512]{3,2,1,0:T(8,128)(2,1)S(1)} %get-tuple-element.42), channel_id=1, source_target_pairs={{1,0},{2,1},{3,2},{4,3},{5,4},{6,5},{7,6},{8,7},{9,8},{10,9},{11,1... | collective-permute-start | bytes 1572872 | tf_op jit(solution)/shard_map/ppermute | solution.py:453
  68.1 5.8 %collective-permute-start.8 = (bf16[64,640]{1,0:T(8,128)(2,1)S(1)}, bf16[64,640]{1,0:T(8,128)(2,1)S(1)}, u32[]{:S(2)}, u32[]{:S(2)}) collective-permute-start(bf16[64,640]{1,0:T(8,128)(2,1)S(1)} %get-tuple-element.46), channel_id=1, source_target_pairs={{0,16},{16,32},{32,48},{48,0},{1,17},{17,33},{33,49},{49,1},{2,18}... | collective-permute-start | bytes 245768 | tf_op jit(solution)/shard_map/ppermute | solution.py:466
  69.6 6.9 %collective-permute-start.9 = (bf16[64,640]{1,0:T(8,128)(2,1)S(1)}, bf16[64,640]{1,0:T(8,128)(2,1)S(1)}, u32[]{:S(2)}, u32[]{:S(2)}) collective-permute-start(bf16[64,640]{1,0:T(8,128)(2,1)S(1)} %get-tuple-element.47), channel_id=1, source_target_pairs={{0,32},{16,48},{32,0},{48,16},{1,33},{17,49},{33,1},{49,17},{2,34}... | collective-permute-start | bytes 245768 | tf_op jit(solution)/shard_map/ppermute | solution.py:466
  72.2 4.4 %collective-permute-start.10 = (bf16[64,640]{1,0:T(8,128)(2,1)S(1)}, bf16[64,640]{1,0:T(8,128)(2,1)S(1)}, u32[]{:S(2)}, u32[]{:S(2)}) collective-permute-start(bf16[64,640]{1,0:T(8,128)(2,1)S(1)} %get-tuple-element.48), channel_id=1, source_target_pairs={{0,48},{16,0},{32,16},{48,32},{1,49},{17,1},{33,17},{49,33},{2,50}... | collective-permute-start | bytes 245768 | tf_op jit(solution)/shard_map/ppermute | solution.py:466
  77.3 13.1 %collective-permute-start.11 = (f32[16,640]{1,0:T(8,128)S(1)}, f32[16,640]{1,0:T(8,128)S(1)}, u32[]{:S(2)}, u32[]{:S(2)}) collective-permute-start(f32[16,640]{1,0:T(8,128)S(1)} %get-tuple-element.50), channel_id=1, source_target_pairs={{0,4},{1,5},{2,6},{3,7},{4,8},{5,9},{6,10},{7,11},{8,12},{9,13},{1... | collective-permute-start | bytes 122888 | tf_op jit(solution)/shard_map/ppermute | solution.py:469
  85.5 6.5 %collective-permute-start.12 = (f32[16,640]{1,0:T(8,128)S(1)}, f32[16,640]{1,0:T(8,128)S(1)}, u32[]{:S(2)}, u32[]{:S(2)}) collective-permute-start(f32[16,640]{1,0:T(8,128)S(1)} %get-tuple-element.51), channel_id=1, source_target_pairs={{0,8},{1,9},{2,10},{3,11},{4,12},{5,13},{6,14},{7,15},{8,0},{9,1},... | collective-permute-start | bytes 122888 | tf_op jit(solution)/shard_map/ppermute | solution.py:469
  89.5 4.0 %collective-permute-start.13 = (f32[16,640]{1,0:T(8,128)S(1)}, f32[16,640]{1,0:T(8,128)S(1)}, u32[]{:S(2)}, u32[]{:S(2)}) collective-permute-start(f32[16,640]{1,0:T(8,128)S(1)} %get-tuple-element.52), channel_id=1, source_target_pairs={{0,12},{1,13},{2,14},{3,15},{4,0},{5,1},{6,2},{7,3},{8,4},{9,5},{1... | collective-permute-start | bytes 122888 | tf_op jit(solution)/shard_map/ppermute | solution.py:469
  94.1 12.9 %collective-permute-start.14 = (f32[4,640]{1,0:T(4,128)S(1)}, f32[4,640]{1,0:T(4,128)S(1)}, u32[]{:S(2)}, u32[]{:S(2)}) collective-permute-start(f32[4,640]{1,0:T(4,128)S(1)} %get-tuple-element.54), channel_id=1, source_target_pairs={{0,1},{1,2},{2,3},{3,0},{4,5},{5,6},{6,7},{7,4},{8,9},{9,10},{10,1... | collective-permute-start | bytes 30728 | tf_op jit(solution)/shard_map/ppermute | solution.py:471
  94.2 12.8 %collective-permute-start.15 = (f32[4,640]{1,0:T(4,128)S(1)}, f32[4,640]{1,0:T(4,128)S(1)}, u32[]{:S(2)}, u32[]{:S(2)}) collective-permute-start(f32[4,640]{1,0:T(4,128)S(1)} %get-tuple-element.55), channel_id=1, source_target_pairs={{0,2},{1,3},{2,0},{3,1},{4,6},{5,7},{6,4},{7,5},{8,10},{9,11},{10,... | collective-permute-start | bytes 30728 | tf_op jit(solution)/shard_map/ppermute | solution.py:471
  94.5 12.6 %collective-permute-start.16 = (f32[4,640]{1,0:T(4,128)S(1)}, f32[4,640]{1,0:T(4,128)S(1)}, u32[]{:S(2)}, u32[]{:S(2)}) collective-permute-start(f32[4,640]{1,0:T(4,128)S(1)} %get-tuple-element.56), channel_id=1, source_target_pairs={{0,3},{1,0},{2,1},{3,2},{4,7},{5,4},{6,5},{7,6},{8,11},{9,8},{10,9... | collective-permute-start | bytes 30728 | tf_op jit(solution)/shard_map/ppermute | solution.py:471

commit v2 on v0

v2 whole, which is shorter than its diff:
```python
import functools

import jax
import jax.numpy as jnp
from jax import lax
from jax.experimental import pallas as pl
from jax.experimental.pallas import tpu as pltpu
from jax.sharding import PartitionSpec as P

HALO = 2
smooth_square = 0.1 * 0.1
gelu_scale = 0.7978845608028654
gelu_cubic = 0.044715
MIB = 1 << 20
f32 = jnp.float32
bf16 = jnp.bfloat16

NN = (((1,), (0,)), ((), ()))
NT = (((1,), (1,)), ((), ()))


def dot(a, b, dims=NN):
    return lax.dot_general(a, b, dims, preferred_element_type=f32)


def vmem():
    return pl.BlockSpec(memory_space=pltpu.VMEM)


def smem():
    return pl.BlockSpec(memory_space=pltpu.SMEM)


def hbm():
    return pl.BlockSpec(memory_space=pltpu.HBM)


def in_hbm(x):
    return pltpu.with_memory_space_constraint(x, pltpu.HBM)


def in_vmem(*xs):
    return [pltpu.with_memory_space_constraint(x, pltpu.VMEM) for x in xs]


def held(dims, dtype):
    return pltpu.VMEM(dims, dtype)


def anywhere():
    return pl.BlockSpec(memory_space=pl.ANY)


def cost(flops, moved, transcendentals=0):
    return pl.CostEstimate(
        flops=int(flops), bytes_accessed=int(moved), transcendentals=int(transcendentals)
    )


def params(mib):
    return pltpu.CompilerParams(vmem_limit_bytes=mib * MIB)


def shape(dims, dtype):
    return jax.ShapeDtypeStruct(dims, dtype)


def rows_at(start, size):
    return pl.ds(pl.multiple_of(start * size, size), size)


def prepare_kernel(
    meta, lat_hbm, weight_hbm, w_in_hbm, w_out,
    acc0, acc1, halo_w, halo_wt, own_wt, w_in_v, w_in_t, w_out_v, w_out_t,
    lat, weight, sems, *, spaces,
):
    tiles, slots, cells, nodes = weight.shape
    members, blocks = lat.shape[0], lat.shape[1]
    copies = [
        pltpu.make_async_copy(weight_hbm, weight, sems.at[0]),
        pltpu.make_async_copy(lat_hbm.at[0], lat.at[0], sems.at[1]),
        pltpu.make_async_copy(lat_hbm.at[1], lat.at[1], sems.at[2]),
        pltpu.make_async_copy(w_in_hbm, w_in_v, sems.at[3]),
    ]
    for c in copies:
        c.start()
    at_space = meta[tiles * slots + tiles]
    halo_w[...] = jnp.zeros_like(halo_w)
    halo_wt[...] = jnp.zeros_like(halo_wt)
    own_wt[...] = jnp.zeros_like(own_wt)
    copies[0].wait()

    def place_tile(t, carry):
        for k in range(slots):
            e = meta[k * tiles + t]
            live = k < meta[slots * tiles + t]
            w = weight[t, k]
            wt = w.T
            below = (e < HALO) & (at_space > 0)
            above = (e >= HALO + blocks) & (at_space < spaces - 1)
            mine = (e >= HALO) & (e < HALO + blocks)
            slot = jnp.where(e < HALO, e, jnp.where(mine, 0, e - blocks))
            block = jnp.clip(e - HALO, 0, blocks - 1)

            @pl.when(live & (below | above))
            def _():
                halo_w[rows_at(t, cells), rows_at(slot, nodes)] += w
                halo_wt[rows_at(slot, nodes), rows_at(t, cells)] += wt

            @pl.when(live & mine)
            def _():
                own_wt[rows_at(block, nodes), rows_at(t, cells)] += wt

        return carry

    lax.fori_loop(0, tiles, place_tile, 0)
    for c in copies[1:]:
        c.wait()

    def gather_tile(t, carry):
        parts, at = [], []
        for k in range(slots):
            e = meta[k * tiles + t]
            mine = (k < meta[slots * tiles + t]) & (e >= HALO) & (e < HALO + blocks)
            w = weight[t, k]
            parts.append(jnp.where(mine, w, jnp.zeros_like(w)))
            at.append(jnp.clip(e - HALO, 0, blocks - 1))
        lhs = jnp.concatenate(parts, axis=1)
        for m, acc in enumerate((acc0, acc1)):
            rhs = jnp.concatenate([lat[m, a] for a in at], axis=0)
            acc[rows_at(t, cells)] = dot(lhs, rhs)
        return carry

    lax.fori_loop(0, tiles, gather_tile, 0)
    w_in_t[...] = w_in_v[...].T
    variables = w_out.shape[0]
    w_out_v[...] = jnp.zeros_like(w_out_v)
    w_out_v[:variables] = w_out[...]
    w_out_t[...] = w_out_v[...].T


def gelu_parts(x):
    square = x * x
    half = 0.5 + 0.5 * jnp.tanh(x * (gelu_scale + (gelu_scale * gelu_cubic) * square))
    return square, half


CHUNK = 256


def fields_kernel(acc, low, high, halo_w, w_in, w_out, lat_out, fields):
    count = acc.shape[0]
    half_k = low.shape[0]
    for start in range(0, count, 2 * CHUNK):
        at = slice(start, start + 2 * CHUNK)
        total = acc[at] + dot(halo_w[at, :half_k], low[...])
        total = total + dot(halo_w[at, half_k:], high[...])
        rounded = total.astype(bf16)
        lat_out[at] = rounded
        pre = dot(w_in[...], rounded, NT)
        _, half = gelu_parts(pre)
        fields[:, at] = dot(w_out[...], (pre * half).astype(bf16)).astype(bf16)


def slopes_kernel(lat, w_in, act_t, slope_t):
    count = lat.shape[0]
    for start in range(0, count, CHUNK):
        at = slice(start, start + CHUNK)
        x = dot(w_in[...], lat[at], NT)
        square, half = gelu_parts(x)
        act_t[:, at] = (x * half).astype(bf16)
        inner = x * (2.0 * gelu_scale + (6.0 * gelu_scale * gelu_cubic) * square)
        slope_t[:, at] = (half + half * (1.0 - half) * inner).astype(bf16)


def smooth_sign(u):
    return u * lax.rsqrt(u * u + smooth_square)


def weights_kernel(
    meta, own0, own1, o10, o11, o20, o21, o30, o31, target, area, var_weight,
    act0, act1, slope0, slope1, lat0, lat1, w_out_t,
    grad_pre0, grad_pre1, keep, send, total_in, total_out, *, ensemble, states, dp_at,
):
    count = own0.shape[1]
    others = (o10, o11, o20, o21, o30, o31)
    for start in range(0, count, CHUNK):
        at = slice(start, start + CHUNK)
        truth = target[:, at].astype(f32)
        mine = [own0[:, at].astype(f32), own1[:, at].astype(f32)]
        pair = smooth_sign(mine[0] - mine[1])
        spread = [pair, -pair]
        for other in others:
            theirs = other[:, at].astype(f32)
            for a in range(2):
                spread[a] = spread[a] + smooth_sign(mine[a] - theirs)
        cell_weight = area[:, at] * var_weight[...] * (1.0 / states)
        cots = []
        for a in range(2):
            value = smooth_sign(mine[a] - truth) * (1.0 / ensemble)
            value = value - spread[a] * (1.0 / (ensemble * (ensemble - 1)))
            cots.append((cell_weight * value).astype(bf16))
        cot = jnp.concatenate(cots, axis=1)
        grad_act = dot(w_out_t[...], cot)
        slope = jnp.concatenate([slope0[:, at], slope1[:, at]], axis=1)
        pre = (grad_act * slope.astype(f32)).astype(bf16)
        grad_pre0[:, at] = pre[:, :CHUNK]
        grad_pre1[:, at] = pre[:, CHUNK:]
        part_in = dot(pre, jnp.concatenate([lat0[at], lat1[at]], axis=0))
        act = jnp.concatenate([act0[:, at], act1[:, at]], axis=1)
        part_out = dot(act, cot, NT)
        if start == 0:
            total_in[...] = part_in
            total_out[...] = jnp.zeros_like(total_out)
            total_out[:, : part_out.shape[1]] = part_out
        else:
            total_in[...] += part_in
            total_out[:, : part_out.shape[1]] += part_out
    rows = keep.shape[0]
    wide = total_in.shape[1]
    here = meta[dp_at]
    stay, leave = rows_at(here, rows), rows_at(1 - here, rows)
    keep[:, :wide] = total_in[stay]
    keep[:, wide:] = total_out[stay]
    send[:, :wide] = total_in[leave].astype(bf16)
    send[:, wide:] = total_out[leave].astype(bf16)


def rim_kernel(grad_pre0, grad_pre1, halo_wt, w_in_t, grad_grid0, grad_grid1, low, high):
    half_k = low.shape[1]
    for m, (grad_pre, grad_grid) in enumerate(
        ((grad_pre0, grad_grid0), (grad_pre1, grad_grid1))
    ):
        grad_grid[...] = dot(w_in_t[...], grad_pre[...]).astype(bf16)
        low[m] = dot(halo_wt[:half_k], grad_grid[...], NT).astype(bf16)
        high[m] = dot(halo_wt[half_k:], grad_grid[...], NT).astype(bf16)


def owned_kernel(grad_grid0, grad_grid1, own_wt, out, edge, parts, sems):
    step = edge.shape[2]
    count = own_wt.shape[0] // step
    copies = []
    for m, grad_grid in enumerate((grad_grid0, grad_grid1)):
        for i in range(count):
            value = dot(own_wt[i * step : (i + 1) * step], grad_grid[...], NT)
            if i == 0:
                edge[m, 0] = value
            elif i == count - 1:
                edge[m, 1] = value
            else:
                slot = len(copies)
                parts[slot] = value
                copy = pltpu.make_async_copy(
                    parts.at[slot], out.at[m, i * step : (i + 1) * step], sems.at[slot]
                )
                copy.start()
                copies.append(copy)
    for copy in copies:
        copy.wait()


def add_rim_kernel(base, edge, below, above, out, parts, sems):
    step = edge.shape[2]
    last = out.shape[1] - step
    copies = []
    for side, (start, got) in enumerate(((0, below), (last, above))):
        for m in range(edge.shape[0]):
            slot = side * edge.shape[0] + m
            parts[slot] = edge[m, side] + got[m].astype(f32)
            copy = pltpu.make_async_copy(
                parts.at[slot], out.at[m, start : start + step], sems.at[slot]
            )
            copy.start()
            copies.append(copy)
    for copy in copies:
        copy.wait()


def split_kernel(meta, kept, swapped, own, send1, send2, send3, total, *, member_at):
    parts, rows = total.shape[0], total.shape[1]
    value = kept[...] + swapped[...].astype(f32)
    for p in range(parts):
        total[p] = value[p * rows : (p + 1) * rows]
    here = meta[member_at]
    own[...] = total[here]
    for d, out in ((1, send1), (2, send2), (3, send3)):
        out[...] = total[lax.rem(here + d, parts)].astype(out.dtype)


def scatter_kernel(kept, got1, got2, got3, later, out):
    value = kept[...] + got1[...].astype(f32) + got2[...].astype(f32) + got3[...].astype(f32)
    parts, rows = out.shape[0], out.shape[1]
    for p in range(parts):
        out[p] = value[p * rows : (p + 1) * rows].astype(out.dtype)


def finish_kernel(got, grad_in, grad_out):
    value = got[0].astype(f32)
    for p in range(1, got.shape[0]):
        value = value + got[p].astype(f32)
    wide = grad_in.shape[1]
    grad_in[...] = value[:, :wide]
    grad_out[...] = value[:, wide : wide + grad_out.shape[1]]


def ring(count, distance):
    return [(i, (i + distance) % count) for i in range(count)]


def local(latents, edge_weight, block_ids, block_count, w_in, w_out, targets, area, var_weight):
    members = latents.shape[1]
    feature = latents.shape[3]
    hidden = w_in.shape[0]
    variables = w_out.shape[0]
    rows_v = (variables + 7) // 8 * 8
    tiles, slots, cells, nodes = edge_weight.shape
    n = tiles * cells
    lat = latents[0].reshape(members, -1, nodes, feature)
    blocks = lat.shape[1]
    edge_rows = HALO * nodes
    rim_rows = 2 * edge_rows
    spaces = lax.axis_size("space")
    chips = lax.axis_size("member")
    meta = jnp.concatenate(
        [
            block_ids.T.reshape(-1),
            block_count,
            jnp.stack(
                [lax.axis_index("space"), lax.axis_index("dp"), lax.axis_index("member")]
            ).astype(jnp.int32),
        ]
    )
    dp_at = tiles * slots + tiles + 1
    member_at = dp_at + 1

    flat = latents[0]
    halos = []
    for m in range(members):
        low = lax.ppermute(flat[m, -edge_rows:], "space", ring(spaces, 1))
        high = lax.ppermute(flat[m, :edge_rows], "space", ring(spaces, -1))
        halos.append((low, high))

    target = jnp.pad(targets[0], ((0, rows_v - variables), (0, 0)))
    scale_v = jnp.pad(var_weight, (0, rows_v - variables))[:, None]
    scale_n = area[None, :]

    acc0, acc1, halo_w, halo_wt, own_wt, w_in_v, w_in_t, w_out_v, w_out_t = pl.pallas_call(
        functools.partial(prepare_kernel, spaces=spaces),
        in_specs=[smem(), hbm(), hbm(), hbm(), vmem()],
        out_specs=[vmem()] * 9,
        out_shape=[
            held((n, feature), f32),
            held((n, feature), f32),
            held((n, rim_rows), bf16),
            held((rim_rows, n), bf16),
            held((blocks * nodes, n), bf16),
            held((hidden, feature), bf16),
            held((feature, hidden), bf16),
            held((rows_v, hidden), bf16),
            held((hidden, rows_v), bf16),
        ],
        scratch_shapes=[
            pltpu.VMEM(lat.shape, bf16),
            pltpu.VMEM(edge_weight.shape, bf16),
            pltpu.SemaphoreType.DMA((4,)),
        ],
        compiler_params=params(28),
        cost_estimate=cost(2 * n * slots * nodes * feature * members, 10 * MIB),
    )(meta, in_hbm(lat), in_hbm(edge_weight), in_hbm(w_in), w_out)

    grid_latent, fields, acts, slopes = [], [], [], []
    for m, acc in enumerate((acc0, acc1)):
        low, high = halos[m]
        lat_m, fields_m = pl.pallas_call(
            fields_kernel,
            in_specs=[vmem()] * 6,
            out_specs=[vmem()] * 2,
            out_shape=[held((n, feature), bf16), shape((rows_v, n), bf16)],
            compiler_params=params(16),
            cost_estimate=cost(4 * n * feature * hidden, MIB, n * hidden),
        )(*in_vmem(acc), low, high, *in_vmem(halo_w, w_in_v, w_out_v))
        grid_latent.append(lat_m)
        fields.append(fields_m)
        act_m, slope_m = pl.pallas_call(
            slopes_kernel,
            in_specs=[vmem()] * 2,
            out_specs=[vmem()] * 2,
            out_shape=[held((hidden, n), bf16)] * 2,
            compiler_params=params(16),
            cost_estimate=cost(4 * n * feature * hidden, MIB, n * hidden),
        )(*in_vmem(lat_m, w_in_v))
        acts.append(act_m)
        slopes.append(slope_m)

    def along(x, distance):
        return lax.ppermute(x, "member", ring(chips, distance))

    left0 = along(fields[0], 1)
    right0 = along(fields[0], -1)
    far0 = along(left0, 1)
    right1 = along(fields[1], -1)
    left1 = along(fields[1], 1)
    far1 = along(right1, -1)

    wide = feature + 128
    half_rows = hidden // 2
    grad_pre0, grad_pre1, keep, send = pl.pallas_call(
        functools.partial(
            weights_kernel,
            ensemble=members * chips,
            states=targets.shape[0] * lax.axis_size("dp"),
            dp_at=dp_at,
        ),
        in_specs=[smem()] + [vmem()] * 18,
        out_specs=[vmem()] * 4,
        out_shape=[
            held((hidden, n), bf16),
            held((hidden, n), bf16),
            shape((half_rows, wide), f32),
            shape((half_rows, wide), bf16),
        ],
        scratch_shapes=[pltpu.VMEM((hidden, feature), f32), pltpu.VMEM((hidden, 128), f32)],
        compiler_params=params(20),
        cost_estimate=cost(4 * n * feature * hidden, MIB),
    )(
        meta, *fields, left0, left1, right0, right1, far0, far1, target, scale_n, scale_v,
        *in_vmem(*acts, *slopes, *grid_latent, w_out_t),
    )

    swapped = lax.ppermute(send, "dp", [(0, 1), (1, 0)])

    grad_grid0, grad_grid1, rim_low, rim_high = pl.pallas_call(
        rim_kernel,
        in_specs=[vmem()] * 4,
        out_specs=[vmem()] * 4,
        out_shape=[held((feature, n), bf16)] * 2 + [shape((members, edge_rows, feature), bf16)] * 2,
        compiler_params=params(16),
        cost_estimate=cost(8 * n * feature * hidden, MIB),
    )(*in_vmem(grad_pre0, grad_pre1, halo_wt, w_in_t))

    from_below = lax.ppermute(rim_high, "space", ring(spaces, 1))
    from_above = lax.ppermute(rim_low, "space", ring(spaces, -1))

    quarter = half_rows // chips
    kept, *sends = pl.pallas_call(
        functools.partial(split_kernel, member_at=member_at),
        in_specs=[smem(), vmem(), vmem()],
        out_specs=[vmem()] * 4,
        out_shape=[shape((quarter, wide), f32)] + [shape((quarter, wide), bf16)] * 3,
        scratch_shapes=[pltpu.VMEM((chips, quarter, wide), f32)],
        compiler_params=params(8),
    )(meta, keep, swapped)
    got = [along(s, d) for d, s in zip((1, 2, 3), sends)]

    middle = blocks // HALO - 2
    owned, edge = pl.pallas_call(
        owned_kernel,
        in_specs=[vmem()] * 3,
        out_specs=[hbm(), vmem()],
        out_shape=[
            shape((members, blocks * nodes, feature), f32),
            held((members, 2, edge_rows, feature), f32),
        ],
        scratch_shapes=[
            pltpu.VMEM((members * middle, edge_rows, feature), f32),
            pltpu.SemaphoreType.DMA((members * middle,)),
        ],
        compiler_params=params(20),
        cost_estimate=cost(2 * blocks * nodes * n * feature * members, 8 * MIB),
    )(*in_vmem(grad_grid0, grad_grid1, own_wt))

    last_rows = quarter // spaces
    spread = pl.pallas_call(
        scatter_kernel,
        in_specs=[vmem()] * 4 + [anywhere()],
        out_specs=vmem(),
        out_shape=shape((spaces, last_rows, wide), bf16),
        compiler_params=params(8),
    )(kept, *got, edge)
    spread = lax.all_to_all(spread, "space", 0, 0, tiled=True)
    grad_w_in, grad_w_out = pl.pallas_call(
        finish_kernel,
        in_specs=[vmem()],
        out_specs=[vmem()] * 2,
        out_shape=[shape((last_rows, feature), f32), shape((last_rows, variables), f32)],
        compiler_params=params(8),
    )(spread)

    grad_latent = pl.pallas_call(
        add_rim_kernel,
        in_specs=[hbm(), vmem(), vmem(), vmem()],
        out_specs=hbm(),
        out_shape=shape(owned.shape, f32),
        scratch_shapes=[
            pltpu.VMEM((2 * members, edge_rows, feature), f32),
            pltpu.SemaphoreType.DMA((2 * members,)),
        ],
        input_output_aliases={0: 0},
        compiler_params=params(8),
    )(owned, *in_vmem(edge), from_below, from_above)
    return grad_latent[None], grad_w_in, grad_w_out.T


def solution(mesh):
    placed = (
        P("dp", "member", "space", None),
        P("space", None, None, None),
        P("space", None),
        P("space"),
        P(),
        P(),
        P("dp", None, "space"),
        P("space"),
        P(),
    )
    return jax.shard_map(
        local,
        mesh=mesh,
        in_specs=placed,
        out_specs=(
            P("dp", "member", "space", None),
            P(("dp", "member", "space"), None),
            P(None, ("dp", "member", "space")),
        ),
        check_vma=False,
    )
```

time: 366 us -> 82 us (0.22)
  waiting for transfers between devices: 174 us -> 5.94 us
  other arithmetic: 63.3 us -> 0 us
  local copies, waits for them, and re-layouts: 69.3 us -> 6.33 us
  matrix products: 32.2 us -> 0 us
  Pallas kernels: 0 us -> 29.2 us
  starting transfers between devices: 9.82 us -> 28.9 us
  between operations: 14.4 us -> 1.04 us
  blocking collectives: 0 us -> 10.2 us
    unnamed x3 -> x0, waiting for transfers between devices: 137 us -> none
    scatter-add x6 -> x0, other arithmetic: 42.6 us -> none  [the longest x4 37.9 us: backward_slot(): return running.at[:, block_ids[:, slot_index]].add(contrib)]
    dot_general x14 -> x0, matrix products: 32.2 us -> none  [the longest x4 11.3 us: backward_slot(): jnp.einsum('tgj,mtgc->mtjc', weights_slot, grad_grid, preferred_element_t...]
    pallas_call x0 -> x12, Pallas kernels: none -> 29.2 us  [the longest x1 7.07 us: local(): pl.pallas_call(functools.partial(prepare_kernel, spaces=spaces), in_specs...]
    all_gather x1 -> x0, waiting for transfers between devices: 26.5 us -> none  [local(): lax.all_gather(fields, 'member', axis=0, tiled=True).astype(jnp.float32)]
    transpose x4 -> x0, local copies, waits for them, and re-layouts: 21.4 us -> none  [backward_slot(): jnp.einsum('tgj,mtgc->mtjc', weights_slot, grad_grid, preferred_element_t...]
    ppermute x4 -> x16, starting transfers between devices: 9.74 us -> 28.9 us  [the longest x9 11.5 us: along(): return lax.ppermute(x, 'member', ring(chips, distance))]
    gather x4 -> x0, local copies, waits for them, and re-layouts: 18 us -> none  [forward_slot(): picked = jnp.take(extended, block_ids[:, slot_index], axis=1)]
  transfers between devices with their start and end apart: 6 -> 16, of which waited for: 4 -> 3; matrix products, arithmetic and copies ran while one was open for 6% -> 3% of each run, Pallas kernels for 0% -> 29%
where the time goes in v2:
time: 82 us; the launch traced here: 81.7 us
  Pallas kernels  29.2 us (36%)
  starting transfers between devices  28.9 us (35%)
  blocking collectives  10.2 us (12%)
  local copies, waits for them, and re-layouts  6.33 us (8%)
  waiting for transfers between devices  5.94 us (7%)
  between operations  1.04 us (1%)
    ppermute x9, starting transfers between devices, along(): return lax.ppermute(x, 'member', ring(chips, distance))  11.5 us
    all_to_all x1, blocking collectives, local(): spread = lax.all_to_all(spread, 'space', 0, 0, tiled=True)  10.2 us
    ppermute x2, starting transfers between devices, local(): high = lax.ppermute(flat[m, :edge_rows], 'space', ring(spaces, -1))  9.92 us
    pallas_call x1, Pallas kernels, local(): pl.pallas_call(functools.partial(prepare_kernel, spaces=spaces), in_specs...  7.07 us
    ppermute x9, waiting for transfers between devices, along(): return lax.ppermute(x, 'member', ring(chips, distance))  5.92 us
    ppermute x1, starting transfers between devices, local(): from_above = lax.ppermute(rim_low, 'space', ring(spaces, -1))  5.33 us
    pallas_call x1, Pallas kernels, local(): pl.pallas_call(owned_kernel, in_specs=[vmem()] * 3, out_specs=[hbm(), vme...  5.21 us
    pallas_call x2, Pallas kernels, local(): pl.pallas_call(fields_kernel, in_specs=[vmem()] * 6, out_specs=[vmem()] *...  4.68 us
  transfers between devices with their start and end apart: 16, of which 3 were waited for; matrix products, arithmetic and copies ran while one was open for 3% of the time, Pallas kernels for 29%

profile of v2, /device:TPU:0, one launch (start us, length us, event | category | flops | bytes accessed | tf_op | source)
XLA Modules:
  0.0 81.7 jit_solution(7195098622238097147)
XLA Ops:
  0.6 2.0 %slice_bitcast_fusion = (bf16[256,512]{1,0:T(8,128)(2,1)S(1)}, bf16[256,512]{1,0:T(8,128)(2,1)S(1)}, bf16[256,512]{1,0:T(8,128)(2,1)}, bf16[256,512]{1,0:T(8,128)(2,1)}) fusion(bf16[2,2048,512]{2,1,0:T(8,128)(2,1)} %bitcast.22), kind=kLoop, calls=%fused_computation | loop fusion | bytes 2097152 | tf_op jit(solution)/shard_map/squeeze | solution.py:340
  2.7 2.0 %collective-permute-start.2 = (bf16[256,512]{1,0:T(8,128)(2,1)S(1)}, bf16[256,512]{1,0:T(8,128)(2,1)S(1)}, u32[]{:S(2)}, u32[]{:S(2)}) collective-permute-start(bf16[256,512]{1,0:T(8,128)(2,1)S(1)} %get-tuple-element.70), channel_id=1, source_target_pairs={{0,1},{1,2},{2,3},{3,4},{4,5},{5,6},{6,7},{7,8},{8,9},{9,10},{10,1... | collective-permute-start | bytes 786440 | tf_op jit(solution)/shard_map/ppermute | solution.py:339
  4.7 4.6 %collective-permute-start.3 = (bf16[256,512]{1,0:T(8,128)(2,1)S(1)}, bf16[256,512]{1,0:T(8,128)(2,1)S(1)}, u32[]{:S(2)}, u32[]{:S(2)}) collective-permute-start(bf16[256,512]{1,0:T(8,128)(2,1)S(1)} %get-tuple-element.69), channel_id=1, source_target_pairs={{0,15},{1,0},{2,1},{3,2},{4,3},{5,4},{6,5},{7,6},{8,7},{9,8},{10,9... | collective-permute-start | bytes 786440 | tf_op jit(solution)/shard_map/ppermute | solution.py:340
  9.3 0.0 collective-permute-start
  9.3 5.3 %collective-permute-start.1 = (bf16[256,512]{1,0:T(8,128)(2,1)}, bf16[256,512]{1,0:T(8,128)(2,1)S(1)}, u32[]{:S(2)}, u32[]{:S(2)}) collective-permute-start(bf16[256,512]{1,0:T(8,128)(2,1)} %get-tuple-element.71), channel_id=1, source_target_pairs={{0,15},{1,0},{2,1},{3,2},{4,3},{5,4},{6,5},{7,6},{8,7},{9,8},{10,9... | collective-permute-start | bytes 786440 | tf_op jit(solution)/shard_map/ppermute | solution.py:340
  14.6 0.8 reshape.9
  15.4 0.7 concatenate.3.meta
  16.1 0.9 %copy-done.2 = bf16[83,512]{1,0:T(8,128)(2,1)S(1)} copy-done((bf16[83,512]{1,0:T(8,128)(2,1)S(1)}, bf16[83,512]{1,0:T(8,128)(2,1)}, u32[]{:S(2)}) %copy-start.2) | copy-done | bytes 85016
  17.0 7.1 %shard_map.112 = (f32[1024,512]{1,0:T(8,128)S(1)}, f32[1024,512]{1,0:T(8,128)S(1)}, bf16[1024,512]{1,0:T(8,128)(2,1)S(1)}, bf16[512,1024]{1,0:T(8,128)(2,1)S(1)}...) custom-call(s32[43]{0:T(128)S(1)} %concatenate.3.meta, ...), custom_call_target="tpu_custom_call" | custom-call | flops 1073741824 | bytes 10485760 | tf_op jit(solution)/shard_map/pallas_call | solution.py:347
  24.1 0.0 copy-start.8
  24.1 0.8 copy-done.8
  24.9 0.0 collective-permute-done.2.low
  24.9 0.0 collective-permute-done.3.high
  24.9 0.0 copy-start.10
  24.9 2.0 %shard_map.114 = (bf16[1024,512]{1,0:T(8,128)(2,1)S(1)}, bf16[88,1024]{1,0:T(8,128)(2,1)S(1)}) custom-call(f32[1024,512]{1,0:T(8,128)S(1)} %get-tuple-element.41.acc, bf16[256,512]{1,0:T(8,128)(2,1)S(1)} %collective-permute-done.2.low, bf16[256,512]{1,0:T(8,128)(2,1)S(1)} %collective-permute-done.3.high, bf16[1024,512]{1,0:T(8,128)(2,1)S(1)} %get-tuple-element.37.halo_w, ...), custom_call_target="tpu_custom_call" | custom-call | flops 1073741824 | bytes 1048576 | tf_op jit(solution)/shard_map/pallas_call | solution.py:374
  26.9 2.8 %collective-permute-start.7 = (bf16[88,1024]{1,0:T(8,128)(2,1)S(1)}, bf16[88,1024]{1,0:T(8,128)(2,1)S(1)}, u32[]{:S(2)}, u32[]{:S(2)}) collective-permute-start(bf16[88,1024]{1,0:T(8,128)(2,1)S(1)} %get-tuple-element.42.own1), channel_id=1, source_target_pairs={{0,48},{16,0},{32,16},{48,32},{1,49},{17,1},{33,17},{49,33},{2,50}... | collective-permute-start | bytes 540680 | tf_op jit(solution)/shard_map/ppermute | solution.py:396
  29.7 0.0 collective-permute-done.low
  29.7 0.0 collective-permute-done.1.high
  29.7 2.7 %shard_map.113 = (bf16[1024,512]{1,0:T(8,128)(2,1)S(1)}, bf16[88,1024]{1,0:T(8,128)(2,1)}) custom-call(f32[1024,512]{1,0:T(8,128)S(1)} %get-tuple-element.36.acc, bf16[256,512]{1,0:T(8,128)(2,1)S(1)} %collective-permute-done.low, bf16[256,512]{1,0:T(8,128)(2,1)S(1)} %collective-permute-done.1.high, bf16[1024,512]{1,0:T(8,128)(2,1)S(1)} %get-tuple-element.37.halo_w, ...), custom_call_target="tpu_custom_call" | custom-call | flops 1073741824 | bytes 1048576 | tf_op jit(solution)/shard_map/pallas_call | solution.py:374
  32.4 0.0 copy-done
  32.4 0.0 copy-done.4
  32.4 0.0 copy-done.6
  32.4 0.1 collective-permute-start.4
  32.5 0.0 copy-done.10
  32.5 0.1 copy.13.var_weight
  32.6 1.0 %pad.8.target = bf16[88,1024]{1,0:T(8,128)(2,1)S(1)} pad(bf16[83,1024]{1,0:T(8,128)(2,1)} %bitcast.24, bf16[]{:T(256)} %constant.18.clone.1), padding=0_5x0_0 | pad | bytes 350210 | tf_op jit(solution)/shard_map/jit(_pad)/pad | solution.py:343
  33.6 0.8 collective-permute-start.5
  34.4 2.6 %collective-permute-start.6 = (bf16[88,1024]{1,0:T(8,128)(2,1)}, bf16[88,1024]{1,0:T(8,128)(2,1)S(1)}, u32[]{:S(2)}, u32[]{:S(2)}) collective-permute-start(bf16[88,1024]{1,0:T(8,128)(2,1)} %get-tuple-element.40.own0), channel_id=1, source_target_pairs={{0,48},{16,0},{32,16},{48,32},{1,49},{17,1},{33,17},{49,33},{2,50}... | collective-permute-start | bytes 540680 | tf_op jit(solution)/shard_map/ppermute | solution.py:396
  37.0 0.0 collective-permute-done.7.o21
  37.0 1.9 %collective-permute-start.9 = (bf16[88,1024]{1,0:T(8,128)(2,1)S(1)}, bf16[88,1024]{1,0:T(8,128)(2,1)S(1)}, u32[]{:S(2)}, u32[]{:S(2)}) collective-permute-start(bf16[88,1024]{1,0:T(8,128)(2,1)S(1)} %collective-permute-done.7.o21), channel_id=1, source_target_pairs={{0,48},{16,0},{32,16},{48,32},{1,49},{17,1},{33,17},{49,33},{2,50}... | collective-permute-start | bytes 540680 | tf_op jit(solution)/shard_map/ppermute | solution.py:396
  38.9 2.3 %collective-permute-done.4.o10 = bf16[88,1024]{1,0:T(8,128)(2,1)S(1)} collective-permute-done((bf16[88,1024]{1,0:T(8,128)(2,1)}, bf16[88,1024]{1,0:T(8,128)(2,1)S(1)}, u32[]{:S(2)}, u32[]{:S(2)}) %collective-permute-start.4) | collective-permute-done | bytes 180256 | tf_op jit(solution)/shard_map/ppermute | solution.py:396
  41.2 0.0 collective-permute-start.8
  41.2 1.5 %shard_map.116 = (bf16[512,1024]{1,0:T(8,128)(2,1)S(1)}, bf16[512,1024]{1,0:T(8,128)(2,1)S(1)}) custom-call(bf16[1024,512]{1,0:T(8,128)(2,1)S(1)} %get-tuple-element.45.lat.lat1, bf16[512,512]{1,0:T(8,128)(2,1)S(1)} %get-tuple-element.38.w_in), custom_call_target="tpu_custom_call" | custom-call | flops 1073741824 | bytes 1048576 | tf_op jit(solution)/shard_map/pallas_call | solution.py:384
  42.7 1.5 %shard_map.115 = (bf16[512,1024]{1,0:T(8,128)(2,1)S(1)}, bf16[512,1024]{1,0:T(8,128)(2,1)S(1)}) custom-call(bf16[1024,512]{1,0:T(8,128)(2,1)S(1)} %get-tuple-element.43.lat.lat0, bf16[512,512]{1,0:T(8,128)(2,1)S(1)} %get-tuple-element.38.w_in), custom_call_target="tpu_custom_call" | custom-call | flops 1073741824 | bytes 1048576 | tf_op jit(solution)/shard_map/pallas_call | solution.py:384
  44.2 0.0 copy-start.7
  44.2 0.0 copy-start.9
  44.2 0.6 collective-permute-done.5.o11
  44.9 0.0 collective-permute-done.6.o20
  44.9 0.0 collective-permute-done.9.o31
  44.9 3.0 %collective-permute-done.8.o30 = bf16[88,1024]{1,0:T(8,128)(2,1)S(1)} collective-permute-done((bf16[88,1024]{1,0:T(8,128)(2,1)S(1)}, bf16[88,1024]{1,0:T(8,128)(2,1)S(1)}, u32[]{:S(2)}, u32[]{:S(2)}) %collective-permute-start.8) | collective-permute-done | bytes 180256 | tf_op jit(solution)/shard_map/ppermute | solution.py:396
  47.9 0.0 copy-done.3
  47.9 0.0 copy-done.1
  47.9 4.1 %shard_map.117 = (bf16[512,1024]{1,0:T(8,128)(2,1)S(1)}, bf16[512,1024]{1,0:T(8,128)(2,1)S(1)}, f32[256,640]{1,0:T(8,128)S(1)}, bf16[256,640]{1,0:T(8,128)(2,1)S(1)}) custom-call(s32[43]{0:T(128)S(1)} %concatenate.3.meta, bf16[88,1024]{1,0:T(8,128)(2,1)} %get-tuple-element.40.own0, bf16[88,1024]{1,0:T(8,128)(2,1)S(1)} %get-tuple-element.42.own1, ...), custom_call_target="tpu_custom_call" | custom-call | flops 1073741824 | bytes 1048576 | tf_op jit(solution)/shard_map/pallas_call | solution.py:407
  52.0 0.1 collective-permute-start.12
  52.1 0.0 copy-done.7
  52.1 0.0 copy-start.5
  52.2 2.4 %shard_map.118 = (bf16[512,1024]{1,0:T(8,128)(2,1)S(1)}, bf16[512,1024]{1,0:T(8,128)(2,1)S(1)}, bf16[2,256,512]{2,1,0:T(8,128)(2,1)S(1)}, bf16[2,256,512]{2,1,0:T(8,128)(2,1)S(1)}) custom-call(bf16[512,1024]{1,0:T(8,128)(2,1)S(1)} %get-tuple-element.50.grad_pre0, bf16[512,1024]{1,0:T(8,128)(2,1)S(1)} %get-tuple-element.51.grad_pre1, ...), custom_call_target="tpu_custom_call" | custom-call | flops 2147483648 | bytes 1048576 | tf_op jit(solution)/shard_map/pallas_call | solution.py:432
  54.6 0.1 collective-permute-start.10
  54.7 5.3 %collective-permute-start.11 = (bf16[2,256,512]{2,1,0:T(8,128)(2,1)S(1)}, bf16[2,256,512]{2,1,0:T(8,128)(2,1)S(1)}, u32[]{:S(2)}, u32[]{:S(2)}) collective-permute-start(bf16[2,256,512]{2,1,0:T(8,128)(2,1)S(1)} %get-tuple-element.60), channel_id=1, source_target_pairs={{0,15},{1,0},{2,1},{3,2},{4,3},{5,4},{6,5},{7,6},{8,7},{9,8},{10,9... | collective-permute-start | bytes 1572872 | tf_op jit(solution)/shard_map/ppermute | solution.py:442
  60.0 0.0 collective-permute-done.12.swapped
  60.0 0.7 shard_map.121
  60.7 0.1 collective-permute-start.13
  60.7 1.2 %collective-permute-start.14 = (bf16[64,640]{1,0:T(8,128)(2,1)S(1)}, bf16[64,640]{1,0:T(8,128)(2,1)S(1)}, u32[]{:S(2)}, u32[]{:S(2)}) collective-permute-start(bf16[64,640]{1,0:T(8,128)(2,1)S(1)} %get-tuple-element.65), channel_id=1, source_target_pairs={{0,32},{16,48},{32,0},{48,16},{1,33},{17,49},{33,1},{49,17},{2,34}... | collective-permute-start | bytes 245768 | tf_op jit(solution)/shard_map/ppermute | solution.py:396
  61.9 2.0 %collective-permute-start.15 = (bf16[64,640]{1,0:T(8,128)(2,1)S(1)}, bf16[64,640]{1,0:T(8,128)(2,1)S(1)}, u32[]{:S(2)}, u32[]{:S(2)}) collective-permute-start(bf16[64,640]{1,0:T(8,128)(2,1)S(1)} %get-tuple-element.66), channel_id=1, source_target_pairs={{0,48},{16,0},{32,16},{48,32},{1,49},{17,1},{33,17},{49,33},{2,50}... | collective-permute-start | bytes 245768 | tf_op jit(solution)/shard_map/ppermute | solution.py:396
  64.0 5.2 %shard_map.119 = (f32[2,2048,512]{2,1,0:T(8,128)}, f32[2,2,256,512]{3,2,1,0:T(8,128)S(1)}) custom-call(bf16[512,1024]{1,0:T(8,128)(2,1)S(1)} %get-tuple-element.54.grad_grid0, bf16[512,1024]{1,0:T(8,128)(2,1)S(1)} %get-tuple-element.55.grad_grid1, bf16[2048,1024]{1,0:T(8,128)(2,1)S(1)} %copy-done.5), custom_call_target="tpu_custom_call" | custom-call | flops 4294967296 | bytes 8388608 | tf_op jit(solution)/shard_map/pallas_call | solution.py:456
  69.2 0.0 collective-permute-done.13.got1
  69.2 0.0 collective-permute-done.14.got2
  69.2 0.0 collective-permute-done.15.got3
  69.2 0.1 shard_map.122
  69.3 10.2 %all_to_all.5.got = bf16[16,4,640]{2,1,0:T(4,128)(2,1)S(1)} all-to-all(bf16[16,4,640]{2,1,0:T(4,128)(2,1)S(1)} %shard_map.122), channel_id=1, replica_groups=mesh['dp'=2,'member'=4,'space'=16] {'space'}, dimensions={0} | all-to-all | bytes 163840 | tf_op jit(solution)/shard_map/all_to_all | solution.py:480
  79.5 0.6 shard_map.123
  80.1 0.0 collective-permute-done.10.below
  80.1 0.0 collective-permute-done.11.above
  80.1 1.4 %shard_map.120 = f32[2,2048,512]{2,1,0:T(8,128)} custom-call(f32[2,2048,512]{2,1,0:T(8,128)} %get-tuple-element.57.base, f32[2,2,256,512]{3,2,1,0:T(8,128)S(1)} %get-tuple-element.58.edge.later, bf16[2,256,512]{2,1,0:T(8,128)(2,1)S(1)} %collective-permute-done.10.below, ...), custom_call_target="tpu_custom_call", output_to_operand_aliasing={{}: (0, {})} | custom-call | tf_op jit(solution)/shard_map/pallas_call | solution.py:489
  (9 shorter events, 0.0 us)
Async XLA Ops:
  2.7 22.2 %collective-permute-start.2 = (bf16[256,512]{1,0:T(8,128)(2,1)S(1)}, bf16[256,512]{1,0:T(8,128)(2,1)S(1)}, u32[]{:S(2)}, u32[]{:S(2)}) collective-permute-start(bf16[256,512]{1,0:T(8,128)(2,1)S(1)} %get-tuple-element.70), channel_id=1, source_target_pairs={{0,1},{1,2},{2,3},{3,4},{4,5},{5,6},{6,7},{7,8},{8,9},{9,10},{10,1... | collective-permute-start | bytes 786440 | tf_op jit(solution)/shard_map/ppermute | solution.py:339
  4.7 20.2 %collective-permute-start.3 = (bf16[256,512]{1,0:T(8,128)(2,1)S(1)}, bf16[256,512]{1,0:T(8,128)(2,1)S(1)}, u32[]{:S(2)}, u32[]{:S(2)}) collective-permute-start(bf16[256,512]{1,0:T(8,128)(2,1)S(1)} %get-tuple-element.69), channel_id=1, source_target_pairs={{0,15},{1,0},{2,1},{3,2},{4,3},{5,4},{6,5},{7,6},{8,7},{9,8},{10,9... | collective-permute-start | bytes 786440 | tf_op jit(solution)/shard_map/ppermute | solution.py:340
  9.3 20.5 %collective-permute-start = (bf16[256,512]{1,0:T(8,128)(2,1)}, bf16[256,512]{1,0:T(8,128)(2,1)S(1)}, u32[]{:S(2)}, u32[]{:S(2)}) collective-permute-start(bf16[256,512]{1,0:T(8,128)(2,1)} %get-tuple-element.72), channel_id=1, source_target_pairs={{0,1},{1,2},{2,3},{3,4},{4,5},{5,6},{6,7},{7,8},{8,9},{9,10},{10,1... | collective-permute-start | bytes 786440 | tf_op jit(solution)/shard_map/ppermute | solution.py:339
  9.3 20.5 %collective-permute-start.1 = (bf16[256,512]{1,0:T(8,128)(2,1)}, bf16[256,512]{1,0:T(8,128)(2,1)S(1)}, u32[]{:S(2)}, u32[]{:S(2)}) collective-permute-start(bf16[256,512]{1,0:T(8,128)(2,1)} %get-tuple-element.71), channel_id=1, source_target_pairs={{0,15},{1,0},{2,1},{3,2},{4,3},{5,4},{6,5},{7,6},{8,7},{9,8},{10,9... | collective-permute-start | bytes 786440 | tf_op jit(solution)/shard_map/ppermute | solution.py:340
  16.1 0.9 %copy-start.2 = (bf16[83,512]{1,0:T(8,128)(2,1)S(1)}, bf16[83,512]{1,0:T(8,128)(2,1)}, u32[]{:S(2)}) copy-start(bf16[83,512]{1,0:T(8,128)(2,1)} %w_out.1) | copy-start | bytes 254980
  24.1 0.8 copy-start.8
  24.9 7.6 %copy-start = (bf16[512,88]{1,0:T(8,128)(2,1)}, bf16[512,88]{1,0:T(8,128)(2,1)S(1)}, u32[]{:S(2)}) copy-start(bf16[512,88]{1,0:T(8,128)(2,1)S(1)} %get-tuple-element.49.w_out_t) | copy-start | bytes 270340
  24.9 7.6 %copy-start.4 = (bf16[2048,1024]{1,0:T(8,128)(2,1)}, bf16[2048,1024]{1,0:T(8,128)(2,1)S(1)}, u32[]{:S(2)}) copy-start(bf16[2048,1024]{1,0:T(8,128)(2,1)S(1)} %get-tuple-element.56.own_wt) | copy-start | bytes 12582916
  24.9 7.6 %copy-start.6 = (bf16[512,1024]{1,0:T(8,128)(2,1)}, bf16[512,1024]{1,0:T(8,128)(2,1)S(1)}, u32[]{:S(2)}) copy-start(bf16[512,1024]{1,0:T(8,128)(2,1)S(1)} %get-tuple-element.52.halo_wt) | copy-start | bytes 3145732
  24.9 7.6 %copy-start.10 = (f32[83]{0:T(128)S(1)}, f32[83]{0:T(128)}, u32[]{:S(2)}) copy-start(f32[83]{0:T(128)} %param.17) | copy-start | bytes 1000
  26.9 10.1 %collective-permute-start.7 = (bf16[88,1024]{1,0:T(8,128)(2,1)S(1)}, bf16[88,1024]{1,0:T(8,128)(2,1)S(1)}, u32[]{:S(2)}, u32[]{:S(2)}) collective-permute-start(bf16[88,1024]{1,0:T(8,128)(2,1)S(1)} %get-tuple-element.42.own1), channel_id=1, source_target_pairs={{0,48},{16,0},{32,16},{48,32},{1,49},{17,1},{33,17},{49,33},{2,50}... | collective-permute-start | bytes 540680 | tf_op jit(solution)/shard_map/ppermute | solution.py:396
  32.4 15.5 %copy-start.3 = (f32[1024]{0:T(1024)S(1)}, f32[1024]{0:T(1024)}, u32[]{:S(2)}) copy-start(f32[1024]{0:T(1024)} %param.16) | copy-start | bytes 12292
  32.4 8.8 %collective-permute-start.4 = (bf16[88,1024]{1,0:T(8,128)(2,1)}, bf16[88,1024]{1,0:T(8,128)(2,1)S(1)}, u32[]{:S(2)}, u32[]{:S(2)}) collective-permute-start(bf16[88,1024]{1,0:T(8,128)(2,1)} %get-tuple-element.40.own0), channel_id=1, source_target_pairs={{0,16},{16,32},{32,48},{48,0},{1,17},{17,33},{33,49},{49,1},{2,18}... | collective-permute-start | bytes 540680 | tf_op jit(solution)/shard_map/ppermute | solution.py:396
  32.6 15.3 %copy-start.1 = (bf16[512,88]{1,0:T(8,128)(2,1)S(1)}, bf16[512,88]{1,0:T(8,128)(2,1)}, u32[]{:S(2)}) copy-start(bf16[512,88]{1,0:T(8,128)(2,1)} %copy-done) | copy-start | bytes 270340
  33.6 11.3 %collective-permute-start.5 = (bf16[88,1024]{1,0:T(8,128)(2,1)S(1)}, bf16[88,1024]{1,0:T(8,128)(2,1)S(1)}, u32[]{:S(2)}, u32[]{:S(2)}) collective-permute-start(bf16[88,1024]{1,0:T(8,128)(2,1)S(1)} %get-tuple-element.42.own1), channel_id=1, source_target_pairs={{0,16},{16,32},{32,48},{48,0},{1,17},{17,33},{33,49},{49,1},{2,18}... | collective-permute-start | bytes 540680 | tf_op jit(solution)/shard_map/ppermute | solution.py:396
  34.4 10.5 %collective-permute-start.6 = (bf16[88,1024]{1,0:T(8,128)(2,1)}, bf16[88,1024]{1,0:T(8,128)(2,1)S(1)}, u32[]{:S(2)}, u32[]{:S(2)}) collective-permute-start(bf16[88,1024]{1,0:T(8,128)(2,1)} %get-tuple-element.40.own0), channel_id=1, source_target_pairs={{0,48},{16,0},{32,16},{48,32},{1,49},{17,1},{33,17},{49,33},{2,50}... | collective-permute-start | bytes 540680 | tf_op jit(solution)/shard_map/ppermute | solution.py:396
  37.0 7.9 %collective-permute-start.9 = (bf16[88,1024]{1,0:T(8,128)(2,1)S(1)}, bf16[88,1024]{1,0:T(8,128)(2,1)S(1)}, u32[]{:S(2)}, u32[]{:S(2)}) collective-permute-start(bf16[88,1024]{1,0:T(8,128)(2,1)S(1)} %collective-permute-done.7.o21), channel_id=1, source_target_pairs={{0,48},{16,0},{32,16},{48,32},{1,49},{17,1},{33,17},{49,33},{2,50}... | collective-permute-start | bytes 540680 | tf_op jit(solution)/shard_map/ppermute | solution.py:396
  41.2 6.7 %collective-permute-start.8 = (bf16[88,1024]{1,0:T(8,128)(2,1)S(1)}, bf16[88,1024]{1,0:T(8,128)(2,1)S(1)}, u32[]{:S(2)}, u32[]{:S(2)}) collective-permute-start(bf16[88,1024]{1,0:T(8,128)(2,1)S(1)} %collective-permute-done.4.o10), channel_id=1, source_target_pairs={{0,16},{16,32},{32,48},{48,0},{1,17},{17,33},{33,49},{49,1},{2,18}... | collective-permute-start | bytes 540680 | tf_op jit(solution)/shard_map/ppermute | solution.py:396
  44.2 7.9 %copy-start.7 = (bf16[512,1024]{1,0:T(8,128)(2,1)S(1)}, bf16[512,1024]{1,0:T(8,128)(2,1)}, u32[]{:S(2)}) copy-start(bf16[512,1024]{1,0:T(8,128)(2,1)} %copy-done.6) | copy-start | bytes 3145732
  44.2 7.9 %copy-start.9 = (bf16[512,512]{1,0:T(8,128)(2,1)S(1)}, bf16[512,512]{1,0:T(8,128)(2,1)}, u32[]{:S(2)}) copy-start(bf16[512,512]{1,0:T(8,128)(2,1)} %copy-done.8) | copy-start | bytes 1572868
  52.0 8.0 %collective-permute-start.12 = (bf16[256,640]{1,0:T(8,128)(2,1)S(1)}, bf16[256,640]{1,0:T(8,128)(2,1)S(1)}, u32[]{:S(2)}, u32[]{:S(2)}) collective-permute-start(bf16[256,640]{1,0:T(8,128)(2,1)S(1)} %get-tuple-element.62), channel_id=1, source_target_pairs={{0,64},{64,0},{1,65},{65,1},{2,66},{66,2},{3,67},{67,3},{4,68},{68... | collective-permute-start | bytes 983048 | tf_op jit(solution)/shard_map/ppermute | solution.py:430
  52.1 11.8 %copy-start.5 = (bf16[2048,1024]{1,0:T(8,128)(2,1)S(1)}, bf16[2048,1024]{1,0:T(8,128)(2,1)}, u32[]{:S(2)}) copy-start(bf16[2048,1024]{1,0:T(8,128)(2,1)} %copy-done.4) | copy-start | bytes 12582916
  54.6 25.6 %collective-permute-start.10 = (bf16[2,256,512]{2,1,0:T(8,128)(2,1)S(1)}, bf16[2,256,512]{2,1,0:T(8,128)(2,1)S(1)}, u32[]{:S(2)}, u32[]{:S(2)}) collective-permute-start(bf16[2,256,512]{2,1,0:T(8,128)(2,1)S(1)} %get-tuple-element.59), channel_id=1, source_target_pairs={{0,1},{1,2},{2,3},{3,4},{4,5},{5,6},{6,7},{7,8},{8,9},{9,10},{10,1... | collective-permute-start | bytes 1572872 | tf_op jit(solution)/shard_map/ppermute | solution.py:441
  54.7 25.5 %collective-permute-start.11 = (bf16[2,256,512]{2,1,0:T(8,128)(2,1)S(1)}, bf16[2,256,512]{2,1,0:T(8,128)(2,1)S(1)}, u32[]{:S(2)}, u32[]{:S(2)}) collective-permute-start(bf16[2,256,512]{2,1,0:T(8,128)(2,1)S(1)} %get-tuple-element.60), channel_id=1, source_target_pairs={{0,15},{1,0},{2,1},{3,2},{4,3},{5,4},{6,5},{7,6},{8,7},{9,8},{10,9... | collective-permute-start | bytes 1572872 | tf_op jit(solution)/shard_map/ppermute | solution.py:442
  60.7 8.5 %collective-permute-start.13 = (bf16[64,640]{1,0:T(8,128)(2,1)S(1)}, bf16[64,640]{1,0:T(8,128)(2,1)S(1)}, u32[]{:S(2)}, u32[]{:S(2)}) collective-permute-start(bf16[64,640]{1,0:T(8,128)(2,1)S(1)} %get-tuple-element.64), channel_id=1, source_target_pairs={{0,16},{16,32},{32,48},{48,0},{1,17},{17,33},{33,49},{49,1},{2,18}... | collective-permute-start | bytes 245768 | tf_op jit(solution)/shard_map/ppermute | solution.py:396
  60.7 8.5 %collective-permute-start.14 = (bf16[64,640]{1,0:T(8,128)(2,1)S(1)}, bf16[64,640]{1,0:T(8,128)(2,1)S(1)}, u32[]{:S(2)}, u32[]{:S(2)}) collective-permute-start(bf16[64,640]{1,0:T(8,128)(2,1)S(1)} %get-tuple-element.65), channel_id=1, source_target_pairs={{0,32},{16,48},{32,0},{48,16},{1,33},{17,49},{33,1},{49,17},{2,34}... | collective-permute-start | bytes 245768 | tf_op jit(solution)/shard_map/ppermute | solution.py:396
  61.9 7.3 %collective-permute-start.15 = (bf16[64,640]{1,0:T(8,128)(2,1)S(1)}, bf16[64,640]{1,0:T(8,128)(2,1)S(1)}, u32[]{:S(2)}, u32[]{:S(2)}) collective-permute-start(bf16[64,640]{1,0:T(8,128)(2,1)S(1)} %get-tuple-element.66), channel_id=1, source_target_pairs={{0,48},{16,0},{32,16},{48,32},{1,49},{17,1},{33,17},{49,33},{2,50}... | collective-permute-start | bytes 245768 | tf_op jit(solution)/shard_map/ppermute | solution.py:396

commit v3 on v2

--- a/solution.py
+++ b/solution.py
@@ -69,13 +69,42 @@
     return pl.ds(pl.multiple_of(start * size, size), size)
 
 
+def parity():
+    return lax.rem(lax.axis_index("space"), 2)
+
+
+def edges_kernel(lat, near0, far0, near1, far1, sems):
+    step = near0.shape[0]
+    last = lat.shape[1] - step
+    odd = parity()
+    top = pl.multiple_of((1 - odd) * last, step)
+    bottom = pl.multiple_of(odd * last, step)
+    copies = []
+    for m, (near, far) in enumerate(((near0, far0), (near1, far1))):
+        for out, start in ((near, top), (far, bottom)):
+            copies.append(
+                pltpu.make_async_copy(lat.at[m, pl.ds(start, step)], out, sems.at[len(copies)])
+            )
+            copies[-1].start()
+    for copy in copies:
+        copy.wait()
+
+
+def halo_slot(e, blocks, spaces):
+    at_space = lax.axis_index("space")
+    odd = parity()
+    below, above = e < HALO, e >= HALO + blocks
+    outside = (below & (at_space > 0)) | (above & (at_space < spaces - 1))
+    slot = jnp.where(below, e + (1 - odd) * HALO, e - HALO - blocks + odd * HALO)
+    return outside, jnp.where(below | above, slot, 0)
+
+
 def prepare_kernel(
-    meta, lat_hbm, weight_hbm, w_in_hbm, w_out,
-    acc0, acc1, halo_w, halo_wt, own_wt, w_in_v, w_in_t, w_out_v, w_out_t,
+    ids, count, lat_hbm, weight_hbm, w_in_hbm, w_out, acc0, acc1, halo_w, w_in_v, w_out_v,
     lat, weight, sems, *, spaces,
 ):
     tiles, slots, cells, nodes = weight.shape
-    members, blocks = lat.shape[0], lat.shape[1]
+    blocks = lat.shape[1]
     copies = [
         pltpu.make_async_copy(weight_hbm, weight, sems.at[0]),
         pltpu.make_async_copy(lat_hbm.at[0], lat.at[0], sems.at[1]),
@@ -84,59 +113,73 @@
     ]
     for c in copies:
         c.start()
-    at_space = meta[tiles * slots + tiles]
     halo_w[...] = jnp.zeros_like(halo_w)
+    w_out_v[...] = jnp.zeros_like(w_out_v)
+    w_out_v[: w_out.shape[0]] = w_out[...]
+    copies[0].wait()
+
+    def place_tile(t, carry):
+        for k in range(slots):
+            e = ids[k, t]
+            outside, slot = halo_slot(e, blocks, spaces)
+
+            @pl.when((k < count[t]) & outside)
+            def _():
+                halo_w[rows_at(t, cells), rows_at(slot, nodes)] += weight[t, k]
+
+        return carry
+
+    lax.fori_loop(0, tiles, place_tile, 0)
+
+    for m, acc in enumerate((acc0, acc1)):
+        copies[1 + m].wait()
+        for t in range(tiles):
+            parts, at = [], []
+            for k in range(slots):
+                e = ids[k, t]
+                mine = (k < count[t]) & (e >= HALO) & (e < HALO + blocks)
+                w = weight[t, k]
+                parts.append(jnp.where(mine, w, jnp.zeros_like(w)))
+                at.append(jnp.clip(e - HALO, 0, blocks - 1))
+            lhs = jnp.concatenate(parts, axis=1)
+            rhs = jnp.concatenate([lat[m, a] for a in at], axis=0)
+            acc[t * cells : (t + 1) * cells] = dot(lhs, rhs)
+    copies[3].wait()
+
+
+def turn_kernel(
+    ids, count, weight_hbm, w_in, w_out, later, halo_wt, own_wt, w_in_t, w_out_t, weight, sems,
+    *, spaces,
+):
+    tiles, slots, cells, nodes = weight.shape
+    blocks = own_wt.shape[0] // nodes
+    copy = pltpu.make_async_copy(weight_hbm, weight, sems.at[0])
+    copy.start()
     halo_wt[...] = jnp.zeros_like(halo_wt)
     own_wt[...] = jnp.zeros_like(own_wt)
-    copies[0].wait()
+    w_in_t[...] = w_in[...].T
+    w_out_t[...] = w_out[...].T
+    copy.wait()
 
     def place_tile(t, carry):
         for k in range(slots):
-            e = meta[k * tiles + t]
-            live = k < meta[slots * tiles + t]
-            w = weight[t, k]
-            wt = w.T
-            below = (e < HALO) & (at_space > 0)
-            above = (e >= HALO + blocks) & (at_space < spaces - 1)
+            e = ids[k, t]
+            live = k < count[t]
+            outside, slot = halo_slot(e, blocks, spaces)
             mine = (e >= HALO) & (e < HALO + blocks)
-            slot = jnp.where(e < HALO, e, jnp.where(mine, 0, e - blocks))
             block = jnp.clip(e - HALO, 0, blocks - 1)
 
-            @pl.when(live & (below | above))
+            @pl.when(live & outside)
             def _():
-                halo_w[rows_at(t, cells), rows_at(slot, nodes)] += w
-                halo_wt[rows_at(slot, nodes), rows_at(t, cells)] += wt
+                halo_wt[rows_at(slot, nodes), rows_at(t, cells)] += weight[t, k].T
 
             @pl.when(live & mine)
             def _():
-                own_wt[rows_at(block, nodes), rows_at(t, cells)] += wt
+                own_wt[rows_at(block, nodes), rows_at(t, cells)] += weight[t, k].T
 
         return carry
 
     lax.fori_loop(0, tiles, place_tile, 0)
-    for c in copies[1:]:
-        c.wait()
-
-    def gather_tile(t, carry):
-        parts, at = [], []
-        for k in range(slots):
-            e = meta[k * tiles + t]
-            mine = (k < meta[slots * tiles + t]) & (e >= HALO) & (e < HALO + blocks)
-            w = weight[t, k]
-            parts.append(jnp.where(mine, w, jnp.zeros_like(w)))
-            at.append(jnp.clip(e - HALO, 0, blocks - 1))
-        lhs = jnp.concatenate(parts, axis=1)
-        for m, acc in enumerate((acc0, acc1)):
-            rhs = jnp.concatenate([lat[m, a] for a in at], axis=0)
-            acc[rows_at(t, cells)] = dot(lhs, rhs)
-        return carry
-
-    lax.fori_loop(0, tiles, gather_tile, 0)
-    w_in_t[...] = w_in_v[...].T
-    variables = w_out.shape[0]
-    w_out_v[...] = jnp.zeros_like(w_out_v)
-    w_out_v[:variables] = w_out[...]
-    w_out_t[...] = w_out_v[...].T
 
 
 def gelu_parts(x):
@@ -148,13 +191,13 @@
 CHUNK = 256
 
 
-def fields_kernel(acc, low, high, halo_w, w_in, w_out, lat_out, fields):
+def fields_kernel(acc, near, far, halo_w, w_in, w_out, lat_out, fields):
     count = acc.shape[0]
-    half_k = low.shape[0]
+    half_k = near.shape[0]
     for start in range(0, count, 2 * CHUNK):
         at = slice(start, start + 2 * CHUNK)
-        total = acc[at] + dot(halo_w[at, :half_k], low[...])
-        total = total + dot(halo_w[at, half_k:], high[...])
+        total = acc[at] + dot(halo_w[at, :half_k], near[...])
+        total = total + dot(halo_w[at, half_k:], far[...])
         rounded = total.astype(bf16)
         lat_out[at] = rounded
         pre = dot(w_in[...], rounded, NT)
@@ -178,9 +221,9 @@
 
 
 def weights_kernel(
-    meta, own0, own1, o10, o11, o20, o21, o30, o31, target, area, var_weight,
+    own0, own1, o10, o11, o20, o21, o30, o31, target, area, var_weight,
     act0, act1, slope0, slope1, lat0, lat1, w_out_t,
-    grad_pre0, grad_pre1, keep, send, total_in, total_out, *, ensemble, states, dp_at,
+    grad_pre0, grad_pre1, keep, send, total_in, total_out, *, ensemble, states,
 ):
     count = own0.shape[1]
     others = (o10, o11, o20, o21, o30, o31)
@@ -218,7 +261,7 @@
             total_out[:, : part_out.shape[1]] += part_out
     rows = keep.shape[0]
     wide = total_in.shape[1]
-    here = meta[dp_at]
+    here = lax.axis_index("dp")
     stay, leave = rows_at(here, rows), rows_at(1 - here, rows)
     keep[:, :wide] = total_in[stay]
     keep[:, wide:] = total_out[stay]
@@ -226,14 +269,14 @@
     send[:, wide:] = total_out[leave].astype(bf16)
 
 
-def rim_kernel(grad_pre0, grad_pre1, halo_wt, w_in_t, grad_grid0, grad_grid1, low, high):
-    half_k = low.shape[1]
+def rim_kernel(grad_pre0, grad_pre1, halo_wt, w_in_t, grad_grid0, grad_grid1, near, far):
+    half_k = near.shape[1]
     for m, (grad_pre, grad_grid) in enumerate(
         ((grad_pre0, grad_grid0), (grad_pre1, grad_grid1))
     ):
         grad_grid[...] = dot(w_in_t[...], grad_pre[...]).astype(bf16)
-        low[m] = dot(halo_wt[:half_k], grad_grid[...], NT).astype(bf16)
-        high[m] = dot(halo_wt[half_k:], grad_grid[...], NT).astype(bf16)
+        near[m] = dot(halo_wt[:half_k], grad_grid[...], NT).astype(bf16)
+        far[m] = dot(halo_wt[half_k:], grad_grid[...], NT).astype(bf16)
 
 
 def owned_kernel(grad_grid0, grad_grid1, own_wt, out, edge, parts, sems):
@@ -259,16 +302,18 @@
         copy.wait()
 
 
-def add_rim_kernel(base, edge, below, above, out, parts, sems):
+def add_rim_kernel(base, edge, near, far, out, parts, sems):
     step = edge.shape[2]
     last = out.shape[1] - step
+    odd = parity()
     copies = []
-    for side, (start, got) in enumerate(((0, below), (last, above))):
+    for side, got in ((1 - odd, near), (odd, far)):
+        start = pl.multiple_of(side * last, step)
         for m in range(edge.shape[0]):
-            slot = side * edge.shape[0] + m
+            slot = len(copies)
             parts[slot] = edge[m, side] + got[m].astype(f32)
             copy = pltpu.make_async_copy(
-                parts.at[slot], out.at[m, start : start + step], sems.at[slot]
+                parts.at[slot], out.at[m, pl.ds(start, step)], sems.at[slot]
             )
             copy.start()
             copies.append(copy)
@@ -276,12 +321,12 @@
         copy.wait()
 
 
-def split_kernel(meta, kept, swapped, own, send1, send2, send3, total, *, member_at):
+def split_kernel(kept, swapped, own, send1, send2, send3, total):
     parts, rows = total.shape[0], total.shape[1]
     value = kept[...] + swapped[...].astype(f32)
     for p in range(parts):
         total[p] = value[p * rows : (p + 1) * rows]
-    here = meta[member_at]
+    here = lax.axis_index("member")
     own[...] = total[here]
     for d, out in ((1, send1), (2, send2), (3, send3)):
         out[...] = total[lax.rem(here + d, parts)].astype(out.dtype)
@@ -321,56 +366,52 @@
     rim_rows = 2 * edge_rows
     spaces = lax.axis_size("space")
     chips = lax.axis_size("member")
-    meta = jnp.concatenate(
-        [
-            block_ids.T.reshape(-1),
-            block_count,
-            jnp.stack(
-                [lax.axis_index("space"), lax.axis_index("dp"), lax.axis_index("member")]
-            ).astype(jnp.int32),
-        ]
-    )
-    dp_at = tiles * slots + tiles + 1
-    member_at = dp_at + 1
-
-    flat = latents[0]
+    ids = block_ids.T
+    first = [(i, i ^ 1) for i in range(spaces)]
+    second = [(i, ((i + 1) ^ 1) - 1) for i in range(spaces)]
+    second = [(i, j % spaces) for i, j in second]
+
+    edges = pl.pallas_call(
+        edges_kernel,
+        in_specs=[hbm()],
+        out_specs=[vmem()] * 4,
+        out_shape=[shape((edge_rows, feature), bf16)] * 4,
+        scratch_shapes=[pltpu.SemaphoreType.DMA((4,))],
+        compiler_params=params(8),
+    )(in_hbm(latents[0]))
     halos = []
     for m in range(members):
-        low = lax.ppermute(flat[m, -edge_rows:], "space", ring(spaces, 1))
-        high = lax.ppermute(flat[m, :edge_rows], "space", ring(spaces, -1))
-        halos.append((low, high))
+        near = lax.ppermute(edges[2 * m], "space", first)
+        far = lax.ppermute(edges[2 * m + 1], "space", second)
+        halos.append((near, far))
 
     target = jnp.pad(targets[0], ((0, rows_v - variables), (0, 0)))
     scale_v = jnp.pad(var_weight, (0, rows_v - variables))[:, None]
     scale_n = area[None, :]
 
-    acc0, acc1, halo_w, halo_wt, own_wt, w_in_v, w_in_t, w_out_v, w_out_t = pl.pallas_call(
+    acc0, acc1, halo_w, w_in_v, w_out_v = pl.pallas_call(
         functools.partial(prepare_kernel, spaces=spaces),
-        in_specs=[smem(), hbm(), hbm(), hbm(), vmem()],
-        out_specs=[vmem()] * 9,
+        in_specs=[smem(), smem(), hbm(), hbm(), hbm(), vmem()],
+        out_specs=[vmem()] * 5,
         out_shape=[
             held((n, feature), f32),
             held((n, feature), f32),
             held((n, rim_rows), bf16),
-            held((rim_rows, n), bf16),
-            held((blocks * nodes, n), bf16),
             held((hidden, feature), bf16),
-            held((feature, hidden), bf16),
             held((rows_v, hidden), bf16),
-            held((hidden, rows_v), bf16),
         ],
         scratch_shapes=[
             pltpu.VMEM(lat.shape, bf16),
             pltpu.VMEM(edge_weight.shape, bf16),
             pltpu.SemaphoreType.DMA((4,)),
         ],
-        compiler_params=params(28),
+        compiler_params=params(24),
         cost_estimate=cost(2 * n * slots * nodes * feature * members, 10 * MIB),
-    )(meta, in_hbm(lat), in_hbm(edge_weight), in_hbm(w_in), w_out)
+    )(ids, block_count, in_hbm(lat), in_hbm(edge_weight), in_hbm(w_in), in_hbm(w_out))
 
     grid_latent, fields, acts, slopes = [], [], [], []
     for m, acc in enumerate((acc0, acc1)):
-        low, high = halos[m]
+        near, far = halos[m]
         lat_m, fields_m = pl.pallas_call(
             fields_kernel,
             in_specs=[vmem()] * 6,
@@ -378,7 +419,7 @@
             out_shape=[held((n, feature), bf16), shape((rows_v, n), bf16)],
             compiler_params=params(16),
             cost_estimate=cost(4 * n * feature * hidden, MIB, n * hidden),
-        )(*in_vmem(acc), low, high, *in_vmem(halo_w, w_in_v, w_out_v))
+        )(*in_vmem(acc), near, far, *in_vmem(halo_w, w_in_v, w_out_v))
         grid_latent.append(lat_m)
         fields.append(fields_m)
         act_m, slope_m = pl.pallas_call(
@@ -392,6 +433,21 @@
         acts.append(act_m)
         slopes.append(slope_m)
 
+    halo_wt, own_wt, w_in_t, w_out_t = pl.pallas_call(
+        functools.partial(turn_kernel, spaces=spaces),
+        in_specs=[smem(), smem(), hbm(), vmem(), vmem(), anywhere()],
+        out_specs=[vmem()] * 4,
+        out_shape=[
+            held((rim_rows, n), bf16),
+            held((blocks * nodes, n), bf16),
+            held((feature, hidden), bf16),
+            held((hidden, rows_v), bf16),
+        ],
+        scratch_shapes=[pltpu.VMEM(edge_weight.shape, bf16), pltpu.SemaphoreType.DMA((1,))],
+        compiler_params=params(16),
+        cost_estimate=cost(MIB, 6 * MIB),
+    )(ids, block_count, in_hbm(edge_weight), *in_vmem(w_in_v, w_out_v), fields[1])
+
     def along(x, distance):
         return lax.ppermute(x, "member", ring(chips, distance))
 
@@ -409,9 +465,8 @@
             weights_kernel,
             ensemble=members * chips,
             states=targets.shape[0] * lax.axis_size("dp"),
-            dp_at=dp_at,
         ),
-        in_specs=[smem()] + [vmem()] * 18,
+        in_specs=[vmem()] * 18,
         out_specs=[vmem()] * 4,
         out_shape=[
             held((hidden, n), bf16),
@@ -423,13 +478,13 @@
         compiler_params=params(20),
         cost_estimate=cost(4 * n * feature * hidden, MIB),
     )(
-        meta, *fields, left0, left1, right0, right1, far0, far1, target, scale_n, scale_v,
+        *fields, left0, left1, right0, right1, far0, far1, target, scale_n, scale_v,
         *in_vmem(*acts, *slopes, *grid_latent, w_out_t),
     )
 
     swapped = lax.ppermute(send, "dp", [(0, 1), (1, 0)])
 
-    grad_grid0, grad_grid1, rim_low, rim_high = pl.pallas_call(
+    grad_grid0, grad_grid1, rim_near, rim_far = pl.pallas_call(
         rim_kernel,
         in_specs=[vmem()] * 4,
         out_specs=[vmem()] * 4,
@@ -438,19 +493,19 @@
         cost_estimate=cost(8 * n * feature * hidden, MIB),
     )(*in_vmem(grad_pre0, grad_pre1, halo_wt, w_in_t))
 
-    from_below = lax.ppermute(rim_high, "space", ring(spaces, 1))
-    from_above = lax.ppermute(rim_low, "space", ring(spaces, -1))
-
     quarter = half_rows // chips
     kept, *sends = pl.pallas_call(
-        functools.partial(split_kernel, member_at=member_at),
-        in_specs=[smem(), vmem(), vmem()],
+        split_kernel,
+        in_specs=[vmem(), vmem()],
         out_specs=[vmem()] * 4,
         out_shape=[shape((quarter, wide), f32)] + [shape((quarter, wide), bf16)] * 3,
         scratch_shapes=[pltpu.VMEM((chips, quarter, wide), f32)],
         compiler_params=params(8),
-    )(meta, keep, swapped)
+    )(keep, swapped)
     got = [along(s, d) for d, s in zip((1, 2, 3), sends)]
+
+    got_near = lax.ppermute(rim_near, "space", first)
+    got_far = lax.ppermute(rim_far, "space", second)
 
     middle = blocks // HALO - 2
     owned, edge = pl.pallas_call(
@@ -497,7 +552,7 @@
         ],
         input_output_aliases={0: 0},
         compiler_params=params(8),
-    )(owned, *in_vmem(edge), from_below, from_above)
+    )(owned, *in_vmem(edge), got_near, got_far)
     return grad_latent[None], grad_w_in, grad_w_out.T
 
 

time: 82 us -> 72.9 us (0.89)
  local copies, waits for them, and re-layouts: 6.33 us -> 1.06 us
  waiting for transfers between devices: 5.94 us -> 3.21 us
  starting transfers between devices: 28.9 us -> 27.7 us
    pallas_call x1 -> x3, Pallas kernels: 0.66 us -> 5.31 us  [the longest x1 3.97 us: local(): pl.pallas_call(functools.partial(turn_kernel, spaces=spaces), in_specs=[s...]
    ppermute x9, waiting for transfers between devices: 5.92 us -> 2.2 us  [along(): return lax.ppermute(x, 'member', ring(chips, distance))]
    ppermute x6, starting transfers between devices: 17.3 us -> 14.5 us  [the longest x2 6.6 us: local(): far = lax.ppermute(edges[2 * m + 1], 'space', second)]
    pallas_call x1, Pallas kernels: 7.07 us -> 4.32 us  [local(): pl.pallas_call(functools.partial(prepare_kernel, spaces=spaces), in_specs...]
    squeeze x1 -> x0, local copies, waits for them, and re-layouts: 2.05 us -> none  [local(): high = lax.ppermute(flat[m, :edge_rows], 'space', ring(spaces, -1))]
    unnamed x22 -> x8, local copies, waits for them, and re-layouts: 1.71 us -> 0.02 us
    ppermute x9, starting transfers between devices: 11.5 us -> 13.1 us  [along(): return lax.ppermute(x, 'member', ring(chips, distance))]
    ppermute x6, waiting for transfers between devices: 0.02 us -> 1.01 us  [the longest x2 1 us: local(): far = lax.ppermute(edges[2 * m + 1], 'space', second)]
  transfers between devices with their start and end apart: 16 -> 16, of which waited for: 3 -> 3; matrix products, arithmetic and copies ran while one was open for 3% -> 1% of each run, Pallas kernels for 29% -> 32%
where the time goes in v3:
time: 72.9 us; the launch traced here: 72.6 us
  Pallas kernels  29.4 us (40%)
  starting transfers between devices  27.7 us (38%)
  blocking collectives  10.2 us (14%)
  waiting for transfers between devices  3.21 us (4%)
  local copies, waits for them, and re-layouts  1.06 us (1%)
  between operations  1.01 us (1%)
    ppermute x9, starting transfers between devices, along(): return lax.ppermute(x, 'member', ring(chips, distance))  13.1 us
    all_to_all x1, blocking collectives, local(): spread = lax.all_to_all(spread, 'space', 0, 0, tiled=True)  10.2 us
    ppermute x2, starting transfers between devices, local(): far = lax.ppermute(edges[2 * m + 1], 'space', second)  6.6 us
    ppermute x1, starting transfers between devices, local(): got_far = lax.ppermute(rim_far, 'space', second)  5.74 us
    pallas_call x1, Pallas kernels, local(): pl.pallas_call(owned_kernel, in_specs=[vmem()] * 3, out_specs=[hbm(), vme...  5.16 us
    pallas_call x1, Pallas kernels, local(): pl.pallas_call(functools.partial(prepare_kernel, spaces=spaces), in_specs...  4.32 us
    pallas_call x1, Pallas kernels, local(): pl.pallas_call(functools.partial(turn_kernel, spaces=spaces), in_specs=[s...  3.97 us
    pallas_call x2, Pallas kernels, local(): pl.pallas_call(fields_kernel, in_specs=[vmem()] * 6, out_specs=[vmem()] *...  3.9 us
  transfers between devices with their start and end apart: 16, of which 3 were waited for; matrix products, arithmetic and copies ran while one was open for 1% of the time, Pallas kernels for 32%

profile of v3, /device:TPU:0, one launch (start us, length us, event | category | flops | bytes accessed | tf_op | source)
XLA Modules:
  0.0 72.6 jit_solution(13361629957458257623)
XLA Ops:
  0.6 0.0 copy-start
  0.6 0.0 copy-start.2
  0.7 1.2 %shard_map.113 = (bf16[256,512]{1,0:T(8,128)(2,1)S(1)}, bf16[256,512]{1,0:T(8,128)(2,1)S(1)}, bf16[256,512]{1,0:T(8,128)(2,1)S(1)}, bf16[256,512]{1,0:T(8,128)(2,1)S(1)}) custom-call(bf16[2,2048,512]{2,1,0:T(8,128)(2,1)} %bitcast.12), custom_call_target="tpu_custom_call" | custom-call | tf_op jit(solution)/shard_map/pallas_call | solution.py:374
  1.9 2.1 %collective-permute-start.2 = (bf16[256,512]{1,0:T(8,128)(2,1)S(1)}, bf16[256,512]{1,0:T(8,128)(2,1)S(1)}, u32[]{:S(2)}, u32[]{:S(2)}) collective-permute-start(bf16[256,512]{1,0:T(8,128)(2,1)S(1)} %get-tuple-element.48), channel_id=1, source_target_pairs={{0,1},{1,0},{2,3},{3,2},{4,5},{5,4},{6,7},{7,6},{8,9},{9,8},{10,11... | collective-permute-start | bytes 786440 | tf_op jit(solution)/shard_map/ppermute | solution.py:384
  4.0 5.0 %collective-permute-start.3 = (bf16[256,512]{1,0:T(8,128)(2,1)S(1)}, bf16[256,512]{1,0:T(8,128)(2,1)S(1)}, u32[]{:S(2)}, u32[]{:S(2)}) collective-permute-start(bf16[256,512]{1,0:T(8,128)(2,1)S(1)} %get-tuple-element.49), channel_id=1, source_target_pairs={{0,15},{1,2},{2,1},{3,4},{4,3},{5,6},{6,5},{7,8},{8,7},{9,10},{10,... | collective-permute-start | bytes 786440 | tf_op jit(solution)/shard_map/ppermute | solution.py:385
  8.9 0.0 collective-permute-start
  8.9 1.6 %collective-permute-start.1 = (bf16[256,512]{1,0:T(8,128)(2,1)S(1)}, bf16[256,512]{1,0:T(8,128)(2,1)S(1)}, u32[]{:S(2)}, u32[]{:S(2)}) collective-permute-start(bf16[256,512]{1,0:T(8,128)(2,1)S(1)} %get-tuple-element.42), channel_id=1, source_target_pairs={{0,15},{1,2},{2,1},{3,4},{4,3},{5,6},{6,5},{7,8},{8,7},{9,10},{10,... | collective-permute-start | bytes 786440 | tf_op jit(solution)/shard_map/ppermute | solution.py:385
  10.6 0.0 copy-done
  10.6 0.0 copy-done.2
  10.6 4.3 %shard_map.112 = (f32[1024,512]{1,0:T(8,128)S(1)}, f32[1024,512]{1,0:T(8,128)S(1)}, bf16[1024,512]{1,0:T(8,128)(2,1)S(1)}, bf16[512,512]{1,0:T(8,128)(2,1)S(1)}, bf16[88,512]{1,0:T(8,128)(2,1)S(1)}) custom-call(s32[4,8]{1,0:T(4,128)S(1)} %bitcast.9, s32[8]{0:T(128)S(1)} %copy-done.2, bf16[2,16,128,512]{3,2,1,0:T(8,128)(2,1)} %bitcast.13, ...), custom_call_target="tpu_custom_call" | custom-call | flops 1073741824 | bytes 10485760 | tf_op jit(solution)/shard_map/pallas_call | solution.py:392
  14.9 0.0 collective-permute-done.2.near
  14.9 1.0 %collective-permute-done.3.far = bf16[256,512]{1,0:T(8,128)(2,1)S(1)} collective-permute-done((bf16[256,512]{1,0:T(8,128)(2,1)S(1)}, bf16[256,512]{1,0:T(8,128)(2,1)S(1)}, u32[]{:S(2)}, u32[]{:S(2)}) %collective-permute-start.3) | collective-permute-done | bytes 262176 | tf_op jit(solution)/shard_map/ppermute | solution.py:385
  15.9 0.0 copy-start.3
  15.9 1.9 %shard_map.115 = (bf16[1024,512]{1,0:T(8,128)(2,1)S(1)}, bf16[88,1024]{1,0:T(8,128)(2,1)S(1)}) custom-call(f32[1024,512]{1,0:T(8,128)S(1)} %get-tuple-element.47.acc, bf16[256,512]{1,0:T(8,128)(2,1)S(1)} %collective-permute-done.2.near, bf16[256,512]{1,0:T(8,128)(2,1)S(1)} %collective-permute-done.3.far, bf16[1024,512]{1,0:T(8,128)(2,1)S(1)} %get-tuple-element.43.halo_w, ...), custom_call_target="tpu_custom_call" | custom-call | flops 1073741824 | bytes 1048576 | tf_op jit(solution)/shard_map/pallas_call | solution.py:415
  17.9 2.8 %collective-permute-start.7 = (bf16[88,1024]{1,0:T(8,128)(2,1)S(1)}, bf16[88,1024]{1,0:T(8,128)(2,1)S(1)}, u32[]{:S(2)}, u32[]{:S(2)}) collective-permute-start(bf16[88,1024]{1,0:T(8,128)(2,1)S(1)} %get-tuple-element.50.later.own1), channel_id=1, source_target_pairs={{0,48},{16,0},{32,16},{48,32},{1,49},{17,1},{33,17},{49,33},{2,50}... | collective-permute-start | bytes 540680 | tf_op jit(solution)/shard_map/ppermute | solution.py:452
  20.7 0.0 collective-permute-done.near
  20.7 0.0 collective-permute-done.1.far
  20.7 1.9 %shard_map.114 = (bf16[1024,512]{1,0:T(8,128)(2,1)S(1)}, bf16[88,1024]{1,0:T(8,128)(2,1)S(1)}) custom-call(f32[1024,512]{1,0:T(8,128)S(1)} %get-tuple-element.40.acc, bf16[256,512]{1,0:T(8,128)(2,1)S(1)} %collective-permute-done.near, bf16[256,512]{1,0:T(8,128)(2,1)S(1)} %collective-permute-done.1.far, bf16[1024,512]{1,0:T(8,128)(2,1)S(1)} %get-tuple-element.43.halo_w, ...), custom_call_target="tpu_custom_call" | custom-call | flops 1073741824 | bytes 1048576 | tf_op jit(solution)/shard_map/pallas_call | solution.py:415
  22.7 1.5 %collective-permute-start.4 = (bf16[88,1024]{1,0:T(8,128)(2,1)S(1)}, bf16[88,1024]{1,0:T(8,128)(2,1)S(1)}, u32[]{:S(2)}, u32[]{:S(2)}) collective-permute-start(bf16[88,1024]{1,0:T(8,128)(2,1)S(1)} %get-tuple-element.46.own0), channel_id=1, source_target_pairs={{0,16},{16,32},{32,48},{48,0},{1,17},{17,33},{33,49},{49,1},{2,18}... | collective-permute-start | bytes 540680 | tf_op jit(solution)/shard_map/ppermute | solution.py:452
  24.2 0.0 copy-done.3
  24.2 0.1 copy.13.var_weight
  24.3 0.9 %pad.8.target = bf16[88,1024]{1,0:T(8,128)(2,1)S(1)} pad(bf16[83,1024]{1,0:T(8,128)(2,1)} %bitcast.15, bf16[]{:T(256)} %constant.3.clone.1), padding=0_5x0_0 | pad | bytes 350210 | tf_op jit(solution)/shard_map/jit(_pad)/pad | solution.py:388
  25.3 1.5 %collective-permute-start.5 = (bf16[88,1024]{1,0:T(8,128)(2,1)S(1)}, bf16[88,1024]{1,0:T(8,128)(2,1)S(1)}, u32[]{:S(2)}, u32[]{:S(2)}) collective-permute-start(bf16[88,1024]{1,0:T(8,128)(2,1)S(1)} %get-tuple-element.50.later.own1), channel_id=1, source_target_pairs={{0,16},{16,32},{32,48},{48,0},{1,17},{17,33},{33,49},{49,1},{2,18}... | collective-permute-start | bytes 540680 | tf_op jit(solution)/shard_map/ppermute | solution.py:452
  26.8 1.8 %collective-permute-start.6 = (bf16[88,1024]{1,0:T(8,128)(2,1)S(1)}, bf16[88,1024]{1,0:T(8,128)(2,1)S(1)}, u32[]{:S(2)}, u32[]{:S(2)}) collective-permute-start(bf16[88,1024]{1,0:T(8,128)(2,1)S(1)} %get-tuple-element.46.own0), channel_id=1, source_target_pairs={{0,48},{16,0},{32,16},{48,32},{1,49},{17,1},{33,17},{49,33},{2,50}... | collective-permute-start | bytes 540680 | tf_op jit(solution)/shard_map/ppermute | solution.py:452
  28.6 4.0 %shard_map.118 = (bf16[512,1024]{1,0:T(8,128)(2,1)S(1)}, bf16[2048,1024]{1,0:T(8,128)(2,1)S(1)}, bf16[512,512]{1,0:T(8,128)(2,1)S(1)}, bf16[512,88]{1,0:T(8,128)(2,1)S(1)}) custom-call(s32[4,8]{1,0:T(4,128)S(1)} %bitcast.10, s32[8]{0:T(128)S(1)} %copy-done.2, bf16[8,4,128,128]{3,2,1,0:T(8,128)(2,1)} %weight_hbm.3, ...), custom_call_target="tpu_custom_call" | custom-call | flops 1048576 | bytes 6291456 | tf_op jit(solution)/shard_map/pallas_call | solution.py:436
  32.5 0.0 copy-start.1
  32.5 0.0 collective-permute-done.7.o21
  32.6 0.6 collective-permute-start.9
  33.2 0.0 collective-permute-done.4.o10
  33.2 1.5 %collective-permute-start.8 = (bf16[88,1024]{1,0:T(8,128)(2,1)S(1)}, bf16[88,1024]{1,0:T(8,128)(2,1)S(1)}, u32[]{:S(2)}, u32[]{:S(2)}) collective-permute-start(bf16[88,1024]{1,0:T(8,128)(2,1)S(1)} %collective-permute-done.4.o10), channel_id=1, source_target_pairs={{0,16},{16,32},{32,48},{48,0},{1,17},{17,33},{33,49},{49,1},{2,18}... | collective-permute-start | bytes 540680 | tf_op jit(solution)/shard_map/ppermute | solution.py:452
  34.7 1.5 %shard_map.117 = (bf16[512,1024]{1,0:T(8,128)(2,1)S(1)}, bf16[512,1024]{1,0:T(8,128)(2,1)S(1)}) custom-call(bf16[1024,512]{1,0:T(8,128)(2,1)S(1)} %get-tuple-element.53.lat.lat1, bf16[512,512]{1,0:T(8,128)(2,1)S(1)} %get-tuple-element.44.w_in), custom_call_target="tpu_custom_call" | custom-call | flops 1073741824 | bytes 1048576 | tf_op jit(solution)/shard_map/pallas_call | solution.py:425
  36.2 1.5 %shard_map.116 = (bf16[512,1024]{1,0:T(8,128)(2,1)S(1)}, bf16[512,1024]{1,0:T(8,128)(2,1)S(1)}) custom-call(bf16[1024,512]{1,0:T(8,128)(2,1)S(1)} %get-tuple-element.51.lat.lat0, bf16[512,512]{1,0:T(8,128)(2,1)S(1)} %get-tuple-element.44.w_in), custom_call_target="tpu_custom_call" | custom-call | flops 1073741824 | bytes 1048576 | tf_op jit(solution)/shard_map/pallas_call | solution.py:425
  37.7 0.0 collective-permute-done.5.o11
  37.7 0.0 collective-permute-done.6.o20
  37.7 0.4 collective-permute-done.9.o31
  38.1 1.8 %collective-permute-done.8.o30 = bf16[88,1024]{1,0:T(8,128)(2,1)S(1)} collective-permute-done((bf16[88,1024]{1,0:T(8,128)(2,1)S(1)}, bf16[88,1024]{1,0:T(8,128)(2,1)S(1)}, u32[]{:S(2)}, u32[]{:S(2)}) %collective-permute-start.8) | collective-permute-done | bytes 180256 | tf_op jit(solution)/shard_map/ppermute | solution.py:452
  39.9 0.0 copy-done.1
  39.9 3.3 %shard_map.119 = (bf16[512,1024]{1,0:T(8,128)(2,1)S(1)}, bf16[512,1024]{1,0:T(8,128)(2,1)S(1)}, f32[256,640]{1,0:T(8,128)S(1)}, bf16[256,640]{1,0:T(8,128)(2,1)S(1)}) custom-call(bf16[88,1024]{1,0:T(8,128)(2,1)S(1)} %get-tuple-element.46.own0, bf16[88,1024]{1,0:T(8,128)(2,1)S(1)} %get-tuple-element.50.later.own1, ...), custom_call_target="tpu_custom_call" | custom-call | flops 1073741824 | bytes 1048576 | tf_op jit(solution)/shard_map/pallas_call | solution.py:463
  43.2 0.1 collective-permute-start.12
  43.3 2.3 %shard_map.120 = (bf16[512,1024]{1,0:T(8,128)(2,1)S(1)}, bf16[512,1024]{1,0:T(8,128)(2,1)S(1)}, bf16[2,256,512]{2,1,0:T(8,128)(2,1)S(1)}, bf16[2,256,512]{2,1,0:T(8,128)(2,1)S(1)}) custom-call(bf16[512,1024]{1,0:T(8,128)(2,1)S(1)} %get-tuple-element.58.grad_pre0, bf16[512,1024]{1,0:T(8,128)(2,1)S(1)} %get-tuple-element.59.grad_pre1, ...), custom_call_target="tpu_custom_call" | custom-call | flops 2147483648 | bytes 1048576 | tf_op jit(solution)/shard_map/pallas_call | solution.py:487
  45.6 0.1 collective-permute-start.10
  45.7 5.7 %collective-permute-start.11 = (bf16[2,256,512]{2,1,0:T(8,128)(2,1)S(1)}, bf16[2,256,512]{2,1,0:T(8,128)(2,1)S(1)}, u32[]{:S(2)}, u32[]{:S(2)}) collective-permute-start(bf16[2,256,512]{2,1,0:T(8,128)(2,1)S(1)} %get-tuple-element.68), channel_id=1, source_target_pairs={{0,15},{1,2},{2,1},{3,4},{4,3},{5,6},{6,5},{7,8},{8,7},{9,10},{10,... | collective-permute-start | bytes 1572872 | tf_op jit(solution)/shard_map/ppermute | solution.py:508
  51.5 0.0 collective-permute-done.12.swapped
  51.5 0.1 shard_map.123
  51.6 0.1 collective-permute-start.13
  51.7 1.5 %collective-permute-start.14 = (bf16[64,640]{1,0:T(8,128)(2,1)S(1)}, bf16[64,640]{1,0:T(8,128)(2,1)S(1)}, u32[]{:S(2)}, u32[]{:S(2)}) collective-permute-start(bf16[64,640]{1,0:T(8,128)(2,1)S(1)} %get-tuple-element.73), channel_id=1, source_target_pairs={{0,32},{16,48},{32,0},{48,16},{1,33},{17,49},{33,1},{49,17},{2,34}... | collective-permute-start | bytes 245768 | tf_op jit(solution)/shard_map/ppermute | solution.py:452
  53.1 1.8 %collective-permute-start.15 = (bf16[64,640]{1,0:T(8,128)(2,1)S(1)}, bf16[64,640]{1,0:T(8,128)(2,1)S(1)}, u32[]{:S(2)}, u32[]{:S(2)}) collective-permute-start(bf16[64,640]{1,0:T(8,128)(2,1)S(1)} %get-tuple-element.74), channel_id=1, source_target_pairs={{0,48},{16,0},{32,16},{48,32},{1,49},{17,1},{33,17},{49,33},{2,50}... | collective-permute-start | bytes 245768 | tf_op jit(solution)/shard_map/ppermute | solution.py:452
  54.9 5.2 %shard_map.121 = (f32[2,2048,512]{2,1,0:T(8,128)}, f32[2,2,256,512]{3,2,1,0:T(8,128)S(1)}) custom-call(bf16[512,1024]{1,0:T(8,128)(2,1)S(1)} %get-tuple-element.62.grad_grid0, bf16[512,1024]{1,0:T(8,128)(2,1)S(1)} %get-tuple-element.63.grad_grid1, bf16[2048,1024]{1,0:T(8,128)(2,1)S(1)} %get-tuple-element.64.own_wt), custom_call_target="tpu_custom_call" | custom-call | flops 4294967296 | bytes 8388608 | tf_op jit(solution)/shard_map/pallas_call | solution.py:511
  60.1 0.0 collective-permute-done.13.got1
  60.1 0.0 collective-permute-done.14.got2
  60.1 0.0 collective-permute-done.15.got3
  60.1 0.1 shard_map.124
  60.1 10.2 %all_to_all.5.got = bf16[16,4,640]{2,1,0:T(4,128)(2,1)S(1)} all-to-all(bf16[16,4,640]{2,1,0:T(4,128)(2,1)S(1)} %shard_map.124), channel_id=1, replica_groups=mesh['dp'=2,'member'=4,'space'=16] {'space'}, dimensions={0} | all-to-all | bytes 163840 | tf_op jit(solution)/shard_map/all_to_all | solution.py:535
  70.4 0.6 shard_map.125
  71.0 0.0 collective-permute-done.10.near
  71.0 0.0 collective-permute-done.11.far
  71.0 1.4 %shard_map.122 = f32[2,2048,512]{2,1,0:T(8,128)} custom-call(f32[2,2048,512]{2,1,0:T(8,128)} %get-tuple-element.65.base, f32[2,2,256,512]{3,2,1,0:T(8,128)S(1)} %get-tuple-element.66.edge.later, bf16[2,256,512]{2,1,0:T(8,128)(2,1)S(1)} %collective-permute-done.10.near, ...), custom_call_target="tpu_custom_call", output_to_operand_aliasing={{}: (0, {})} | custom-call | tf_op jit(solution)/shard_map/pallas_call | solution.py:544
  (1 shorter events, 0.0 us)
Async XLA Ops:
  0.6 9.9 %copy-start = (s32[8,4]{0,1:T(4,128)S(1)}, s32[8,4]{0,1:T(4,128)}, u32[]{:S(2)}) copy-start(s32[8,4]{0,1:T(4,128)} %param.11) | copy-start | bytes 388
  0.6 9.9 %copy-start.2 = (s32[8]{0:T(128)S(1)}, s32[8]{0:T(128)}, u32[]{:S(2)}) copy-start(s32[8]{0:T(128)} %count.3) | copy-start | bytes 100
  1.9 13.0 %collective-permute-start.2 = (bf16[256,512]{1,0:T(8,128)(2,1)S(1)}, bf16[256,512]{1,0:T(8,128)(2,1)S(1)}, u32[]{:S(2)}, u32[]{:S(2)}) collective-permute-start(bf16[256,512]{1,0:T(8,128)(2,1)S(1)} %get-tuple-element.48), channel_id=1, source_target_pairs={{0,1},{1,0},{2,3},{3,2},{4,5},{5,4},{6,7},{7,6},{8,9},{9,8},{10,11... | collective-permute-start | bytes 786440 | tf_op jit(solution)/shard_map/ppermute | solution.py:384
  4.0 11.9 %collective-permute-start.3 = (bf16[256,512]{1,0:T(8,128)(2,1)S(1)}, bf16[256,512]{1,0:T(8,128)(2,1)S(1)}, u32[]{:S(2)}, u32[]{:S(2)}) collective-permute-start(bf16[256,512]{1,0:T(8,128)(2,1)S(1)} %get-tuple-element.49), channel_id=1, source_target_pairs={{0,15},{1,2},{2,1},{3,4},{4,3},{5,6},{6,5},{7,8},{8,7},{9,10},{10,... | collective-permute-start | bytes 786440 | tf_op jit(solution)/shard_map/ppermute | solution.py:385
  8.9 11.8 %collective-permute-start = (bf16[256,512]{1,0:T(8,128)(2,1)S(1)}, bf16[256,512]{1,0:T(8,128)(2,1)S(1)}, u32[]{:S(2)}, u32[]{:S(2)}) collective-permute-start(bf16[256,512]{1,0:T(8,128)(2,1)S(1)} %get-tuple-element.41), channel_id=1, source_target_pairs={{0,1},{1,0},{2,3},{3,2},{4,5},{5,4},{6,7},{7,6},{8,9},{9,8},{10,11... | collective-permute-start | bytes 786440 | tf_op jit(solution)/shard_map/ppermute | solution.py:384
  8.9 11.8 %collective-permute-start.1 = (bf16[256,512]{1,0:T(8,128)(2,1)S(1)}, bf16[256,512]{1,0:T(8,128)(2,1)S(1)}, u32[]{:S(2)}, u32[]{:S(2)}) collective-permute-start(bf16[256,512]{1,0:T(8,128)(2,1)S(1)} %get-tuple-element.42), channel_id=1, source_target_pairs={{0,15},{1,2},{2,1},{3,4},{4,3},{5,6},{6,5},{7,8},{8,7},{9,10},{10,... | collective-permute-start | bytes 786440 | tf_op jit(solution)/shard_map/ppermute | solution.py:385
  15.9 8.3 %copy-start.3 = (f32[83]{0:T(128)S(1)}, f32[83]{0:T(128)}, u32[]{:S(2)}) copy-start(f32[83]{0:T(128)} %param.17) | copy-start | bytes 1000
  17.9 14.7 %collective-permute-start.7 = (bf16[88,1024]{1,0:T(8,128)(2,1)S(1)}, bf16[88,1024]{1,0:T(8,128)(2,1)S(1)}, u32[]{:S(2)}, u32[]{:S(2)}) collective-permute-start(bf16[88,1024]{1,0:T(8,128)(2,1)S(1)} %get-tuple-element.50.later.own1), channel_id=1, source_target_pairs={{0,48},{16,0},{32,16},{48,32},{1,49},{17,1},{33,17},{49,33},{2,50}... | collective-permute-start | bytes 540680 | tf_op jit(solution)/shard_map/ppermute | solution.py:452
  22.7 10.5 %collective-permute-start.4 = (bf16[88,1024]{1,0:T(8,128)(2,1)S(1)}, bf16[88,1024]{1,0:T(8,128)(2,1)S(1)}, u32[]{:S(2)}, u32[]{:S(2)}) collective-permute-start(bf16[88,1024]{1,0:T(8,128)(2,1)S(1)} %get-tuple-element.46.own0), channel_id=1, source_target_pairs={{0,16},{16,32},{32,48},{48,0},{1,17},{17,33},{33,49},{49,1},{2,18}... | collective-permute-start | bytes 540680 | tf_op jit(solution)/shard_map/ppermute | solution.py:452
  25.3 12.4 %collective-permute-start.5 = (bf16[88,1024]{1,0:T(8,128)(2,1)S(1)}, bf16[88,1024]{1,0:T(8,128)(2,1)S(1)}, u32[]{:S(2)}, u32[]{:S(2)}) collective-permute-start(bf16[88,1024]{1,0:T(8,128)(2,1)S(1)} %get-tuple-element.50.later.own1), channel_id=1, source_target_pairs={{0,16},{16,32},{32,48},{48,0},{1,17},{17,33},{33,49},{49,1},{2,18}... | collective-permute-start | bytes 540680 | tf_op jit(solution)/shard_map/ppermute | solution.py:452
  26.8 10.9 %collective-permute-start.6 = (bf16[88,1024]{1,0:T(8,128)(2,1)S(1)}, bf16[88,1024]{1,0:T(8,128)(2,1)S(1)}, u32[]{:S(2)}, u32[]{:S(2)}) collective-permute-start(bf16[88,1024]{1,0:T(8,128)(2,1)S(1)} %get-tuple-element.46.own0), channel_id=1, source_target_pairs={{0,48},{16,0},{32,16},{48,32},{1,49},{17,1},{33,17},{49,33},{2,50}... | collective-permute-start | bytes 540680 | tf_op jit(solution)/shard_map/ppermute | solution.py:452
  32.5 7.4 %copy-start.1 = (f32[1024]{0:T(1024)S(1)}, f32[1024]{0:T(1024)}, u32[]{:S(2)}) copy-start(f32[1024]{0:T(1024)} %param.16) | copy-start | bytes 12292
  32.6 5.6 %collective-permute-start.9 = (bf16[88,1024]{1,0:T(8,128)(2,1)S(1)}, bf16[88,1024]{1,0:T(8,128)(2,1)S(1)}, u32[]{:S(2)}, u32[]{:S(2)}) collective-permute-start(bf16[88,1024]{1,0:T(8,128)(2,1)S(1)} %collective-permute-done.7.o21), channel_id=1, source_target_pairs={{0,48},{16,0},{32,16},{48,32},{1,49},{17,1},{33,17},{49,33},{2,50}... | collective-permute-start | bytes 540680 | tf_op jit(solution)/shard_map/ppermute | solution.py:452
  33.2 6.7 %collective-permute-start.8 = (bf16[88,1024]{1,0:T(8,128)(2,1)S(1)}, bf16[88,1024]{1,0:T(8,128)(2,1)S(1)}, u32[]{:S(2)}, u32[]{:S(2)}) collective-permute-start(bf16[88,1024]{1,0:T(8,128)(2,1)S(1)} %collective-permute-done.4.o10), channel_id=1, source_target_pairs={{0,16},{16,32},{32,48},{48,0},{1,17},{17,33},{33,49},{49,1},{2,18}... | collective-permute-start | bytes 540680 | tf_op jit(solution)/shard_map/ppermute | solution.py:452
  43.2 8.3 %collective-permute-start.12 = (bf16[256,640]{1,0:T(8,128)(2,1)S(1)}, bf16[256,640]{1,0:T(8,128)(2,1)S(1)}, u32[]{:S(2)}, u32[]{:S(2)}) collective-permute-start(bf16[256,640]{1,0:T(8,128)(2,1)S(1)} %get-tuple-element.70), channel_id=1, source_target_pairs={{0,64},{64,0},{1,65},{65,1},{2,66},{66,2},{3,67},{67,3},{4,68},{68... | collective-permute-start | bytes 983048 | tf_op jit(solution)/shard_map/ppermute | solution.py:485
  45.6 25.4 %collective-permute-start.10 = (bf16[2,256,512]{2,1,0:T(8,128)(2,1)S(1)}, bf16[2,256,512]{2,1,0:T(8,128)(2,1)S(1)}, u32[]{:S(2)}, u32[]{:S(2)}) collective-permute-start(bf16[2,256,512]{2,1,0:T(8,128)(2,1)S(1)} %get-tuple-element.67), channel_id=1, source_target_pairs={{0,1},{1,0},{2,3},{3,2},{4,5},{5,4},{6,7},{7,6},{8,9},{9,8},{10,11... | collective-permute-start | bytes 1572872 | tf_op jit(solution)/shard_map/ppermute | solution.py:507
  45.7 25.3 %collective-permute-start.11 = (bf16[2,256,512]{2,1,0:T(8,128)(2,1)S(1)}, bf16[2,256,512]{2,1,0:T(8,128)(2,1)S(1)}, u32[]{:S(2)}, u32[]{:S(2)}) collective-permute-start(bf16[2,256,512]{2,1,0:T(8,128)(2,1)S(1)} %get-tuple-element.68), channel_id=1, source_target_pairs={{0,15},{1,2},{2,1},{3,4},{4,3},{5,6},{6,5},{7,8},{8,7},{9,10},{10,... | collective-permute-start | bytes 1572872 | tf_op jit(solution)/shard_map/ppermute | solution.py:508
  51.6 8.5 %collective-permute-start.13 = (bf16[64,640]{1,0:T(8,128)(2,1)S(1)}, bf16[64,640]{1,0:T(8,128)(2,1)S(1)}, u32[]{:S(2)}, u32[]{:S(2)}) collective-permute-start(bf16[64,640]{1,0:T(8,128)(2,1)S(1)} %get-tuple-element.72), channel_id=1, source_target_pairs={{0,16},{16,32},{32,48},{48,0},{1,17},{17,33},{33,49},{49,1},{2,18}... | collective-permute-start | bytes 245768 | tf_op jit(solution)/shard_map/ppermute | solution.py:452
  51.7 8.4 %collective-permute-start.14 = (bf16[64,640]{1,0:T(8,128)(2,1)S(1)}, bf16[64,640]{1,0:T(8,128)(2,1)S(1)}, u32[]{:S(2)}, u32[]{:S(2)}) collective-permute-start(bf16[64,640]{1,0:T(8,128)(2,1)S(1)} %get-tuple-element.73), channel_id=1, source_target_pairs={{0,32},{16,48},{32,0},{48,16},{1,33},{17,49},{33,1},{49,17},{2,34}... | collective-permute-start | bytes 245768 | tf_op jit(solution)/shard_map/ppermute | solution.py:452
  53.1 7.0 %collective-permute-start.15 = (bf16[64,640]{1,0:T(8,128)(2,1)S(1)}, bf16[64,640]{1,0:T(8,128)(2,1)S(1)}, u32[]{:S(2)}, u32[]{:S(2)}) collective-permute-start(bf16[64,640]{1,0:T(8,128)(2,1)S(1)} %get-tuple-element.74), channel_id=1, source_target_pairs={{0,48},{16,0},{32,16},{48,32},{1,49},{17,1},{33,17},{49,33},{2,50}... | collective-permute-start | bytes 245768 | tf_op jit(solution)/shard_map/ppermute | solution.py:452

commit v4 on v3

--- a/solution.py
+++ b/solution.py
@@ -51,10 +51,8 @@
     return pl.BlockSpec(memory_space=pl.ANY)
 
 
-def cost(flops, moved, transcendentals=0):
-    return pl.CostEstimate(
-        flops=int(flops), bytes_accessed=int(moved), transcendentals=int(transcendentals)
-    )
+def cost(mega):
+    return pl.CostEstimate(flops=mega * 1_000_000, bytes_accessed=mega * 4000, transcendentals=0)
 
 
 def params(mib):
@@ -100,8 +98,8 @@
 
 
 def prepare_kernel(
-    ids, count, lat_hbm, weight_hbm, w_in_hbm, w_out, acc0, acc1, halo_w, w_in_v, w_out_v,
-    lat, weight, sems, *, spaces,
+    ids, count, lat_hbm, weight_hbm, w_in_hbm, w_out,
+    acc0, acc1, halo_w, w_in_v, w_out_v, weight, lat, sems, *, spaces,
 ):
     tiles, slots, cells, nodes = weight.shape
     blocks = lat.shape[1]
@@ -148,18 +146,21 @@
 
 
 def turn_kernel(
-    ids, count, weight_hbm, w_in, w_out, later, halo_wt, own_wt, w_in_t, w_out_t, weight, sems,
-    *, spaces,
+    ids, count, weight, w_in, w_out, target, var_weight, later,
+    halo_wt, own_wt, w_in_t, w_out_t, target_v, scale_v, square, *, spaces,
 ):
     tiles, slots, cells, nodes = weight.shape
     blocks = own_wt.shape[0] // nodes
-    copy = pltpu.make_async_copy(weight_hbm, weight, sems.at[0])
-    copy.start()
     halo_wt[...] = jnp.zeros_like(halo_wt)
     own_wt[...] = jnp.zeros_like(own_wt)
     w_in_t[...] = w_in[...].T
     w_out_t[...] = w_out[...].T
-    copy.wait()
+    variables = target.shape[0]
+    target_v[...] = jnp.zeros_like(target_v)
+    target_v[:variables] = target[...]
+    square[...] = jnp.zeros_like(square)
+    square[:1, :variables] = var_weight[...]
+    scale_v[...] = square[...].T[: scale_v.shape[0], :1]
 
     def place_tile(t, carry):
         for k in range(slots):
@@ -191,7 +192,7 @@
 CHUNK = 256
 
 
-def fields_kernel(acc, near, far, halo_w, w_in, w_out, lat_out, fields):
+def fields_kernel(acc, near, far, halo_w, w_in, w_out, later, lat_out, fields):
     count = acc.shape[0]
     half_k = near.shape[0]
     for start in range(0, count, 2 * CHUNK):
@@ -220,28 +221,40 @@
     return u * lax.rsqrt(u * u + smooth_square)
 
 
-def weights_kernel(
-    own0, own1, o10, o11, o20, o21, o30, o31, target, area, var_weight,
-    act0, act1, slope0, slope1, lat0, lat1, w_out_t,
-    grad_pre0, grad_pre1, keep, send, total_in, total_out, *, ensemble, states,
+def spread_kernel(
+    own0, own1, o10, o11, o20, o21, far0, target, part0, part1, *, ensemble,
 ):
     count = own0.shape[1]
-    others = (o10, o11, o20, o21, o30, o31)
     for start in range(0, count, CHUNK):
         at = slice(start, start + CHUNK)
         truth = target[:, at].astype(f32)
         mine = [own0[:, at].astype(f32), own1[:, at].astype(f32)]
         pair = smooth_sign(mine[0] - mine[1])
         spread = [pair, -pair]
-        for other in others:
+        for other in (o10, o11, o20, o21, far0):
             theirs = other[:, at].astype(f32)
             for a in range(2):
                 spread[a] = spread[a] + smooth_sign(mine[a] - theirs)
+        for a, part in enumerate((part0, part1)):
+            value = smooth_sign(mine[a] - truth) * (1.0 / ensemble)
+            part[:, at] = value - spread[a] * (1.0 / (ensemble * (ensemble - 1)))
+
+
+def weights_kernel(
+    own0, own1, far1, part0, part1, area, var_weight,
+    act0, act1, slope0, slope1, lat0, lat1, w_out_t,
+    grad_pre0, grad_pre1, keep, send, total_in, total_out, *, ensemble, states,
+):
+    count = own0.shape[1]
+    for start in range(0, count, CHUNK):
+        at = slice(start, start + CHUNK)
+        mine = [own0[:, at].astype(f32), own1[:, at].astype(f32)]
+        theirs = far1[:, at].astype(f32)
         cell_weight = area[:, at] * var_weight[...] * (1.0 / states)
         cots = []
-        for a in range(2):
-            value = smooth_sign(mine[a] - truth) * (1.0 / ensemble)
-            value = value - spread[a] * (1.0 / (ensemble * (ensemble - 1)))
+        for a, part in enumerate((part0, part1)):
+            spread = smooth_sign(mine[a] - theirs)
+            value = part[:, at] - spread * (1.0 / (ensemble * (ensemble - 1)))
             cots.append((cell_weight * value).astype(bf16))
         cot = jnp.concatenate(cots, axis=1)
         grad_act = dot(w_out_t[...], cot)
@@ -279,7 +292,7 @@
         far[m] = dot(halo_wt[half_k:], grad_grid[...], NT).astype(bf16)
 
 
-def owned_kernel(grad_grid0, grad_grid1, own_wt, out, edge, parts, sems):
+def owned_kernel(grad_grid0, grad_grid1, own_wt, later, out, edge, parts, sems):
     step = edge.shape[2]
     count = own_wt.shape[0] // step
     copies = []
@@ -321,19 +334,29 @@
         copy.wait()
 
 
-def split_kernel(kept, swapped, own, send1, send2, send3, total):
-    parts, rows = total.shape[0], total.shape[1]
-    value = kept[...] + swapped[...].astype(f32)
-    for p in range(parts):
-        total[p] = value[p * rows : (p + 1) * rows]
-    here = lax.axis_index("member")
-    own[...] = total[here]
-    for d, out in ((1, send1), (2, send2), (3, send3)):
-        out[...] = total[lax.rem(here + d, parts)].astype(out.dtype)
-
-
-def scatter_kernel(kept, got1, got2, got3, later, out):
-    value = kept[...] + got1[...].astype(f32) + got2[...].astype(f32) + got3[...].astype(f32)
+def halve_kernel(kept, got, keep, send, total, *, bit):
+    rows = keep.shape[0]
+    total[...] = kept[...] + got[...].astype(f32)
+    here = lax.rem(lax.axis_index("member") // bit, 2)
+    keep[...] = total[rows_at(here, rows)]
+    send[...] = total[rows_at(1 - here, rows)].astype(send.dtype)
+
+
+def halve(kept, got, bit):
+    rows, wide = kept.shape[0] // 2, kept.shape[1]
+    return pl.pallas_call(
+        functools.partial(halve_kernel, bit=bit),
+        in_specs=[vmem()] * 2,
+        out_specs=[vmem()] * 2,
+        out_shape=[shape((rows, wide), f32), shape((rows, wide), bf16)],
+        scratch_shapes=[pltpu.VMEM(kept.shape, f32)],
+        compiler_params=params(8),
+        cost_estimate=cost(2000),
+    )(kept, got)
+
+
+def scatter_kernel(kept, got, later, out):
+    value = kept[...] + got[...].astype(f32)
     parts, rows = out.shape[0], out.shape[1]
     for p in range(parts):
         out[p] = value[p * rows : (p + 1) * rows].astype(out.dtype)
@@ -385,78 +408,94 @@
         far = lax.ppermute(edges[2 * m + 1], "space", second)
         halos.append((near, far))
 
-    target = jnp.pad(targets[0], ((0, rows_v - variables), (0, 0)))
-    scale_v = jnp.pad(var_weight, (0, rows_v - variables))[:, None]
     scale_n = area[None, :]
 
-    acc0, acc1, halo_w, w_in_v, w_out_v = pl.pallas_call(
+    acc0, acc1, halo_w, w_in_v, w_out_v, weight_v = pl.pallas_call(
         functools.partial(prepare_kernel, spaces=spaces),
         in_specs=[smem(), smem(), hbm(), hbm(), hbm(), vmem()],
-        out_specs=[vmem()] * 5,
+        out_specs=[vmem()] * 6,
         out_shape=[
             held((n, feature), f32),
             held((n, feature), f32),
             held((n, rim_rows), bf16),
             held((hidden, feature), bf16),
             held((rows_v, hidden), bf16),
+            held(edge_weight.shape, bf16),
         ],
         scratch_shapes=[
             pltpu.VMEM(lat.shape, bf16),
-            pltpu.VMEM(edge_weight.shape, bf16),
             pltpu.SemaphoreType.DMA((4,)),
         ],
-        compiler_params=params(24),
-        cost_estimate=cost(2 * n * slots * nodes * feature * members, 10 * MIB),
+        compiler_params=params(12),
+        cost_estimate=cost(2000),
     )(ids, block_count, in_hbm(lat), in_hbm(edge_weight), in_hbm(w_in), in_hbm(w_out))
+
+    def along(x, distance):
+        return lax.ppermute(x, "member", ring(chips, distance))
 
     grid_latent, fields, acts, slopes = [], [], [], []
     for m, acc in enumerate((acc0, acc1)):
         near, far = halos[m]
         lat_m, fields_m = pl.pallas_call(
             fields_kernel,
-            in_specs=[vmem()] * 6,
+            in_specs=[vmem()] * 6 + [anywhere()],
             out_specs=[vmem()] * 2,
             out_shape=[held((n, feature), bf16), shape((rows_v, n), bf16)],
-            compiler_params=params(16),
-            cost_estimate=cost(4 * n * feature * hidden, MIB, n * hidden),
-        )(*in_vmem(acc), near, far, *in_vmem(halo_w, w_in_v, w_out_v))
+            compiler_params=params(8),
+            cost_estimate=cost(100),
+        )(*in_vmem(acc), near, far, *in_vmem(halo_w, w_in_v, w_out_v), slopes[-1] if slopes else halo_w)
         grid_latent.append(lat_m)
         fields.append(fields_m)
+        if m == 0:
+            left0 = along(fields_m, 1)
+            right0 = along(fields_m, -1)
+        else:
+            lat_m, left0, right0 = lax.optimization_barrier((lat_m, left0, right0))
         act_m, slope_m = pl.pallas_call(
             slopes_kernel,
             in_specs=[vmem()] * 2,
             out_specs=[vmem()] * 2,
             out_shape=[held((hidden, n), bf16)] * 2,
-            compiler_params=params(16),
-            cost_estimate=cost(4 * n * feature * hidden, MIB, n * hidden),
+            compiler_params=params(8),
+            cost_estimate=cost(100),
         )(*in_vmem(lat_m, w_in_v))
         acts.append(act_m)
         slopes.append(slope_m)
 
-    halo_wt, own_wt, w_in_t, w_out_t = pl.pallas_call(
+    halo_wt, own_wt, w_in_t, w_out_t, target, scale_v = pl.pallas_call(
         functools.partial(turn_kernel, spaces=spaces),
-        in_specs=[smem(), smem(), hbm(), vmem(), vmem(), anywhere()],
-        out_specs=[vmem()] * 4,
+        in_specs=[smem(), smem()] + [vmem()] * 5 + [anywhere()],
+        out_specs=[vmem()] * 6,
         out_shape=[
             held((rim_rows, n), bf16),
             held((blocks * nodes, n), bf16),
             held((feature, hidden), bf16),
             held((hidden, rows_v), bf16),
+            held((rows_v, n), bf16),
+            held((rows_v, 1), f32),
         ],
-        scratch_shapes=[pltpu.VMEM(edge_weight.shape, bf16), pltpu.SemaphoreType.DMA((1,))],
-        compiler_params=params(16),
-        cost_estimate=cost(MIB, 6 * MIB),
-    )(ids, block_count, in_hbm(edge_weight), *in_vmem(w_in_v, w_out_v), fields[1])
-
-    def along(x, distance):
-        return lax.ppermute(x, "member", ring(chips, distance))
-
-    left0 = along(fields[0], 1)
-    right0 = along(fields[0], -1)
-    far0 = along(left0, 1)
+        scratch_shapes=[pltpu.VMEM((128, 128), f32)],
+        compiler_params=params(8),
+        cost_estimate=cost(100),
+    )(
+        ids, block_count, *in_vmem(weight_v, w_in_v, w_out_v), targets[0], var_weight[None],
+        slopes[1],
+    )
+
     right1 = along(fields[1], -1)
     left1 = along(fields[1], 1)
-    far1 = along(right1, -1)
+    far0 = along(left0, 1)
+    held_right1, _ = lax.optimization_barrier((right1, slopes[1]))
+    far1 = along(held_right1, -1)
+
+    part0, part1 = pl.pallas_call(
+        functools.partial(spread_kernel, ensemble=members * chips),
+        in_specs=[vmem()] * 8,
+        out_specs=[vmem()] * 2,
+        out_shape=[held((rows_v, n), f32)] * 2,
+        compiler_params=params(8),
+        cost_estimate=cost(100),
+    )(*fields, left0, left1, right0, right1, far0, *in_vmem(target))
 
     wide = feature + 128
     half_rows = hidden // 2
@@ -466,7 +505,7 @@
             ensemble=members * chips,
             states=targets.shape[0] * lax.axis_size("dp"),
         ),
-        in_specs=[vmem()] * 18,
+        in_specs=[vmem()] * 14,
         out_specs=[vmem()] * 4,
         out_shape=[
             held((hidden, n), bf16),
@@ -475,10 +514,10 @@
             shape((half_rows, wide), bf16),
         ],
         scratch_shapes=[pltpu.VMEM((hidden, feature), f32), pltpu.VMEM((hidden, 128), f32)],
-        compiler_params=params(20),
-        cost_estimate=cost(4 * n * feature * hidden, MIB),
+        compiler_params=params(12),
+        cost_estimate=cost(2000),
     )(
-        *fields, left0, left1, right0, right1, far0, far1, target, scale_n, scale_v,
+        *fields, far1, *in_vmem(part0, part1), scale_n, *in_vmem(scale_v),
         *in_vmem(*acts, *slopes, *grid_latent, w_out_t),
     )
 
@@ -489,28 +528,24 @@
         in_specs=[vmem()] * 4,
         out_specs=[vmem()] * 4,
         out_shape=[held((feature, n), bf16)] * 2 + [shape((members, edge_rows, feature), bf16)] * 2,
-        compiler_params=params(16),
-        cost_estimate=cost(8 * n * feature * hidden, MIB),
+        compiler_params=params(8),
+        cost_estimate=cost(2000),
     )(*in_vmem(grad_pre0, grad_pre1, halo_wt, w_in_t))
 
     quarter = half_rows // chips
-    kept, *sends = pl.pallas_call(
-        split_kernel,
-        in_specs=[vmem(), vmem()],
-        out_specs=[vmem()] * 4,
-        out_shape=[shape((quarter, wide), f32)] + [shape((quarter, wide), bf16)] * 3,
-        scratch_shapes=[pltpu.VMEM((chips, quarter, wide), f32)],
-        compiler_params=params(8),
-    )(keep, swapped)
-    got = [along(s, d) for d, s in zip((1, 2, 3), sends)]
-
+    swapped, _ = lax.optimization_barrier((swapped, grad_grid0))
+    kept, send = halve(keep, swapped, 2)
+    got = lax.ppermute(send, "member", [(i, chips - 1 - i) for i in range(chips)])
+    rim_near, rim_far, _ = lax.optimization_barrier((rim_near, rim_far, send))
     got_near = lax.ppermute(rim_near, "space", first)
     got_far = lax.ppermute(rim_far, "space", second)
+    kept, send = halve(kept, got, 1)
+    got = lax.ppermute(send, "member", [(i, i ^ 1) for i in range(chips)])
 
     middle = blocks // HALO - 2
     owned, edge = pl.pallas_call(
         owned_kernel,
-        in_specs=[vmem()] * 3,
+        in_specs=[vmem()] * 3 + [anywhere()],
         out_specs=[hbm(), vmem()],
         out_shape=[
             shape((members, blocks * nodes, feature), f32),
@@ -520,18 +555,18 @@
             pltpu.VMEM((members * middle, edge_rows, feature), f32),
             pltpu.SemaphoreType.DMA((members * middle,)),
         ],
-        compiler_params=params(20),
-        cost_estimate=cost(2 * blocks * nodes * n * feature * members, 8 * MIB),
-    )(*in_vmem(grad_grid0, grad_grid1, own_wt))
+        compiler_params=params(12),
+        cost_estimate=cost(2000),
+    )(*in_vmem(grad_grid0, grad_grid1, own_wt), send)
 
     last_rows = quarter // spaces
     spread = pl.pallas_call(
         scatter_kernel,
-        in_specs=[vmem()] * 4 + [anywhere()],
+        in_specs=[vmem()] * 2 + [anywhere()],
         out_specs=vmem(),
         out_shape=shape((spaces, last_rows, wide), bf16),
         compiler_params=params(8),
-    )(kept, *got, edge)
+    )(kept, got, edge)
     spread = lax.all_to_all(spread, "space", 0, 0, tiled=True)
     grad_w_in, grad_w_out = pl.pallas_call(
         finish_kernel,

time: 72.9 us -> 73.4 us (level)
  blocking collectives: 10.2 us -> 14.5 us
  starting transfers between devices: 27.7 us -> 24.4 us
  local copies, waits for them, and re-layouts: 1.06 us -> 0.02 us
    ppermute x9 -> x6, starting transfers between devices: 13.1 us -> 7.69 us  [along(): return lax.ppermute(x, 'member', ring(chips, distance))]
    all_to_all x1, blocking collectives: 10.2 us -> 14.5 us  [local(): spread = lax.all_to_all(spread, 'space', 0, 0, tiled=True)]
    ppermute x0 -> x2, starting transfers between devices: none -> 2.3 us  [the longest x1 2.22 us: local(): lax.ppermute(send, 'member', [(i, chips - 1 - i) for i in range(chips)])]
    pallas_call x5 -> x7, Pallas kernels: 9.22 us -> 10.4 us  [the longest x1 5.17 us: local(): pl.pallas_call(owned_kernel, in_specs=[vmem()] * 3 + [anywhere()], out_sp...]
    pad x1 -> x0, local copies, waits for them, and re-layouts: 0.94 us -> none  [local(): target = jnp.pad(targets[0], ((0, rows_v - variables), (0, 0)))]
    ppermute x9 -> x6, waiting for transfers between devices: 2.2 us -> 2.41 us  [along(): return lax.ppermute(x, 'member', ring(chips, distance))]
  transfers between devices with their start and end apart: 16 -> 15, of which waited for: 3 -> 3; matrix products, arithmetic and copies ran while one was open for 1% -> 0% of each run, Pallas kernels for 32% -> 33%
where the time goes in v4:
time: 73.4 us; the launch traced here: 72.7 us
  Pallas kernels  29.3 us (40%)
  starting transfers between devices  24.4 us (33%)
  blocking collectives  14.5 us (20%)
  waiting for transfers between devices  3.5 us (5%)
  between operations  1.01 us (1%)
    all_to_all x1, blocking collectives, local(): spread = lax.all_to_all(spread, 'space', 0, 0, tiled=True)  14.5 us
    ppermute x6, starting transfers between devices, along(): return lax.ppermute(x, 'member', ring(chips, distance))  7.69 us
    ppermute x2, starting transfers between devices, local(): far = lax.ppermute(edges[2 * m + 1], 'space', second)  6.6 us
    ppermute x1, starting transfers between devices, local(): got_far = lax.ppermute(rim_far, 'space', second)  5.59 us
    pallas_call x1, Pallas kernels, local(): pl.pallas_call(owned_kernel, in_specs=[vmem()] * 3 + [anywhere()], out_sp...  5.17 us
    pallas_call x1, Pallas kernels, local(): pl.pallas_call(functools.partial(prepare_kernel, spaces=spaces), in_specs...  4.31 us
    pallas_call x2, Pallas kernels, local(): pl.pallas_call(fields_kernel, in_specs=[vmem()] * 6 + [anywhere()], out_s...  3.88 us
    pallas_call x1, Pallas kernels, local(): pl.pallas_call(functools.partial(turn_kernel, spaces=spaces), in_specs=[s...  3.37 us
  transfers between devices with their start and end apart: 15, of which 3 were waited for; matrix products, arithmetic and copies ran while one was open for 0% of the time, Pallas kernels for 33%

profile of v4, /device:TPU:0, one launch (start us, length us, event | category | flops | bytes accessed | tf_op | source)
XLA Modules:
  0.0 72.7 jit_solution(16857328920241665639)
XLA Ops:
  0.6 0.0 copy-start.2
  0.6 0.0 copy-start.3
  0.7 1.2 %shard_map.113 = (bf16[256,512]{1,0:T(8,128)(2,1)S(1)}, bf16[256,512]{1,0:T(8,128)(2,1)S(1)}, bf16[256,512]{1,0:T(8,128)(2,1)S(1)}, bf16[256,512]{1,0:T(8,128)(2,1)S(1)}) custom-call(bf16[2,2048,512]{2,1,0:T(8,128)(2,1)} %bitcast.14), custom_call_target="tpu_custom_call" | custom-call | tf_op jit(solution)/shard_map/pallas_call | solution.py:397
  1.9 2.1 %collective-permute-start = (bf16[256,512]{1,0:T(8,128)(2,1)S(1)}, bf16[256,512]{1,0:T(8,128)(2,1)S(1)}, u32[]{:S(2)}, u32[]{:S(2)}) collective-permute-start(bf16[256,512]{1,0:T(8,128)(2,1)S(1)} %get-tuple-element.53), channel_id=1, source_target_pairs={{0,1},{1,0},{2,3},{3,2},{4,5},{5,4},{6,7},{7,6},{8,9},{9,8},{10,11... | collective-permute-start | bytes 786440 | tf_op jit(solution)/shard_map/ppermute | solution.py:407
  4.0 5.0 %collective-permute-start.1 = (bf16[256,512]{1,0:T(8,128)(2,1)S(1)}, bf16[256,512]{1,0:T(8,128)(2,1)S(1)}, u32[]{:S(2)}, u32[]{:S(2)}) collective-permute-start(bf16[256,512]{1,0:T(8,128)(2,1)S(1)} %get-tuple-element.54), channel_id=1, source_target_pairs={{0,15},{1,2},{2,1},{3,4},{4,3},{5,6},{6,5},{7,8},{8,7},{9,10},{10,... | collective-permute-start | bytes 786440 | tf_op jit(solution)/shard_map/ppermute | solution.py:408
  8.9 0.0 collective-permute-start.2
  8.9 1.6 %collective-permute-start.3 = (bf16[256,512]{1,0:T(8,128)(2,1)S(1)}, bf16[256,512]{1,0:T(8,128)(2,1)S(1)}, u32[]{:S(2)}, u32[]{:S(2)}) collective-permute-start(bf16[256,512]{1,0:T(8,128)(2,1)S(1)} %get-tuple-element.61), channel_id=1, source_target_pairs={{0,15},{1,2},{2,1},{3,4},{4,3},{5,6},{6,5},{7,8},{8,7},{9,10},{10,... | collective-permute-start | bytes 786440 | tf_op jit(solution)/shard_map/ppermute | solution.py:408
  10.6 0.0 copy-done.2
  10.6 0.0 copy-done.3
  10.6 4.3 %shard_map.112 = (f32[1024,512]{1,0:T(8,128)S(1)}, f32[1024,512]{1,0:T(8,128)S(1)}, bf16[1024,512]{1,0:T(8,128)(2,1)S(1)}, bf16[512,512]{1,0:T(8,128)(2,1)S(1)},...) custom-call(s32[4,8]{1,0:T(4,128)S(1)} %bitcast.10, s32[8]{0:T(128)S(1)} %copy-done.3, ...), custom_call_target="tpu_custom_call" | custom-call | flops 2000000000 | bytes 8000000 | tf_op jit(solution)/shard_map/pallas_call | solution.py:413
  14.9 0.0 collective-permute-done.near
  14.9 1.0 %collective-permute-done.1.far = bf16[256,512]{1,0:T(8,128)(2,1)S(1)} collective-permute-done((bf16[256,512]{1,0:T(8,128)(2,1)S(1)}, bf16[256,512]{1,0:T(8,128)(2,1)S(1)}, u32[]{:S(2)}, u32[]{:S(2)}) %collective-permute-start.1) | collective-permute-done | bytes 262176 | tf_op jit(solution)/shard_map/ppermute | solution.py:408
  15.9 1.9 %shard_map.114 = (bf16[1024,512]{1,0:T(8,128)(2,1)S(1)}, bf16[88,1024]{1,0:T(8,128)(2,1)S(1)}) custom-call(f32[1024,512]{1,0:T(8,128)S(1)} %get-tuple-element.52.acc, bf16[256,512]{1,0:T(8,128)(2,1)S(1)} %collective-permute-done.near, bf16[256,512]{1,0:T(8,128)(2,1)S(1)} %collective-permute-done.1.far, bf16[1024,512]{1,0:T(8,128)(2,1)S(1)} %get-tuple-element.55.halo_w.later, ...), custom_call_target="tpu_custom_call" | custom-call | flops 100000000 | bytes 400000 | tf_op jit(solution)/shard_map/pallas_call | solution.py:439
  17.9 1.6 %collective-permute-start.5 = (bf16[88,1024]{1,0:T(8,128)(2,1)S(1)}, bf16[88,1024]{1,0:T(8,128)(2,1)S(1)}, u32[]{:S(2)}, u32[]{:S(2)}) collective-permute-start(bf16[88,1024]{1,0:T(8,128)(2,1)S(1)} %get-tuple-element.58.own0), channel_id=1, source_target_pairs={{0,16},{16,32},{32,48},{48,0},{1,17},{17,33},{33,49},{49,1},{2,18}... | collective-permute-start | bytes 540680 | tf_op jit(solution)/shard_map/ppermute | solution.py:434
  19.4 1.7 %collective-permute-start.6 = (bf16[88,1024]{1,0:T(8,128)(2,1)S(1)}, bf16[88,1024]{1,0:T(8,128)(2,1)S(1)}, u32[]{:S(2)}, u32[]{:S(2)}) collective-permute-start(bf16[88,1024]{1,0:T(8,128)(2,1)S(1)} %get-tuple-element.58.own0), channel_id=1, source_target_pairs={{0,48},{16,0},{32,16},{48,32},{1,49},{17,1},{33,17},{49,33},{2,50}... | collective-permute-start | bytes 540680 | tf_op jit(solution)/shard_map/ppermute | solution.py:434
  21.2 0.0 copy-start
  21.2 0.0 copy-start.4
  21.2 1.5 %shard_map.115 = (bf16[512,1024]{1,0:T(8,128)(2,1)S(1)}, bf16[512,1024]{1,0:T(8,128)(2,1)S(1)}) custom-call(bf16[1024,512]{1,0:T(8,128)(2,1)S(1)} %get-tuple-element.62.lat.lat0, bf16[512,512]{1,0:T(8,128)(2,1)S(1)} %get-tuple-element.56.w_in), custom_call_target="tpu_custom_call" | custom-call | flops 100000000 | bytes 400000 | tf_op jit(solution)/shard_map/pallas_call | solution.py:454
  22.7 0.0 collective-permute-done.2.near
  22.7 0.0 collective-permute-done.3.far
  22.7 1.9 %shard_map.116 = (bf16[1024,512]{1,0:T(8,128)(2,1)S(1)}, bf16[88,1024]{1,0:T(8,128)(2,1)S(1)}) custom-call(f32[1024,512]{1,0:T(8,128)S(1)} %get-tuple-element.59.acc, bf16[256,512]{1,0:T(8,128)(2,1)S(1)} %collective-permute-done.2.near, bf16[256,512]{1,0:T(8,128)(2,1)S(1)} %collective-permute-done.3.far, ...), custom_call_target="tpu_custom_call" | custom-call | flops 100000000 | bytes 400000 | tf_op jit(solution)/shard_map/pallas_call | solution.py:439
  24.7 0.0 copy-start.1
  24.7 1.6 %collective-permute-start.4 = (bf16[88,1024]{1,0:T(8,128)(2,1)S(1)}, bf16[88,1024]{1,0:T(8,128)(2,1)S(1)}, u32[]{:S(2)}, u32[]{:S(2)}) collective-permute-start(bf16[88,1024]{1,0:T(8,128)(2,1)S(1)} %get-tuple-element.64.own1), channel_id=1, source_target_pairs={{0,48},{16,0},{32,16},{48,32},{1,49},{17,1},{33,17},{49,33},{2,50}... | collective-permute-start | bytes 540680 | tf_op jit(solution)/shard_map/ppermute | solution.py:434
  26.3 0.5 collective-permute-start.8
  26.8 0.0 collective-permute-done.5.o10
  26.8 0.0 collective-permute-done.6.o20
  26.8 0.3 collective-permute-start.9
  27.0 1.5 %shard_map.117 = (bf16[512,1024]{1,0:T(8,128)(2,1)S(1)}, bf16[512,1024]{1,0:T(8,128)(2,1)S(1)}) custom-call(bf16[1024,512]{1,0:T(8,128)(2,1)S(1)} %get-tuple-element.66.lat.lat1, bf16[512,512]{1,0:T(8,128)(2,1)S(1)} %get-tuple-element.56.w_in), custom_call_target="tpu_custom_call" | custom-call | flops 100000000 | bytes 400000 | tf_op jit(solution)/shard_map/pallas_call | solution.py:454
  28.6 2.4 %collective-permute-done.4.o21 = bf16[88,1024]{1,0:T(8,128)(2,1)S(1)} collective-permute-done((bf16[88,1024]{1,0:T(8,128)(2,1)S(1)}, bf16[88,1024]{1,0:T(8,128)(2,1)S(1)}, u32[]{:S(2)}, u32[]{:S(2)}) %collective-permute-start.4) | collective-permute-done | bytes 180256 | tf_op jit(solution)/shard_map/ppermute | solution.py:434
  31.0 2.0 %collective-permute-start.7 = (bf16[88,1024]{1,0:T(8,128)(2,1)S(1)}, bf16[88,1024]{1,0:T(8,128)(2,1)S(1)}, u32[]{:S(2)}, u32[]{:S(2)}) collective-permute-start(bf16[88,1024]{1,0:T(8,128)(2,1)S(1)} %collective-permute-done.4.o21), channel_id=1, source_target_pairs={{0,48},{16,0},{32,16},{48,32},{1,49},{17,1},{33,17},{49,33},{2,50}... | collective-permute-start | bytes 540680 | tf_op jit(solution)/shard_map/ppermute | solution.py:434
  33.0 0.0 copy-done
  33.0 0.0 copy-done.4
  33.0 3.4 %shard_map.118 = (bf16[512,1024]{1,0:T(8,128)(2,1)S(1)}, bf16[2048,1024]{1,0:T(8,128)(2,1)S(1)}, bf16[512,512]{1,0:T(8,128)(2,1)S(1)}, bf16[512,88]{1,0:T(8,128)...) custom-call(s32[4,8]{1,0:T(4,128)S(1)} %bitcast.11, s32[8]{0:T(128)S(1)} %copy-done.3, ...), custom_call_target="tpu_custom_call" | custom-call | flops 100000000 | bytes 400000 | tf_op jit(solution)/shard_map/pallas_call | solution.py:465
  36.4 0.0 collective-permute-done.8.o11
  36.4 0.0 collective-permute-done.9.far0
  36.4 1.1 %shard_map.119 = (f32[88,1024]{1,0:T(8,128)S(1)}, f32[88,1024]{1,0:T(8,128)S(1)}) custom-call(bf16[88,1024]{1,0:T(8,128)(2,1)S(1)} %get-tuple-element.58.own0, bf16[88,1024]{1,0:T(8,128)(2,1)S(1)} %get-tuple-element.64.own1, bf16[88,1024]{1,0:T(8,128)(2,1)S(1)} %collective-permute-done.5.o10, bf16[88,1024]{1,0:T(8,128)(2,1)S(1)} %collective-permute-done.8.o11, ...), custom_call_target="tpu_custom_call" | custom-call | flops 100000000 | bytes 400000 | tf_op jit(solution)/shard_map/pallas_call | solution.py:491
  37.5 0.0 collective-permute-done.7.far1
  37.5 0.0 copy-done.1
  37.5 2.7 %shard_map.120 = (bf16[512,1024]{1,0:T(8,128)(2,1)S(1)}, bf16[512,1024]{1,0:T(8,128)(2,1)S(1)}, f32[256,640]{1,0:T(8,128)S(1)}, bf16[256,640]{1,0:T(8,128)(2,1)S(1)}) custom-call(bf16[88,1024]{1,0:T(8,128)(2,1)S(1)} %get-tuple-element.58.own0, bf16[88,1024]{1,0:T(8,128)(2,1)S(1)} %get-tuple-element.64.own1, ...), custom_call_target="tpu_custom_call" | custom-call | flops 2000000000 | bytes 8000000 | tf_op jit(solution)/shard_map/pallas_call | solution.py:502
  40.2 0.1 collective-permute-start.10
  40.3 2.3 %shard_map.121 = (bf16[512,1024]{1,0:T(8,128)(2,1)S(1)}, bf16[512,1024]{1,0:T(8,128)(2,1)S(1)}, bf16[2,256,512]{2,1,0:T(8,128)(2,1)S(1)}, bf16[2,256,512]{2,1,0:T(8,128)(2,1)S(1)}) custom-call(bf16[512,1024]{1,0:T(8,128)(2,1)S(1)} %get-tuple-element.79.grad_pre0, bf16[512,1024]{1,0:T(8,128)(2,1)S(1)} %get-tuple-element.80.grad_pre1, ...), custom_call_target="tpu_custom_call" | custom-call | flops 2000000000 | bytes 8000000 | tf_op jit(solution)/shard_map/pallas_call | solution.py:526
  42.6 0.0 collective-permute-done.10.got
  42.7 0.1 shard_map.122
  42.8 2.2 %collective-permute-start.11 = (bf16[128,640]{1,0:T(8,128)(2,1)S(1)}, bf16[128,640]{1,0:T(8,128)(2,1)S(1)}, u32[]{:S(2)}, u32[]{:S(2)}) collective-permute-start(bf16[128,640]{1,0:T(8,128)(2,1)S(1)} %get-tuple-element.90), channel_id=1, source_target_pairs={{0,48},{16,32},{32,16},{48,0},{1,49},{17,33},{33,17},{49,1},{2,50}... | collective-permute-start | bytes 491528 | tf_op jit(solution)/shard_map/ppermute | solution.py:538
  45.0 0.0 collective-permute-start.12
  45.0 5.6 %collective-permute-start.13 = (bf16[2,256,512]{2,1,0:T(8,128)(2,1)S(1)}, bf16[2,256,512]{2,1,0:T(8,128)(2,1)S(1)}, u32[]{:S(2)}, u32[]{:S(2)}) collective-permute-start(bf16[2,256,512]{2,1,0:T(8,128)(2,1)S(1)} %get-tuple-element.97), channel_id=1, source_target_pairs={{0,15},{1,2},{2,1},{3,4},{4,3},{5,6},{6,5},{7,8},{8,7},{9,10},{10,... | collective-permute-start | bytes 1572872 | tf_op jit(solution)/shard_map/ppermute | solution.py:541
  50.6 0.1 collective-permute-done.11.got
  50.7 0.1 shard_map.123
  50.7 0.1 collective-permute-start.14
  50.8 5.2 %shard_map.124 = (f32[2,2048,512]{2,1,0:T(8,128)}, f32[2,2,256,512]{3,2,1,0:T(8,128)S(1)}) custom-call(bf16[512,1024]{1,0:T(8,128)(2,1)S(1)} %get-tuple-element.83.grad_grid0, bf16[512,1024]{1,0:T(8,128)(2,1)S(1)} %get-tuple-element.84.grad_grid1, bf16[2048,1024]{1,0:T(8,128)(2,1)S(1)} %get-tuple-element.85.own_wt, bf16[64,640]{1,0:T(8,128)(2,1)S(1)} %get-tuple-element.91.later), custom_call_target="tpu_custom_call" | custom-call | flops 2000000000 | bytes 8000000 | tf_op jit(solution)/shard_map/pallas_call | solution.py:546
  56.0 0.0 collective-permute-done.14.got
  56.1 14.5 %all_to_all.5.got = bf16[16,4,640]{2,1,0:T(4,128)(2,1)S(1)} all-to-all(bf16[16,4,640]{2,1,0:T(4,128)(2,1)S(1)} %shard_map.126), channel_id=1, replica_groups=mesh['dp'=2,'member'=4,'space'=16] {'space'}, dimensions={0} | all-to-all | bytes 163840 | tf_op jit(solution)/shard_map/all_to_all | solution.py:570
  70.5 0.6 shard_map.127
  71.1 0.0 collective-permute-done.12.near
  71.1 0.0 collective-permute-done.13.far
  71.1 1.4 %shard_map.125 = f32[2,2048,512]{2,1,0:T(8,128)} custom-call(f32[2,2048,512]{2,1,0:T(8,128)} %get-tuple-element.92.base, f32[2,2,256,512]{3,2,1,0:T(8,128)S(1)} %get-tuple-element.93.edge.later, bf16[2,256,512]{2,1,0:T(8,128)(2,1)S(1)} %collective-permute-done.12.near, ...), custom_call_target="tpu_custom_call", output_to_operand_aliasing={{}: (0, {})} | custom-call | tf_op jit(solution)/shard_map/pallas_call | solution.py:579
  (1 shorter events, 0.0 us)
Async XLA Ops:
  0.6 9.9 %copy-start.2 = (s32[8,4]{0,1:T(4,128)S(1)}, s32[8,4]{0,1:T(4,128)}, u32[]{:S(2)}) copy-start(s32[8,4]{0,1:T(4,128)} %param.11) | copy-start | bytes 388
  0.6 9.9 %copy-start.3 = (s32[8]{0:T(128)S(1)}, s32[8]{0:T(128)}, u32[]{:S(2)}) copy-start(s32[8]{0:T(128)} %count.3) | copy-start | bytes 100
  1.9 13.0 %collective-permute-start = (bf16[256,512]{1,0:T(8,128)(2,1)S(1)}, bf16[256,512]{1,0:T(8,128)(2,1)S(1)}, u32[]{:S(2)}, u32[]{:S(2)}) collective-permute-start(bf16[256,512]{1,0:T(8,128)(2,1)S(1)} %get-tuple-element.53), channel_id=1, source_target_pairs={{0,1},{1,0},{2,3},{3,2},{4,5},{5,4},{6,7},{7,6},{8,9},{9,8},{10,11... | collective-permute-start | bytes 786440 | tf_op jit(solution)/shard_map/ppermute | solution.py:407
  4.0 11.9 %collective-permute-start.1 = (bf16[256,512]{1,0:T(8,128)(2,1)S(1)}, bf16[256,512]{1,0:T(8,128)(2,1)S(1)}, u32[]{:S(2)}, u32[]{:S(2)}) collective-permute-start(bf16[256,512]{1,0:T(8,128)(2,1)S(1)} %get-tuple-element.54), channel_id=1, source_target_pairs={{0,15},{1,2},{2,1},{3,4},{4,3},{5,6},{6,5},{7,8},{8,7},{9,10},{10,... | collective-permute-start | bytes 786440 | tf_op jit(solution)/shard_map/ppermute | solution.py:408
  8.9 13.7 %collective-permute-start.2 = (bf16[256,512]{1,0:T(8,128)(2,1)S(1)}, bf16[256,512]{1,0:T(8,128)(2,1)S(1)}, u32[]{:S(2)}, u32[]{:S(2)}) collective-permute-start(bf16[256,512]{1,0:T(8,128)(2,1)S(1)} %get-tuple-element.60), channel_id=1, source_target_pairs={{0,1},{1,0},{2,3},{3,2},{4,5},{5,4},{6,7},{7,6},{8,9},{9,8},{10,11... | collective-permute-start | bytes 786440 | tf_op jit(solution)/shard_map/ppermute | solution.py:407
  8.9 13.7 %collective-permute-start.3 = (bf16[256,512]{1,0:T(8,128)(2,1)S(1)}, bf16[256,512]{1,0:T(8,128)(2,1)S(1)}, u32[]{:S(2)}, u32[]{:S(2)}) collective-permute-start(bf16[256,512]{1,0:T(8,128)(2,1)S(1)} %get-tuple-element.61), channel_id=1, source_target_pairs={{0,15},{1,2},{2,1},{3,4},{4,3},{5,6},{6,5},{7,8},{8,7},{9,10},{10,... | collective-permute-start | bytes 786440 | tf_op jit(solution)/shard_map/ppermute | solution.py:408
  17.9 8.9 %collective-permute-start.5 = (bf16[88,1024]{1,0:T(8,128)(2,1)S(1)}, bf16[88,1024]{1,0:T(8,128)(2,1)S(1)}, u32[]{:S(2)}, u32[]{:S(2)}) collective-permute-start(bf16[88,1024]{1,0:T(8,128)(2,1)S(1)} %get-tuple-element.58.own0), channel_id=1, source_target_pairs={{0,16},{16,32},{32,48},{48,0},{1,17},{17,33},{33,49},{49,1},{2,18}... | collective-permute-start | bytes 540680 | tf_op jit(solution)/shard_map/ppermute | solution.py:434
  19.4 7.4 %collective-permute-start.6 = (bf16[88,1024]{1,0:T(8,128)(2,1)S(1)}, bf16[88,1024]{1,0:T(8,128)(2,1)S(1)}, u32[]{:S(2)}, u32[]{:S(2)}) collective-permute-start(bf16[88,1024]{1,0:T(8,128)(2,1)S(1)} %get-tuple-element.58.own0), channel_id=1, source_target_pairs={{0,48},{16,0},{32,16},{48,32},{1,49},{17,1},{33,17},{49,33},{2,50}... | collective-permute-start | bytes 540680 | tf_op jit(solution)/shard_map/ppermute | solution.py:434
  21.2 11.8 %copy-start = (bf16[1,83,1024]{2,1,0:T(8,128)(2,1)S(1)}, bf16[1,83,1024]{2,1,0:T(8,128)(2,1)}, u32[]{:S(2)}) copy-start(bf16[1,83,1024]{2,1,0:T(8,128)(2,1)} %param.15) | copy-start | bytes 509956
  21.2 11.8 %copy-start.4 = (f32[83]{0:T(128)S(1)}, f32[83]{0:T(128)}, u32[]{:S(2)}) copy-start(f32[83]{0:T(128)} %param.17) | copy-start | bytes 1000
  24.7 12.9 %copy-start.1 = (f32[1024]{0:T(1024)S(1)}, f32[1024]{0:T(1024)}, u32[]{:S(2)}) copy-start(f32[1024]{0:T(1024)} %param.16) | copy-start | bytes 12292
  24.7 6.3 %collective-permute-start.4 = (bf16[88,1024]{1,0:T(8,128)(2,1)S(1)}, bf16[88,1024]{1,0:T(8,128)(2,1)S(1)}, u32[]{:S(2)}, u32[]{:S(2)}) collective-permute-start(bf16[88,1024]{1,0:T(8,128)(2,1)S(1)} %get-tuple-element.64.own1), channel_id=1, source_target_pairs={{0,48},{16,0},{32,16},{48,32},{1,49},{17,1},{33,17},{49,33},{2,50}... | collective-permute-start | bytes 540680 | tf_op jit(solution)/shard_map/ppermute | solution.py:434
  26.3 10.1 %collective-permute-start.8 = (bf16[88,1024]{1,0:T(8,128)(2,1)S(1)}, bf16[88,1024]{1,0:T(8,128)(2,1)S(1)}, u32[]{:S(2)}, u32[]{:S(2)}) collective-permute-start(bf16[88,1024]{1,0:T(8,128)(2,1)S(1)} %get-tuple-element.64.own1), channel_id=1, source_target_pairs={{0,16},{16,32},{32,48},{48,0},{1,17},{17,33},{33,49},{49,1},{2,18}... | collective-permute-start | bytes 540680 | tf_op jit(solution)/shard_map/ppermute | solution.py:434
  26.8 9.6 %collective-permute-start.9 = (bf16[88,1024]{1,0:T(8,128)(2,1)S(1)}, bf16[88,1024]{1,0:T(8,128)(2,1)S(1)}, u32[]{:S(2)}, u32[]{:S(2)}) collective-permute-start(bf16[88,1024]{1,0:T(8,128)(2,1)S(1)} %collective-permute-done.5.o10), channel_id=1, source_target_pairs={{0,16},{16,32},{32,48},{48,0},{1,17},{17,33},{33,49},{49,1},{2,18}... | collective-permute-start | bytes 540680 | tf_op jit(solution)/shard_map/ppermute | solution.py:434
  31.0 6.6 %collective-permute-start.7 = (bf16[88,1024]{1,0:T(8,128)(2,1)S(1)}, bf16[88,1024]{1,0:T(8,128)(2,1)S(1)}, u32[]{:S(2)}, u32[]{:S(2)}) collective-permute-start(bf16[88,1024]{1,0:T(8,128)(2,1)S(1)} %collective-permute-done.4.o21), channel_id=1, source_target_pairs={{0,48},{16,0},{32,16},{48,32},{1,49},{17,1},{33,17},{49,33},{2,50}... | collective-permute-start | bytes 540680 | tf_op jit(solution)/shard_map/ppermute | solution.py:434
  40.2 2.5 %collective-permute-start.10 = (bf16[256,640]{1,0:T(8,128)(2,1)S(1)}, bf16[256,640]{1,0:T(8,128)(2,1)S(1)}, u32[]{:S(2)}, u32[]{:S(2)}) collective-permute-start(bf16[256,640]{1,0:T(8,128)(2,1)S(1)} %get-tuple-element.87), channel_id=1, source_target_pairs={{0,64},{64,0},{1,65},{65,1},{2,66},{66,2},{3,67},{67,3},{4,68},{68... | collective-permute-start | bytes 983048 | tf_op jit(solution)/shard_map/ppermute | solution.py:524
  42.8 7.9 %collective-permute-start.11 = (bf16[128,640]{1,0:T(8,128)(2,1)S(1)}, bf16[128,640]{1,0:T(8,128)(2,1)S(1)}, u32[]{:S(2)}, u32[]{:S(2)}) collective-permute-start(bf16[128,640]{1,0:T(8,128)(2,1)S(1)} %get-tuple-element.90), channel_id=1, source_target_pairs={{0,48},{16,32},{32,16},{48,0},{1,49},{17,33},{33,17},{49,1},{2,50}... | collective-permute-start | bytes 491528 | tf_op jit(solution)/shard_map/ppermute | solution.py:538
  45.0 26.1 %collective-permute-start.12 = (bf16[2,256,512]{2,1,0:T(8,128)(2,1)S(1)}, bf16[2,256,512]{2,1,0:T(8,128)(2,1)S(1)}, u32[]{:S(2)}, u32[]{:S(2)}) collective-permute-start(bf16[2,256,512]{2,1,0:T(8,128)(2,1)S(1)} %get-tuple-element.96), channel_id=1, source_target_pairs={{0,1},{1,0},{2,3},{3,2},{4,5},{5,4},{6,7},{7,6},{8,9},{9,8},{10,11... | collective-permute-start | bytes 1572872 | tf_op jit(solution)/shard_map/ppermute | solution.py:540
  45.0 26.1 %collective-permute-start.13 = (bf16[2,256,512]{2,1,0:T(8,128)(2,1)S(1)}, bf16[2,256,512]{2,1,0:T(8,128)(2,1)S(1)}, u32[]{:S(2)}, u32[]{:S(2)}) collective-permute-start(bf16[2,256,512]{2,1,0:T(8,128)(2,1)S(1)} %get-tuple-element.97), channel_id=1, source_target_pairs={{0,15},{1,2},{2,1},{3,4},{4,3},{5,6},{6,5},{7,8},{8,7},{9,10},{10,... | collective-permute-start | bytes 1572872 | tf_op jit(solution)/shard_map/ppermute | solution.py:541
  50.7 5.3 %collective-permute-start.14 = (bf16[64,640]{1,0:T(8,128)(2,1)S(1)}, bf16[64,640]{1,0:T(8,128)(2,1)S(1)}, u32[]{:S(2)}, u32[]{:S(2)}) collective-permute-start(bf16[64,640]{1,0:T(8,128)(2,1)S(1)} %get-tuple-element.91.later), channel_id=1, source_target_pairs={{0,16},{16,0},{32,48},{48,32},{1,17},{17,1},{33,49},{49,33},{2,18}... | collective-permute-start | bytes 245768 | tf_op jit(solution)/shard_map/ppermute | solution.py:543

commit v5 on v4

--- a/solution.py
+++ b/solution.py
@@ -68,7 +68,7 @@
 
 
 def parity():
-    return lax.rem(lax.axis_index("space"), 2)
+    return lax.rem(lax.axis_index("space") + 1, 2)
 
 
 def edges_kernel(lat, near0, far0, near1, far1, sems):
@@ -192,7 +192,7 @@
 CHUNK = 256
 
 
-def fields_kernel(acc, near, far, halo_w, w_in, w_out, later, lat_out, fields):
+def fields_kernel(acc, near, far, halo_w, w_in, w_out, lat_out, fields):
     count = acc.shape[0]
     half_k = near.shape[0]
     for start in range(0, count, 2 * CHUNK):
@@ -292,44 +292,51 @@
         far[m] = dot(halo_wt[half_k:], grad_grid[...], NT).astype(bf16)
 
 
-def owned_kernel(grad_grid0, grad_grid1, own_wt, later, out, edge, parts, sems):
-    step = edge.shape[2]
+def owned_kernel(grad_grid, own_wt, base, out, edge, parts, sems, *, member):
+    step = edge.shape[1]
     count = own_wt.shape[0] // step
     copies = []
-    for m, grad_grid in enumerate((grad_grid0, grad_grid1)):
-        for i in range(count):
-            value = dot(own_wt[i * step : (i + 1) * step], grad_grid[...], NT)
-            if i == 0:
-                edge[m, 0] = value
-            elif i == count - 1:
-                edge[m, 1] = value
-            else:
-                slot = len(copies)
-                parts[slot] = value
-                copy = pltpu.make_async_copy(
-                    parts.at[slot], out.at[m, i * step : (i + 1) * step], sems.at[slot]
-                )
-                copy.start()
-                copies.append(copy)
+    for i in range(count):
+        value = dot(own_wt[i * step : (i + 1) * step], grad_grid[...], NT)
+        if i == 0:
+            edge[0] = value
+        elif i == count - 1:
+            edge[1] = value
+        else:
+            slot = len(copies)
+            parts[slot] = value
+            copy = pltpu.make_async_copy(
+                parts.at[slot], out.at[member, i * step : (i + 1) * step], sems.at[slot]
+            )
+            copy.start()
+            copies.append(copy)
     for copy in copies:
         copy.wait()
 
 
-def add_rim_kernel(base, edge, near, far, out, parts, sems):
-    step = edge.shape[2]
+def finish_kernel(
+    base, edge0, edge1, near, far, got, out, grad_in, grad_out, parts, sems,
+):
+    step = edge0.shape[1]
     last = out.shape[1] - step
     odd = parity()
     copies = []
-    for side, got in ((1 - odd, near), (odd, far)):
+    for side, rim in ((1 - odd, near), (odd, far)):
         start = pl.multiple_of(side * last, step)
-        for m in range(edge.shape[0]):
+        for m, edge in enumerate((edge0, edge1)):
             slot = len(copies)
-            parts[slot] = edge[m, side] + got[m].astype(f32)
+            parts[slot] = edge[side] + rim[m].astype(f32)
             copy = pltpu.make_async_copy(
                 parts.at[slot], out.at[m, pl.ds(start, step)], sems.at[slot]
             )
             copy.start()
             copies.append(copy)
+    value = got[0].astype(f32)
+    for p in range(1, got.shape[0]):
+        value = value + got[p].astype(f32)
+    wide = grad_in.shape[1]
+    grad_in[...] = value[:, :wide]
+    grad_out[...] = value[:, wide : wide + grad_out.shape[1]]
     for copy in copies:
         copy.wait()
 
@@ -355,20 +362,11 @@
     )(kept, got)
 
 
-def scatter_kernel(kept, got, later, out):
+def scatter_kernel(kept, got, out):
     value = kept[...] + got[...].astype(f32)
     parts, rows = out.shape[0], out.shape[1]
     for p in range(parts):
         out[p] = value[p * rows : (p + 1) * rows].astype(out.dtype)
-
-
-def finish_kernel(got, grad_in, grad_out):
-    value = got[0].astype(f32)
-    for p in range(1, got.shape[0]):
-        value = value + got[p].astype(f32)
-    wide = grad_in.shape[1]
-    grad_in[...] = value[:, :wide]
-    grad_out[...] = value[:, wide : wide + grad_out.shape[1]]
 
 
 def ring(count, distance):
@@ -390,9 +388,8 @@
     spaces = lax.axis_size("space")
     chips = lax.axis_size("member")
     ids = block_ids.T
-    first = [(i, i ^ 1) for i in range(spaces)]
-    second = [(i, ((i + 1) ^ 1) - 1) for i in range(spaces)]
-    second = [(i, j % spaces) for i, j in second]
+    first = [(i, (((i + 1) ^ 1) - 1) % spaces) for i in range(spaces)]
+    second = [(i, i ^ 1) for i in range(spaces)]
 
     edges = pl.pallas_call(
         edges_kernel,
@@ -404,8 +401,8 @@
     )(in_hbm(latents[0]))
     halos = []
     for m in range(members):
+        far = lax.ppermute(edges[2 * m + 1], "space", second)
         near = lax.ppermute(edges[2 * m], "space", first)
-        far = lax.ppermute(edges[2 * m + 1], "space", second)
         halos.append((near, far))
 
     scale_n = area[None, :]
@@ -433,25 +430,18 @@
     def along(x, distance):
         return lax.ppermute(x, "member", ring(chips, distance))
 
-    grid_latent, fields, acts, slopes = [], [], [], []
-    for m, acc in enumerate((acc0, acc1)):
-        near, far = halos[m]
-        lat_m, fields_m = pl.pallas_call(
+    def fields_of(acc, near, far):
+        return pl.pallas_call(
             fields_kernel,
-            in_specs=[vmem()] * 6 + [anywhere()],
+            in_specs=[vmem()] * 6,
             out_specs=[vmem()] * 2,
             out_shape=[held((n, feature), bf16), shape((rows_v, n), bf16)],
             compiler_params=params(8),
             cost_estimate=cost(100),
-        )(*in_vmem(acc), near, far, *in_vmem(halo_w, w_in_v, w_out_v), slopes[-1] if slopes else halo_w)
-        grid_latent.append(lat_m)
-        fields.append(fields_m)
-        if m == 0:
-            left0 = along(fields_m, 1)
-            right0 = along(fields_m, -1)
-        else:
-            lat_m, left0, right0 = lax.optimization_barrier((lat_m, left0, right0))
-        act_m, slope_m = pl.pallas_call(
+        )(*in_vmem(acc), near, far, *in_vmem(halo_w, w_in_v, w_out_v))
+
+    def slopes_of(lat_m):
+        return pl.pallas_call(
             slopes_kernel,
             in_specs=[vmem()] * 2,
             out_specs=[vmem()] * 2,
@@ -459,8 +449,22 @@
             compiler_params=params(8),
             cost_estimate=cost(100),
         )(*in_vmem(lat_m, w_in_v))
-        acts.append(act_m)
-        slopes.append(slope_m)
+
+    lat0, fields0 = fields_of(acc0, *halos[0])
+    left0 = along(fields0, 1)
+    right0 = along(fields0, -1)
+    lat1, fields1 = fields_of(acc1, *halos[1])
+    right1 = along(fields1, -1)
+    left1 = along(fields1, 1)
+    fields = [fields0, fields1]
+    first_lat, left0, right0 = lax.optimization_barrier((lat0, left0, right0))
+    act0, slope0 = slopes_of(first_lat)
+    far0 = along(left0, 1)
+    second_lat, _ = lax.optimization_barrier((lat1, slope0))
+    act1, slope1 = slopes_of(second_lat)
+    held_right1, _ = lax.optimization_barrier((right1, slope1))
+    far1 = along(held_right1, -1)
+    grid_latent, acts, slopes = [lat0, lat1], [act0, act1], [slope0, slope1]
 
     halo_wt, own_wt, w_in_t, w_out_t, target, scale_v = pl.pallas_call(
         functools.partial(turn_kernel, spaces=spaces),
@@ -481,12 +485,6 @@
         ids, block_count, *in_vmem(weight_v, w_in_v, w_out_v), targets[0], var_weight[None],
         slopes[1],
     )
-
-    right1 = along(fields[1], -1)
-    left1 = along(fields[1], 1)
-    far0 = along(left0, 1)
-    held_right1, _ = lax.optimization_barrier((right1, slopes[1]))
-    far1 = along(held_right1, -1)
 
     part0, part1 = pl.pallas_call(
         functools.partial(spread_kernel, ensemble=members * chips),
@@ -533,61 +531,67 @@
     )(*in_vmem(grad_pre0, grad_pre1, halo_wt, w_in_t))
 
     quarter = half_rows // chips
+    middle = blocks // HALO - 2
+
+    def owned_of(member, grad_grid, base):
+        whole = shape((members, blocks * nodes, feature), f32)
+        aliased = {} if base is None else {2: 0}
+        base = grad_grid if base is None else base
+        return pl.pallas_call(
+            functools.partial(owned_kernel, member=member),
+            in_specs=[vmem()] * 2 + [anywhere()],
+            out_specs=[hbm(), vmem()],
+            out_shape=[whole, held((2, edge_rows, feature), f32)],
+            scratch_shapes=[
+                pltpu.VMEM((middle, edge_rows, feature), f32),
+                pltpu.SemaphoreType.DMA((middle,)),
+            ],
+            input_output_aliases=aliased,
+            compiler_params=params(8),
+            cost_estimate=cost(2000),
+        )(*in_vmem(grad_grid, own_wt), base)
+
     swapped, _ = lax.optimization_barrier((swapped, grad_grid0))
     kept, send = halve(keep, swapped, 2)
     got = lax.ppermute(send, "member", [(i, chips - 1 - i) for i in range(chips)])
-    rim_near, rim_far, _ = lax.optimization_barrier((rim_near, rim_far, send))
+    rim_near, rim_far, grad_grid0, _ = lax.optimization_barrier(
+        (rim_near, rim_far, grad_grid0, send)
+    )
+    got_far = lax.ppermute(rim_far, "space", second)
     got_near = lax.ppermute(rim_near, "space", first)
-    got_far = lax.ppermute(rim_far, "space", second)
+    owned, edge0 = owned_of(0, grad_grid0, None)
+    got, _ = lax.optimization_barrier((got, edge0))
     kept, send = halve(kept, got, 1)
     got = lax.ppermute(send, "member", [(i, i ^ 1) for i in range(chips)])
-
-    middle = blocks // HALO - 2
-    owned, edge = pl.pallas_call(
-        owned_kernel,
-        in_specs=[vmem()] * 3 + [anywhere()],
-        out_specs=[hbm(), vmem()],
-        out_shape=[
-            shape((members, blocks * nodes, feature), f32),
-            held((members, 2, edge_rows, feature), f32),
-        ],
-        scratch_shapes=[
-            pltpu.VMEM((members * middle, edge_rows, feature), f32),
-            pltpu.SemaphoreType.DMA((members * middle,)),
-        ],
-        compiler_params=params(12),
-        cost_estimate=cost(2000),
-    )(*in_vmem(grad_grid0, grad_grid1, own_wt), send)
+    grad_grid1, _ = lax.optimization_barrier((grad_grid1, send))
+    owned, edge1 = owned_of(1, grad_grid1, owned)
+    got, _ = lax.optimization_barrier((got, edge1))
 
     last_rows = quarter // spaces
     spread = pl.pallas_call(
         scatter_kernel,
-        in_specs=[vmem()] * 2 + [anywhere()],
+        in_specs=[vmem()] * 2,
         out_specs=vmem(),
         out_shape=shape((spaces, last_rows, wide), bf16),
         compiler_params=params(8),
-    )(kept, got, edge)
+    )(kept, got)
     spread = lax.all_to_all(spread, "space", 0, 0, tiled=True)
-    grad_w_in, grad_w_out = pl.pallas_call(
+    grad_latent, grad_w_in, grad_w_out = pl.pallas_call(
         finish_kernel,
-        in_specs=[vmem()],
-        out_specs=[vmem()] * 2,
-        out_shape=[shape((last_rows, feature), f32), shape((last_rows, variables), f32)],
-        compiler_params=params(8),
-    )(spread)
-
-    grad_latent = pl.pallas_call(
-        add_rim_kernel,
-        in_specs=[hbm(), vmem(), vmem(), vmem()],
-        out_specs=hbm(),
-        out_shape=shape(owned.shape, f32),
+        in_specs=[hbm()] + [vmem()] * 5,
+        out_specs=[hbm(), vmem(), vmem()],
+        out_shape=[
+            shape(owned.shape, f32),
+            shape((last_rows, feature), f32),
+            shape((last_rows, variables), f32),
+        ],
         scratch_shapes=[
             pltpu.VMEM((2 * members, edge_rows, feature), f32),
             pltpu.SemaphoreType.DMA((2 * members,)),
         ],
         input_output_aliases={0: 0},
         compiler_params=params(8),
-    )(owned, *in_vmem(edge), got_near, got_far)
+    )(owned, *in_vmem(edge0, edge1), got_near, got_far, spread)
     return grad_latent[None], grad_w_in, grad_w_out.T
 
 

time: 73.4 us -> 73.8 us (level)
  waiting for transfers between devices: 3.5 us -> 6.13 us
  blocking collectives: 14.5 us -> 12.7 us
    ppermute x1, starting transfers between devices: 5.59 us -> 0.01 us  [local(): got_far = lax.ppermute(rim_far, 'space', second)]
    ppermute x2, starting transfers between devices: 2.08 us -> 7.16 us  [local(): near = lax.ppermute(edges[2 * m], 'space', first)]
    ppermute x2, starting transfers between devices: 6.6 us -> 1.52 us  [local(): far = lax.ppermute(edges[2 * m + 1], 'space', second)]
    ppermute x1, starting transfers between devices: 0.01 us -> 2.95 us  [local(): got_near = lax.ppermute(rim_near, 'space', first)]
    ppermute x6, starting transfers between devices: 7.69 us -> 9.62 us  [along(): return lax.ppermute(x, 'member', ring(chips, distance))]
    all_to_all x1, blocking collectives: 14.5 us -> 12.7 us  [local(): spread = lax.all_to_all(spread, 'space', 0, 0, tiled=True)]
    ppermute x1, waiting for transfers between devices: 0.01 us -> 1.47 us  [local(): got = lax.ppermute(send, 'member', [(i, i ^ 1) for i in range(chips)])]
    ppermute x2, waiting for transfers between devices: 1 us -> 2.1 us  [local(): far = lax.ppermute(edges[2 * m + 1], 'space', second)]
  transfers between devices with their start and end apart: 15 -> 15, of which waited for: 3 -> 4; matrix products, arithmetic and copies ran while one was open for 0% -> 0% of each run, Pallas kernels for 33% -> 33%
where the time goes in v5:
time: 73.8 us; the launch traced here: 73.6 us
  Pallas kernels  30 us (41%)
  starting transfers between devices  23.7 us (32%)
  blocking collectives  12.7 us (17%)
  waiting for transfers between devices  6.13 us (8%)
  between operations  1.02 us (1%)
    all_to_all x1, blocking collectives, local(): spread = lax.all_to_all(spread, 'space', 0, 0, tiled=True)  12.7 us
    ppermute x6, starting transfers between devices, along(): return lax.ppermute(x, 'member', ring(chips, distance))  9.62 us
    ppermute x2, starting transfers between devices, local(): near = lax.ppermute(edges[2 * m], 'space', first)  7.16 us
    pallas_call x2, Pallas kernels, owned_of(): pl.pallas_call(functools.partial(owned_kernel, member=member), in_specs=[...  5.89 us
    pallas_call x1, Pallas kernels, local(): pl.pallas_call(functools.partial(prepare_kernel, spaces=spaces), in_specs...  4.32 us
    pallas_call x2, Pallas kernels, fields_of(): pl.pallas_call(fields_kernel, in_specs=[vmem()] * 6, out_specs=[vmem()] *...  3.88 us
    pallas_call x1, Pallas kernels, local(): pl.pallas_call(functools.partial(turn_kernel, spaces=spaces), in_specs=[s...  3.32 us
    pallas_call x2, Pallas kernels, slopes_of(): pl.pallas_call(slopes_kernel, in_specs=[vmem()] * 2, out_specs=[vmem()] *...  3.02 us
  transfers between devices with their start and end apart: 15, of which 4 were waited for; matrix products, arithmetic and copies ran while one was open for 0% of the time, Pallas kernels for 33%

profile of v5, /device:TPU:0, one launch (start us, length us, event | category | flops | bytes accessed | tf_op | source)
XLA Modules:
  0.0 73.6 jit_solution(5738724423417144766)
XLA Ops:
  0.6 0.0 copy-start.3
  0.6 0.0 copy-start.2
  0.7 1.2 %shard_map.113 = (bf16[256,512]{1,0:T(8,128)(2,1)S(1)}, bf16[256,512]{1,0:T(8,128)(2,1)S(1)}, bf16[256,512]{1,0:T(8,128)(2,1)S(1)}, bf16[256,512]{1,0:T(8,128)(2,1)S(1)}) custom-call(bf16[2,2048,512]{2,1,0:T(8,128)(2,1)} %bitcast.14), custom_call_target="tpu_custom_call" | custom-call | tf_op jit(solution)/shard_map/pallas_call | solution.py:394
  1.9 6.7 %collective-permute-start = (bf16[256,512]{1,0:T(8,128)(2,1)S(1)}, bf16[256,512]{1,0:T(8,128)(2,1)S(1)}, u32[]{:S(2)}, u32[]{:S(2)}) collective-permute-start(bf16[256,512]{1,0:T(8,128)(2,1)S(1)} %get-tuple-element.61), channel_id=1, source_target_pairs={{0,15},{1,2},{2,1},{3,4},{4,3},{5,6},{6,5},{7,8},{8,7},{9,10},{10,... | collective-permute-start | bytes 786440 | tf_op jit(solution)/shard_map/ppermute | solution.py:405
  8.5 0.0 collective-permute-start.1
  8.5 0.5 collective-permute-start.2
  9.1 1.5 %collective-permute-start.3 = (bf16[256,512]{1,0:T(8,128)(2,1)S(1)}, bf16[256,512]{1,0:T(8,128)(2,1)S(1)}, u32[]{:S(2)}, u32[]{:S(2)}) collective-permute-start(bf16[256,512]{1,0:T(8,128)(2,1)S(1)} %get-tuple-element.69), channel_id=1, source_target_pairs={{0,1},{1,0},{2,3},{3,2},{4,5},{5,4},{6,7},{7,6},{8,9},{9,8},{10,11... | collective-permute-start | bytes 786440 | tf_op jit(solution)/shard_map/ppermute | solution.py:404
  10.6 0.0 copy-done.3
  10.6 0.0 copy-done.2
  10.6 4.3 %shard_map.112 = (f32[1024,512]{1,0:T(8,128)S(1)}, f32[1024,512]{1,0:T(8,128)S(1)}, bf16[1024,512]{1,0:T(8,128)(2,1)S(1)}, bf16[512,512]{1,0:T(8,128)(2,1)S(1)},...) custom-call(s32[4,8]{1,0:T(4,128)S(1)} %bitcast.10, s32[8]{0:T(128)S(1)} %copy-done.3, ...), custom_call_target="tpu_custom_call" | custom-call | flops 2000000000 | bytes 8000000 | tf_op jit(solution)/shard_map/pallas_call | solution.py:410
  14.9 0.8 %collective-permute-done.near = bf16[256,512]{1,0:T(8,128)(2,1)S(1)} collective-permute-done((bf16[256,512]{1,0:T(8,128)(2,1)S(1)}, bf16[256,512]{1,0:T(8,128)(2,1)S(1)}, u32[]{:S(2)}, u32[]{:S(2)}) %collective-permute-start) | collective-permute-done | bytes 262176 | tf_op jit(solution)/shard_map/ppermute | solution.py:405
  15.7 2.1 %collective-permute-done.1.far = bf16[256,512]{1,0:T(8,128)(2,1)S(1)} collective-permute-done((bf16[256,512]{1,0:T(8,128)(2,1)S(1)}, bf16[256,512]{1,0:T(8,128)(2,1)S(1)}, u32[]{:S(2)}, u32[]{:S(2)}) %collective-permute-start.1) | collective-permute-done | bytes 262176 | tf_op jit(solution)/shard_map/ppermute | solution.py:404
  17.8 1.9 %shard_map.114 = (bf16[1024,512]{1,0:T(8,128)(2,1)S(1)}, bf16[88,1024]{1,0:T(8,128)(2,1)S(1)}) custom-call(f32[1024,512]{1,0:T(8,128)S(1)} %get-tuple-element.60.acc, bf16[256,512]{1,0:T(8,128)(2,1)S(1)} %collective-permute-done.near, bf16[256,512]{1,0:T(8,128)(2,1)S(1)} %collective-permute-done.1.far, bf16[1024,512]{1,0:T(8,128)(2,1)S(1)} %get-tuple-element.63.halo_w, ...), custom_call_target="tpu_custom_call" | custom-call | flops 100000000 | bytes 400000 | tf_op jit(solution)/shard_map/pallas_call | solution.py:434
  19.7 0.0 copy-start
  19.7 0.0 copy-start.4
  19.7 2.8 %collective-permute-start.6 = (bf16[88,1024]{1,0:T(8,128)(2,1)S(1)}, bf16[88,1024]{1,0:T(8,128)(2,1)S(1)}, u32[]{:S(2)}, u32[]{:S(2)}) collective-permute-start(bf16[88,1024]{1,0:T(8,128)(2,1)S(1)} %get-tuple-element.66.own0), channel_id=1, source_target_pairs={{0,48},{16,0},{32,16},{48,32},{1,49},{17,1},{33,17},{49,33},{2,50}... | collective-permute-start | bytes 540680 | tf_op jit(solution)/shard_map/ppermute | solution.py:431
  22.6 0.0 collective-permute-start.5
  22.6 0.0 collective-permute-done.2.near
  22.6 0.0 collective-permute-done.3.far
  22.6 1.9 %shard_map.115 = (bf16[1024,512]{1,0:T(8,128)(2,1)S(1)}, bf16[88,1024]{1,0:T(8,128)(2,1)S(1)}) custom-call(f32[1024,512]{1,0:T(8,128)S(1)} %get-tuple-element.67.acc, bf16[256,512]{1,0:T(8,128)(2,1)S(1)} %collective-permute-done.2.near, bf16[256,512]{1,0:T(8,128)(2,1)S(1)} %collective-permute-done.3.far, bf16[1024,512]{1,0:T(8,128)(2,1)S(1)} %get-tuple-element.63.halo_w, ...), custom_call_target="tpu_custom_call" | custom-call | flops 100000000 | bytes 400000 | tf_op jit(solution)/shard_map/pallas_call | solution.py:434
  24.5 0.0 copy-start.1
  24.6 3.3 %collective-permute-start.4 = (bf16[88,1024]{1,0:T(8,128)(2,1)S(1)}, bf16[88,1024]{1,0:T(8,128)(2,1)S(1)}, u32[]{:S(2)}, u32[]{:S(2)}) collective-permute-start(bf16[88,1024]{1,0:T(8,128)(2,1)S(1)} %get-tuple-element.70.own1), channel_id=1, source_target_pairs={{0,48},{16,0},{32,16},{48,32},{1,49},{17,1},{33,17},{49,33},{2,50}... | collective-permute-start | bytes 540680 | tf_op jit(solution)/shard_map/ppermute | solution.py:431
  27.9 0.0 collective-permute-start.8
  27.9 0.0 collective-permute-done.6.o20
  27.9 1.8 %collective-permute-done.5.o10 = bf16[88,1024]{1,0:T(8,128)(2,1)S(1)} collective-permute-done((bf16[88,1024]{1,0:T(8,128)(2,1)S(1)}, bf16[88,1024]{1,0:T(8,128)(2,1)S(1)}, u32[]{:S(2)}, u32[]{:S(2)}) %collective-permute-start.5) | collective-permute-done | bytes 180256 | tf_op jit(solution)/shard_map/ppermute | solution.py:431
  29.6 0.0 collective-permute-start.9
  29.6 1.5 %shard_map.116 = (bf16[512,1024]{1,0:T(8,128)(2,1)S(1)}, bf16[512,1024]{1,0:T(8,128)(2,1)S(1)}) custom-call(bf16[1024,512]{1,0:T(8,128)(2,1)S(1)} %get-tuple-element.73.lat.lat0, bf16[512,512]{1,0:T(8,128)(2,1)S(1)} %get-tuple-element.64.w_in), custom_call_target="tpu_custom_call" | custom-call | flops 100000000 | bytes 400000 | tf_op jit(solution)/shard_map/pallas_call | solution.py:444
  31.1 1.5 %shard_map.117 = (bf16[512,1024]{1,0:T(8,128)(2,1)S(1)}, bf16[512,1024]{1,0:T(8,128)(2,1)S(1)}) custom-call(bf16[1024,512]{1,0:T(8,128)(2,1)S(1)} %get-tuple-element.75.lat.lat1, bf16[512,512]{1,0:T(8,128)(2,1)S(1)} %get-tuple-element.64.w_in), custom_call_target="tpu_custom_call" | custom-call | flops 100000000 | bytes 400000 | tf_op jit(solution)/shard_map/pallas_call | solution.py:444
  32.7 0.0 collective-permute-done.4.o21
  32.7 3.5 %collective-permute-start.7 = (bf16[88,1024]{1,0:T(8,128)(2,1)S(1)}, bf16[88,1024]{1,0:T(8,128)(2,1)S(1)}, u32[]{:S(2)}, u32[]{:S(2)}) collective-permute-start(bf16[88,1024]{1,0:T(8,128)(2,1)S(1)} %collective-permute-done.4.o21), channel_id=1, source_target_pairs={{0,48},{16,0},{32,16},{48,32},{1,49},{17,1},{33,17},{49,33},{2,50}... | collective-permute-start | bytes 540680 | tf_op jit(solution)/shard_map/ppermute | solution.py:431
  36.2 0.0 copy-done
  36.2 0.0 copy-done.4
  36.2 3.3 %shard_map.118 = (bf16[512,1024]{1,0:T(8,128)(2,1)S(1)}, bf16[2048,1024]{1,0:T(8,128)(2,1)S(1)}, bf16[512,512]{1,0:T(8,128)(2,1)S(1)}, bf16[512,88]{1,0:T(8,128)...) custom-call(s32[4,8]{1,0:T(4,128)S(1)} %bitcast.11, s32[8]{0:T(128)S(1)} %copy-done.3, ...), custom_call_target="tpu_custom_call" | custom-call | flops 100000000 | bytes 400000 | tf_op jit(solution)/shard_map/pallas_call | solution.py:469
  39.5 0.0 collective-permute-done.8.o11
  39.5 0.0 collective-permute-done.9.far0
  39.5 1.1 %shard_map.119 = (f32[88,1024]{1,0:T(8,128)S(1)}, f32[88,1024]{1,0:T(8,128)S(1)}) custom-call(bf16[88,1024]{1,0:T(8,128)(2,1)S(1)} %get-tuple-element.66.own0, bf16[88,1024]{1,0:T(8,128)(2,1)S(1)} %get-tuple-element.70.own1, bf16[88,1024]{1,0:T(8,128)(2,1)S(1)} %collective-permute-done.5.o10, bf16[88,1024]{1,0:T(8,128)(2,1)S(1)} %collective-permute-done.8.o11, ...), custom_call_target="tpu_custom_call" | custom-call | flops 100000000 | bytes 400000 | tf_op jit(solution)/shard_map/pallas_call | solution.py:489
  40.6 0.0 collective-permute-done.7.far1
  40.6 0.0 copy-done.1
  40.7 2.7 %shard_map.120 = (bf16[512,1024]{1,0:T(8,128)(2,1)S(1)}, bf16[512,1024]{1,0:T(8,128)(2,1)S(1)}, f32[256,640]{1,0:T(8,128)S(1)}, bf16[256,640]{1,0:T(8,128)(2,1)S(1)}) custom-call(bf16[88,1024]{1,0:T(8,128)(2,1)S(1)} %get-tuple-element.66.own0, bf16[88,1024]{1,0:T(8,128)(2,1)S(1)} %get-tuple-element.70.own1, ...), custom_call_target="tpu_custom_call" | custom-call | flops 2000000000 | bytes 8000000 | tf_op jit(solution)/shard_map/pallas_call | solution.py:500
  43.3 0.1 collective-permute-start.10
  43.4 2.3 %shard_map.121 = (bf16[512,1024]{1,0:T(8,128)(2,1)S(1)}, bf16[512,1024]{1,0:T(8,128)(2,1)S(1)}, bf16[2,256,512]{2,1,0:T(8,128)(2,1)S(1)}, bf16[2,256,512]{2,1,0:T(8,128)(2,1)S(1)}) custom-call(bf16[512,1024]{1,0:T(8,128)(2,1)S(1)} %get-tuple-element.88.grad_pre0, bf16[512,1024]{1,0:T(8,128)(2,1)S(1)} %get-tuple-element.89.grad_pre1, ...), custom_call_target="tpu_custom_call" | custom-call | flops 2000000000 | bytes 8000000 | tf_op jit(solution)/shard_map/pallas_call | solution.py:524
  45.8 0.0 collective-permute-done.10.got
  45.8 0.1 shard_map.122
  45.9 2.3 %collective-permute-start.11 = (bf16[128,640]{1,0:T(8,128)(2,1)S(1)}, bf16[128,640]{1,0:T(8,128)(2,1)S(1)}, u32[]{:S(2)}, u32[]{:S(2)}) collective-permute-start(bf16[128,640]{1,0:T(8,128)(2,1)S(1)} %get-tuple-element.98), channel_id=1, source_target_pairs={{0,48},{16,32},{32,16},{48,0},{1,49},{17,33},{33,17},{49,1},{2,50}... | collective-permute-start | bytes 491528 | tf_op jit(solution)/shard_map/ppermute | solution.py:556
  48.2 2.9 %collective-permute-start.12 = (bf16[2,256,512]{2,1,0:T(8,128)(2,1)S(1)}, bf16[2,256,512]{2,1,0:T(8,128)(2,1)S(1)}, u32[]{:S(2)}, u32[]{:S(2)}) collective-permute-start(bf16[2,256,512]{2,1,0:T(8,128)(2,1)S(1)} %get-tuple-element.110), channel_id=1, source_target_pairs={{0,15},{1,2},{2,1},{3,4},{4,3},{5,6},{6,5},{7,8},{8,7},{9,10},{10,... | collective-permute-start | bytes 1572872 | tf_op jit(solution)/shard_map/ppermute | solution.py:561
  51.1 0.0 collective-permute-start.13
  51.1 2.9 %shard_map.123 = (f32[2,2048,512]{2,1,0:T(8,128)}, f32[2,256,512]{2,1,0:T(8,128)S(1)}) custom-call(bf16[512,1024]{1,0:T(8,128)(2,1)S(1)} %get-tuple-element.101.grad_grid.base, bf16[2048,1024]{1,0:T(8,128)(2,1)S(1)} %get-tuple-element.102.own_wt, bf16[512,1024]{1,0:T(8,128)(2,1)S(1)} %get-tuple-element.101.grad_grid.base), custom_call_target="tpu_custom_call" | custom-call | flops 2000000000 | bytes 8000000 | tf_op jit(solution)/shard_map/pallas_call | solution.py:540
  54.1 0.0 collective-permute-done.11.got
  54.1 0.1 shard_map.124
  54.2 0.1 collective-permute-start.14
  54.3 2.9 %shard_map.125 = (f32[2,2048,512]{2,1,0:T(8,128)}, f32[2,256,512]{2,1,0:T(8,128)S(1)}) custom-call(bf16[512,1024]{1,0:T(8,128)(2,1)S(1)} %get-tuple-element.106.grad_grid, bf16[2048,1024]{1,0:T(8,128)(2,1)S(1)} %get-tuple-element.102.own_wt, f32[2,2048,512]{2,1,0:T(8,128)} %get-tuple-element.107.base), custom_call_target="tpu_custom_call", output_to_operand_aliasing={{0}: (2, {})} | custom-call | flops 2000000000 | bytes 8000000 | tf_op jit(solution)/shard_map/pallas_call | solution.py:540
  57.2 1.5 %collective-permute-done.14.got = bf16[64,640]{1,0:T(8,128)(2,1)S(1)} collective-permute-done((bf16[64,640]{1,0:T(8,128)(2,1)S(1)}, bf16[64,640]{1,0:T(8,128)(2,1)S(1)}, u32[]{:S(2)}, u32[]{:S(2)}) %collective-permute-start.14) | collective-permute-done | bytes 81952 | tf_op jit(solution)/shard_map/ppermute | solution.py:565
  58.7 12.7 %all_to_all.5.got = bf16[16,4,640]{2,1,0:T(4,128)(2,1)S(1)} all-to-all(bf16[16,4,640]{2,1,0:T(4,128)(2,1)S(1)} %shard_map.126), channel_id=1, replica_groups=mesh['dp'=2,'member'=4,'space'=16] {'space'}, dimensions={0} | all-to-all | bytes 163840 | tf_op jit(solution)/shard_map/all_to_all | solution.py:578
  71.4 0.0 collective-permute-done.12.near
  71.4 0.0 collective-permute-done.13.far
  71.4 2.0 %shard_map.127 = (f32[2,2048,512]{2,1,0:T(8,128)}, f32[4,512]{1,0:T(4,128)}, f32[4,83]{1,0:T(4,128)}) custom-call(f32[2,2048,512]{2,1,0:T(8,128)} %get-tuple-element.108.base, f32[2,256,512]{2,1,0:T(8,128)S(1)} %get-tuple-element.103.edge0, f32[2,256,512]{2,1,0:T(8,128)S(1)} %get-tuple-element.109.edge1, ...), custom_call_target="tpu_custom_call", output_to_operand_aliasing={{0}: (0, {})} | custom-call | tf_op jit(solution)/shard_map/pallas_call | solution.py:579
  (1 shorter events, 0.0 us)
Async XLA Ops:
  0.6 9.9 %copy-start.3 = (s32[8]{0:T(128)S(1)}, s32[8]{0:T(128)}, u32[]{:S(2)}) copy-start(s32[8]{0:T(128)} %count.3) | copy-start | bytes 100
  0.6 9.9 %copy-start.2 = (s32[8,4]{0,1:T(4,128)S(1)}, s32[8,4]{0,1:T(4,128)}, u32[]{:S(2)}) copy-start(s32[8,4]{0,1:T(4,128)} %param.11) | copy-start | bytes 388
  1.9 13.8 %collective-permute-start = (bf16[256,512]{1,0:T(8,128)(2,1)S(1)}, bf16[256,512]{1,0:T(8,128)(2,1)S(1)}, u32[]{:S(2)}, u32[]{:S(2)}) collective-permute-start(bf16[256,512]{1,0:T(8,128)(2,1)S(1)} %get-tuple-element.61), channel_id=1, source_target_pairs={{0,15},{1,2},{2,1},{3,4},{4,3},{5,6},{6,5},{7,8},{8,7},{9,10},{10,... | collective-permute-start | bytes 786440 | tf_op jit(solution)/shard_map/ppermute | solution.py:405
  8.5 9.2 %collective-permute-start.1 = (bf16[256,512]{1,0:T(8,128)(2,1)S(1)}, bf16[256,512]{1,0:T(8,128)(2,1)S(1)}, u32[]{:S(2)}, u32[]{:S(2)}) collective-permute-start(bf16[256,512]{1,0:T(8,128)(2,1)S(1)} %get-tuple-element.62), channel_id=1, source_target_pairs={{0,1},{1,0},{2,3},{3,2},{4,5},{5,4},{6,7},{7,6},{8,9},{9,8},{10,11... | collective-permute-start | bytes 786440 | tf_op jit(solution)/shard_map/ppermute | solution.py:404
  8.5 14.0 %collective-permute-start.2 = (bf16[256,512]{1,0:T(8,128)(2,1)S(1)}, bf16[256,512]{1,0:T(8,128)(2,1)S(1)}, u32[]{:S(2)}, u32[]{:S(2)}) collective-permute-start(bf16[256,512]{1,0:T(8,128)(2,1)S(1)} %get-tuple-element.68), channel_id=1, source_target_pairs={{0,15},{1,2},{2,1},{3,4},{4,3},{5,6},{6,5},{7,8},{8,7},{9,10},{10,... | collective-permute-start | bytes 786440 | tf_op jit(solution)/shard_map/ppermute | solution.py:405
  9.1 13.5 %collective-permute-start.3 = (bf16[256,512]{1,0:T(8,128)(2,1)S(1)}, bf16[256,512]{1,0:T(8,128)(2,1)S(1)}, u32[]{:S(2)}, u32[]{:S(2)}) collective-permute-start(bf16[256,512]{1,0:T(8,128)(2,1)S(1)} %get-tuple-element.69), channel_id=1, source_target_pairs={{0,1},{1,0},{2,3},{3,2},{4,5},{5,4},{6,7},{7,6},{8,9},{9,8},{10,11... | collective-permute-start | bytes 786440 | tf_op jit(solution)/shard_map/ppermute | solution.py:404
  19.7 16.4 %copy-start = (bf16[1,83,1024]{2,1,0:T(8,128)(2,1)S(1)}, bf16[1,83,1024]{2,1,0:T(8,128)(2,1)}, u32[]{:S(2)}) copy-start(bf16[1,83,1024]{2,1,0:T(8,128)(2,1)} %param.15) | copy-start | bytes 509956
  19.7 16.4 %copy-start.4 = (f32[83]{0:T(128)S(1)}, f32[83]{0:T(128)}, u32[]{:S(2)}) copy-start(f32[83]{0:T(128)} %param.17) | copy-start | bytes 1000
  19.7 8.1 %collective-permute-start.6 = (bf16[88,1024]{1,0:T(8,128)(2,1)S(1)}, bf16[88,1024]{1,0:T(8,128)(2,1)S(1)}, u32[]{:S(2)}, u32[]{:S(2)}) collective-permute-start(bf16[88,1024]{1,0:T(8,128)(2,1)S(1)} %get-tuple-element.66.own0), channel_id=1, source_target_pairs={{0,48},{16,0},{32,16},{48,32},{1,49},{17,1},{33,17},{49,33},{2,50}... | collective-permute-start | bytes 540680 | tf_op jit(solution)/shard_map/ppermute | solution.py:431
  22.6 7.0 %collective-permute-start.5 = (bf16[88,1024]{1,0:T(8,128)(2,1)S(1)}, bf16[88,1024]{1,0:T(8,128)(2,1)S(1)}, u32[]{:S(2)}, u32[]{:S(2)}) collective-permute-start(bf16[88,1024]{1,0:T(8,128)(2,1)S(1)} %get-tuple-element.66.own0), channel_id=1, source_target_pairs={{0,16},{16,32},{32,48},{48,0},{1,17},{17,33},{33,49},{49,1},{2,18}... | collective-permute-start | bytes 540680 | tf_op jit(solution)/shard_map/ppermute | solution.py:431
  24.5 16.1 %copy-start.1 = (f32[1024]{0:T(1024)S(1)}, f32[1024]{0:T(1024)}, u32[]{:S(2)}) copy-start(f32[1024]{0:T(1024)} %param.16) | copy-start | bytes 12292
  24.6 8.1 %collective-permute-start.4 = (bf16[88,1024]{1,0:T(8,128)(2,1)S(1)}, bf16[88,1024]{1,0:T(8,128)(2,1)S(1)}, u32[]{:S(2)}, u32[]{:S(2)}) collective-permute-start(bf16[88,1024]{1,0:T(8,128)(2,1)S(1)} %get-tuple-element.70.own1), channel_id=1, source_target_pairs={{0,48},{16,0},{32,16},{48,32},{1,49},{17,1},{33,17},{49,33},{2,50}... | collective-permute-start | bytes 540680 | tf_op jit(solution)/shard_map/ppermute | solution.py:431
  27.9 11.6 %collective-permute-start.8 = (bf16[88,1024]{1,0:T(8,128)(2,1)S(1)}, bf16[88,1024]{1,0:T(8,128)(2,1)S(1)}, u32[]{:S(2)}, u32[]{:S(2)}) collective-permute-start(bf16[88,1024]{1,0:T(8,128)(2,1)S(1)} %get-tuple-element.70.own1), channel_id=1, source_target_pairs={{0,16},{16,32},{32,48},{48,0},{1,17},{17,33},{33,49},{49,1},{2,18}... | collective-permute-start | bytes 540680 | tf_op jit(solution)/shard_map/ppermute | solution.py:431
  29.6 9.9 %collective-permute-start.9 = (bf16[88,1024]{1,0:T(8,128)(2,1)S(1)}, bf16[88,1024]{1,0:T(8,128)(2,1)S(1)}, u32[]{:S(2)}, u32[]{:S(2)}) collective-permute-start(bf16[88,1024]{1,0:T(8,128)(2,1)S(1)} %collective-permute-done.5.o10), channel_id=1, source_target_pairs={{0,16},{16,32},{32,48},{48,0},{1,17},{17,33},{33,49},{49,1},{2,18}... | collective-permute-start | bytes 540680 | tf_op jit(solution)/shard_map/ppermute | solution.py:431
  32.7 8.0 %collective-permute-start.7 = (bf16[88,1024]{1,0:T(8,128)(2,1)S(1)}, bf16[88,1024]{1,0:T(8,128)(2,1)S(1)}, u32[]{:S(2)}, u32[]{:S(2)}) collective-permute-start(bf16[88,1024]{1,0:T(8,128)(2,1)S(1)} %collective-permute-done.4.o21), channel_id=1, source_target_pairs={{0,48},{16,0},{32,16},{48,32},{1,49},{17,1},{33,17},{49,33},{2,50}... | collective-permute-start | bytes 540680 | tf_op jit(solution)/shard_map/ppermute | solution.py:431
  43.3 2.5 %collective-permute-start.10 = (bf16[256,640]{1,0:T(8,128)(2,1)S(1)}, bf16[256,640]{1,0:T(8,128)(2,1)S(1)}, u32[]{:S(2)}, u32[]{:S(2)}) collective-permute-start(bf16[256,640]{1,0:T(8,128)(2,1)S(1)} %get-tuple-element.94), channel_id=1, source_target_pairs={{0,64},{64,0},{1,65},{65,1},{2,66},{66,2},{3,67},{67,3},{4,68},{68... | collective-permute-start | bytes 983048 | tf_op jit(solution)/shard_map/ppermute | solution.py:522
  45.9 8.2 %collective-permute-start.11 = (bf16[128,640]{1,0:T(8,128)(2,1)S(1)}, bf16[128,640]{1,0:T(8,128)(2,1)S(1)}, u32[]{:S(2)}, u32[]{:S(2)}) collective-permute-start(bf16[128,640]{1,0:T(8,128)(2,1)S(1)} %get-tuple-element.98), channel_id=1, source_target_pairs={{0,48},{16,32},{32,16},{48,0},{1,49},{17,33},{33,17},{49,1},{2,50}... | collective-permute-start | bytes 491528 | tf_op jit(solution)/shard_map/ppermute | solution.py:556
  48.2 23.3 %collective-permute-start.12 = (bf16[2,256,512]{2,1,0:T(8,128)(2,1)S(1)}, bf16[2,256,512]{2,1,0:T(8,128)(2,1)S(1)}, u32[]{:S(2)}, u32[]{:S(2)}) collective-permute-start(bf16[2,256,512]{2,1,0:T(8,128)(2,1)S(1)} %get-tuple-element.110), channel_id=1, source_target_pairs={{0,15},{1,2},{2,1},{3,4},{4,3},{5,6},{6,5},{7,8},{8,7},{9,10},{10,... | collective-permute-start | bytes 1572872 | tf_op jit(solution)/shard_map/ppermute | solution.py:561
  51.1 20.3 %collective-permute-start.13 = (bf16[2,256,512]{2,1,0:T(8,128)(2,1)S(1)}, bf16[2,256,512]{2,1,0:T(8,128)(2,1)S(1)}, u32[]{:S(2)}, u32[]{:S(2)}) collective-permute-start(bf16[2,256,512]{2,1,0:T(8,128)(2,1)S(1)} %get-tuple-element.111), channel_id=1, source_target_pairs={{0,1},{1,0},{2,3},{3,2},{4,5},{5,4},{6,7},{7,6},{8,9},{9,8},{10,11... | collective-permute-start | bytes 1572872 | tf_op jit(solution)/shard_map/ppermute | solution.py:560
  54.2 4.5 %collective-permute-start.14 = (bf16[64,640]{1,0:T(8,128)(2,1)S(1)}, bf16[64,640]{1,0:T(8,128)(2,1)S(1)}, u32[]{:S(2)}, u32[]{:S(2)}) collective-permute-start(bf16[64,640]{1,0:T(8,128)(2,1)S(1)} %get-tuple-element.105), channel_id=1, source_target_pairs={{0,16},{16,0},{32,48},{48,32},{1,17},{17,1},{33,49},{49,33},{2,18}... | collective-permute-start | bytes 245768 | tf_op jit(solution)/shard_map/ppermute | solution.py:565

commit v6 on v5

--- a/solution.py
+++ b/solution.py
@@ -98,12 +98,14 @@
 
 
 def prepare_kernel(
-    ids, count, lat_hbm, weight_hbm, w_in_hbm, w_out,
-    acc0, acc1, halo_w, w_in_v, w_out_v, weight, lat, sems, *, spaces,
+    ids_hbm, count_hbm, lat_hbm, weight_hbm, w_in_hbm, w_out,
+    acc0, acc1, halo_w, w_in_v, w_out_v, weight, ids, count, lat, sems, *, spaces,
 ):
     tiles, slots, cells, nodes = weight.shape
     blocks = lat.shape[1]
     copies = [
+        pltpu.make_async_copy(ids_hbm, ids, sems.at[4]),
+        pltpu.make_async_copy(count_hbm, count, sems.at[5]),
         pltpu.make_async_copy(weight_hbm, weight, sems.at[0]),
         pltpu.make_async_copy(lat_hbm.at[0], lat.at[0], sems.at[1]),
         pltpu.make_async_copy(lat_hbm.at[1], lat.at[1], sems.at[2]),
@@ -114,23 +116,19 @@
     halo_w[...] = jnp.zeros_like(halo_w)
     w_out_v[...] = jnp.zeros_like(w_out_v)
     w_out_v[: w_out.shape[0]] = w_out[...]
-    copies[0].wait()
-
-    def place_tile(t, carry):
+    for c in copies[:3]:
+        c.wait()
+
+    unused = halo_w.shape[1] // nodes - 1
+    for t in range(tiles):
+        rows = slice(t * cells, (t + 1) * cells)
         for k in range(slots):
-            e = ids[k, t]
-            outside, slot = halo_slot(e, blocks, spaces)
-
-            @pl.when((k < count[t]) & outside)
-            def _():
-                halo_w[rows_at(t, cells), rows_at(slot, nodes)] += weight[t, k]
-
-        return carry
-
-    lax.fori_loop(0, tiles, place_tile, 0)
+            outside, slot = halo_slot(ids[k, t], blocks, spaces)
+            slot = jnp.where((k < count[t]) & outside, slot, unused)
+            halo_w[rows, rows_at(slot, nodes)] += weight[t, k]
 
     for m, acc in enumerate((acc0, acc1)):
-        copies[1 + m].wait()
+        copies[3 + m].wait()
         for t in range(tiles):
             parts, at = [], []
             for k in range(slots):
@@ -142,17 +140,15 @@
             lhs = jnp.concatenate(parts, axis=1)
             rhs = jnp.concatenate([lat[m, a] for a in at], axis=0)
             acc[t * cells : (t + 1) * cells] = dot(lhs, rhs)
-    copies[3].wait()
+    copies[5].wait()
 
 
 def turn_kernel(
     ids, count, weight, w_in, w_out, target, var_weight, later,
-    halo_wt, own_wt, w_in_t, w_out_t, target_v, scale_v, square, *, spaces,
+    turned, w_in_t, w_out_t, target_v, scale_v, square, *, spaces, blocks,
 ):
     tiles, slots, cells, nodes = weight.shape
-    blocks = own_wt.shape[0] // nodes
-    halo_wt[...] = jnp.zeros_like(halo_wt)
-    own_wt[...] = jnp.zeros_like(own_wt)
+    turned[...] = jnp.zeros_like(turned)
     w_in_t[...] = w_in[...].T
     w_out_t[...] = w_out[...].T
     variables = target.shape[0]
@@ -161,26 +157,16 @@
     square[...] = jnp.zeros_like(square)
     square[:1, :variables] = var_weight[...]
     scale_v[...] = square[...].T[: scale_v.shape[0], :1]
-
-    def place_tile(t, carry):
+    unused = turned.shape[0] // nodes - 1
+    for t in range(tiles):
+        columns = slice(t * cells, (t + 1) * cells)
         for k in range(slots):
             e = ids[k, t]
-            live = k < count[t]
             outside, slot = halo_slot(e, blocks, spaces)
             mine = (e >= HALO) & (e < HALO + blocks)
-            block = jnp.clip(e - HALO, 0, blocks - 1)
-
-            @pl.when(live & outside)
-            def _():
-                halo_wt[rows_at(slot, nodes), rows_at(t, cells)] += weight[t, k].T
-
-            @pl.when(live & mine)
-            def _():
-                own_wt[rows_at(block, nodes), rows_at(t, cells)] += weight[t, k].T
-
-        return carry
-
-    lax.fori_loop(0, tiles, place_tile, 0)
+            block = jnp.where(mine, e - HALO, jnp.where(outside, blocks + slot, unused))
+            block = jnp.where(k < count[t], block, unused)
+            turned[rows_at(block, nodes), columns] += weight[t, k].T
 
 
 def gelu_parts(x):
@@ -198,7 +184,7 @@
     for start in range(0, count, 2 * CHUNK):
         at = slice(start, start + 2 * CHUNK)
         total = acc[at] + dot(halo_w[at, :half_k], near[...])
-        total = total + dot(halo_w[at, half_k:], far[...])
+        total = total + dot(halo_w[at, half_k : 2 * half_k], far[...])
         rounded = total.astype(bf16)
         lat_out[at] = rounded
         pre = dot(w_in[...], rounded, NT)
@@ -282,34 +268,34 @@
     send[:, wide:] = total_out[leave].astype(bf16)
 
 
-def rim_kernel(grad_pre0, grad_pre1, halo_wt, w_in_t, grad_grid0, grad_grid1, near, far):
+def rim_kernel(
+    grad_pre0, grad_pre1, turned, w_in_t, grad_grid0, grad_grid1, near, far, *, own_rows,
+):
     half_k = near.shape[1]
+    middle = own_rows + half_k
     for m, (grad_pre, grad_grid) in enumerate(
         ((grad_pre0, grad_grid0), (grad_pre1, grad_grid1))
     ):
         grad_grid[...] = dot(w_in_t[...], grad_pre[...]).astype(bf16)
-        near[m] = dot(halo_wt[:half_k], grad_grid[...], NT).astype(bf16)
-        far[m] = dot(halo_wt[half_k:], grad_grid[...], NT).astype(bf16)
-
-
-def owned_kernel(grad_grid, own_wt, base, out, edge, parts, sems, *, member):
-    step = edge.shape[1]
-    count = own_wt.shape[0] // step
+        near[m] = dot(turned[own_rows:middle], grad_grid[...], NT).astype(bf16)
+        far[m] = dot(turned[middle : middle + half_k], grad_grid[...], NT).astype(bf16)
+
+
+def owned_kernel(grad_grid, turned, base, out, edge, parts, sems, *, member, own_rows):
+    step, size = edge.shape[1], parts.shape[1]
     copies = []
-    for i in range(count):
-        value = dot(own_wt[i * step : (i + 1) * step], grad_grid[...], NT)
-        if i == 0:
-            edge[0] = value
-        elif i == count - 1:
-            edge[1] = value
-        else:
-            slot = len(copies)
-            parts[slot] = value
-            copy = pltpu.make_async_copy(
-                parts.at[slot], out.at[member, i * step : (i + 1) * step], sems.at[slot]
-            )
-            copy.start()
-            copies.append(copy)
+    for slot in range(parts.shape[0]):
+        start = step + slot * size
+        parts[slot] = dot(turned[start : start + size], grad_grid[...], NT)
+        copy = pltpu.make_async_copy(
+            parts.at[slot], out.at[member, start : start + size], sems.at[slot]
+        )
+        copy.start()
+        copies.append(copy)
+    ends = jnp.concatenate([turned[:step], turned[own_rows - step : own_rows]], axis=0)
+    value = dot(ends, grad_grid[...], NT)
+    edge[0] = value[:step]
+    edge[1] = value[step:]
     for copy in copies:
         copy.wait()
 
@@ -409,23 +395,28 @@
 
     acc0, acc1, halo_w, w_in_v, w_out_v, weight_v = pl.pallas_call(
         functools.partial(prepare_kernel, spaces=spaces),
-        in_specs=[smem(), smem(), hbm(), hbm(), hbm(), vmem()],
+        in_specs=[hbm()] * 5 + [vmem()],
         out_specs=[vmem()] * 6,
         out_shape=[
             held((n, feature), f32),
             held((n, feature), f32),
-            held((n, rim_rows), bf16),
+            held((n, rim_rows + nodes), bf16),
             held((hidden, feature), bf16),
             held((rows_v, hidden), bf16),
             held(edge_weight.shape, bf16),
         ],
         scratch_shapes=[
+            pltpu.SMEM(ids.shape, jnp.int32),
+            pltpu.SMEM(block_count.shape, jnp.int32),
             pltpu.VMEM(lat.shape, bf16),
-            pltpu.SemaphoreType.DMA((4,)),
+            pltpu.SemaphoreType.DMA((6,)),
         ],
         compiler_params=params(12),
         cost_estimate=cost(2000),
-    )(ids, block_count, in_hbm(lat), in_hbm(edge_weight), in_hbm(w_in), in_hbm(w_out))
+    )(
+        in_hbm(ids), in_hbm(block_count), in_hbm(lat), in_hbm(edge_weight), in_hbm(w_in),
+        in_hbm(w_out),
+    )
 
     def along(x, distance):
         return lax.ppermute(x, "member", ring(chips, distance))
@@ -462,17 +453,17 @@
     far0 = along(left0, 1)
     second_lat, _ = lax.optimization_barrier((lat1, slope0))
     act1, slope1 = slopes_of(second_lat)
-    held_right1, _ = lax.optimization_barrier((right1, slope1))
+    held_right1, _ = lax.optimization_barrier((right1, slope0))
     far1 = along(held_right1, -1)
     grid_latent, acts, slopes = [lat0, lat1], [act0, act1], [slope0, slope1]
 
-    halo_wt, own_wt, w_in_t, w_out_t, target, scale_v = pl.pallas_call(
-        functools.partial(turn_kernel, spaces=spaces),
+    own_rows = blocks * nodes
+    turned, w_in_t, w_out_t, target, scale_v = pl.pallas_call(
+        functools.partial(turn_kernel, spaces=spaces, blocks=blocks),
         in_specs=[smem(), smem()] + [vmem()] * 5 + [anywhere()],
-        out_specs=[vmem()] * 6,
+        out_specs=[vmem()] * 5,
         out_shape=[
-            held((rim_rows, n), bf16),
-            held((blocks * nodes, n), bf16),
+            held((own_rows + rim_rows + nodes, n), bf16),
             held((feature, hidden), bf16),
             held((hidden, rows_v), bf16),
             held((rows_v, n), bf16),
@@ -522,34 +513,35 @@
     swapped = lax.ppermute(send, "dp", [(0, 1), (1, 0)])
 
     grad_grid0, grad_grid1, rim_near, rim_far = pl.pallas_call(
-        rim_kernel,
+        functools.partial(rim_kernel, own_rows=own_rows),
         in_specs=[vmem()] * 4,
         out_specs=[vmem()] * 4,
         out_shape=[held((feature, n), bf16)] * 2 + [shape((members, edge_rows, feature), bf16)] * 2,
         compiler_params=params(8),
         cost_estimate=cost(2000),
-    )(*in_vmem(grad_pre0, grad_pre1, halo_wt, w_in_t))
+    )(*in_vmem(grad_pre0, grad_pre1, turned, w_in_t))
 
     quarter = half_rows // chips
-    middle = blocks // HALO - 2
+    pieces = 3
+    size = (own_rows - 2 * edge_rows) // pieces
 
     def owned_of(member, grad_grid, base):
         whole = shape((members, blocks * nodes, feature), f32)
         aliased = {} if base is None else {2: 0}
         base = grad_grid if base is None else base
         return pl.pallas_call(
-            functools.partial(owned_kernel, member=member),
+            functools.partial(owned_kernel, member=member, own_rows=own_rows),
             in_specs=[vmem()] * 2 + [anywhere()],
             out_specs=[hbm(), vmem()],
             out_shape=[whole, held((2, edge_rows, feature), f32)],
             scratch_shapes=[
-                pltpu.VMEM((middle, edge_rows, feature), f32),
-                pltpu.SemaphoreType.DMA((middle,)),
+                pltpu.VMEM((pieces, size, feature), f32),
+                pltpu.SemaphoreType.DMA((pieces,)),
             ],
             input_output_aliases=aliased,
             compiler_params=params(8),
             cost_estimate=cost(2000),
-        )(*in_vmem(grad_grid, own_wt), base)
+        )(*in_vmem(grad_grid, turned), base)
 
     swapped, _ = lax.optimization_barrier((swapped, grad_grid0))
     kept, send = halve(keep, swapped, 2)

time: 73.8 us -> 72.1 us (0.977)
  Pallas kernels: 30 us -> 28 us
    pallas_call x4, Pallas kernels: 11.6 us -> 9.55 us  [the longest x2 5.65 us: owned_of(): pl.pallas_call(functools.partial(owned_kernel, member=member, own_rows=ow...]
  transfers between devices with their start and end apart: 15 -> 15, of which waited for: 4 -> 4; matrix products, arithmetic and copies ran while one was open for 0% -> 0% of each run, Pallas kernels for 33% -> 31%
where the time goes in v6:
time: 72.1 us; the launch traced here: 71.9 us
  Pallas kernels  28 us (39%)
  starting transfers between devices  24.2 us (34%)
  blocking collectives  12.5 us (17%)
  waiting for transfers between devices  6.25 us (9%)
  between operations  1.02 us (1%)
    all_to_all x1, blocking collectives, local(): spread = lax.all_to_all(spread, 'space', 0, 0, tiled=True)  12.5 us
    ppermute x6, starting transfers between devices, along(): return lax.ppermute(x, 'member', ring(chips, distance))  9.62 us
    ppermute x2, starting transfers between devices, local(): near = lax.ppermute(edges[2 * m], 'space', first)  7.16 us
    pallas_call x2, Pallas kernels, owned_of(): pl.pallas_call(functools.partial(owned_kernel, member=member, own_rows=ow...  5.65 us
    pallas_call x1, Pallas kernels, local(): pl.pallas_call(functools.partial(prepare_kernel, spaces=spaces), in_specs...  4.32 us
    pallas_call x2, Pallas kernels, fields_of(): pl.pallas_call(fields_kernel, in_specs=[vmem()] * 6, out_specs=[vmem()] *...  3.89 us
    ppermute x1, starting transfers between devices, local(): got_near = lax.ppermute(rim_near, 'space', first)  3.22 us
    pallas_call x2, Pallas kernels, slopes_of(): pl.pallas_call(slopes_kernel, in_specs=[vmem()] * 2, out_specs=[vmem()] *...  3.02 us
  transfers between devices with their start and end apart: 15, of which 4 were waited for; matrix products, arithmetic and copies ran while one was open for 0% of the time, Pallas kernels for 31%

profile of v6, /device:TPU:0, one launch (start us, length us, event | category | flops | bytes accessed | tf_op | source)
XLA Modules:
  0.0 71.9 jit_solution(9856691036469870421)
XLA Ops:
  0.6 1.2 %shard_map.113 = (bf16[256,512]{1,0:T(8,128)(2,1)S(1)}, bf16[256,512]{1,0:T(8,128)(2,1)S(1)}, bf16[256,512]{1,0:T(8,128)(2,1)S(1)}, bf16[256,512]{1,0:T(8,128)(2,1)S(1)}) custom-call(bf16[2,2048,512]{2,1,0:T(8,128)(2,1)} %bitcast.14), custom_call_target="tpu_custom_call" | custom-call | tf_op jit(solution)/shard_map/pallas_call | solution.py:380
  1.9 6.7 %collective-permute-start = (bf16[256,512]{1,0:T(8,128)(2,1)S(1)}, bf16[256,512]{1,0:T(8,128)(2,1)S(1)}, u32[]{:S(2)}, u32[]{:S(2)}) collective-permute-start(bf16[256,512]{1,0:T(8,128)(2,1)S(1)} %get-tuple-element.60), channel_id=1, source_target_pairs={{0,15},{1,2},{2,1},{3,4},{4,3},{5,6},{6,5},{7,8},{8,7},{9,10},{10,... | collective-permute-start | bytes 786440 | tf_op jit(solution)/shard_map/ppermute | solution.py:391
  8.5 0.0 collective-permute-start.1
  8.5 0.5 collective-permute-start.2
  9.0 1.5 %collective-permute-start.3 = (bf16[256,512]{1,0:T(8,128)(2,1)S(1)}, bf16[256,512]{1,0:T(8,128)(2,1)S(1)}, u32[]{:S(2)}, u32[]{:S(2)}) collective-permute-start(bf16[256,512]{1,0:T(8,128)(2,1)S(1)} %get-tuple-element.68), channel_id=1, source_target_pairs={{0,1},{1,0},{2,3},{3,2},{4,5},{5,4},{6,7},{7,6},{8,9},{9,8},{10,11... | collective-permute-start | bytes 786440 | tf_op jit(solution)/shard_map/ppermute | solution.py:390
  10.6 4.3 %shard_map.112 = (f32[1024,512]{1,0:T(8,128)S(1)}, f32[1024,512]{1,0:T(8,128)S(1)}, bf16[1024,640]{1,0:T(8,128)(2,1)S(1)}, bf16[512,512]{1,0:T(8,128)(2,1)S(1)},...) custom-call(s32[4,8]{1,0:T(4,128)} %bitcast.10, s32[8]{0:T(128)} %count.1, ...), custom_call_target="tpu_custom_call" | custom-call | flops 2000000000 | bytes 8000000 | tf_op jit(solution)/shard_map/pallas_call | solution.py:396
  14.9 0.8 %collective-permute-done.near = bf16[256,512]{1,0:T(8,128)(2,1)S(1)} collective-permute-done((bf16[256,512]{1,0:T(8,128)(2,1)S(1)}, bf16[256,512]{1,0:T(8,128)(2,1)S(1)}, u32[]{:S(2)}, u32[]{:S(2)}) %collective-permute-start) | collective-permute-done | bytes 262176 | tf_op jit(solution)/shard_map/ppermute | solution.py:391
  15.7 2.1 %collective-permute-done.1.far = bf16[256,512]{1,0:T(8,128)(2,1)S(1)} collective-permute-done((bf16[256,512]{1,0:T(8,128)(2,1)S(1)}, bf16[256,512]{1,0:T(8,128)(2,1)S(1)}, u32[]{:S(2)}, u32[]{:S(2)}) %collective-permute-start.1) | collective-permute-done | bytes 262176 | tf_op jit(solution)/shard_map/ppermute | solution.py:390
  17.8 0.0 copy-start
  17.8 0.0 copy-start.2
  17.8 0.0 copy-start.3
  17.8 0.0 copy-start.4
  17.8 1.9 %shard_map.114 = (bf16[1024,512]{1,0:T(8,128)(2,1)S(1)}, bf16[88,1024]{1,0:T(8,128)(2,1)S(1)}) custom-call(f32[1024,512]{1,0:T(8,128)S(1)} %get-tuple-element.59.acc, bf16[256,512]{1,0:T(8,128)(2,1)S(1)} %collective-permute-done.near, bf16[256,512]{1,0:T(8,128)(2,1)S(1)} %collective-permute-done.1.far, bf16[1024,640]{1,0:T(8,128)(2,1)S(1)} %get-tuple-element.62.halo_w, ...), custom_call_target="tpu_custom_call" | custom-call | flops 100000000 | bytes 400000 | tf_op jit(solution)/shard_map/pallas_call | solution.py:425
  19.7 2.8 %collective-permute-start.6 = (bf16[88,1024]{1,0:T(8,128)(2,1)S(1)}, bf16[88,1024]{1,0:T(8,128)(2,1)S(1)}, u32[]{:S(2)}, u32[]{:S(2)}) collective-permute-start(bf16[88,1024]{1,0:T(8,128)(2,1)S(1)} %get-tuple-element.65.own0), channel_id=1, source_target_pairs={{0,48},{16,0},{32,16},{48,32},{1,49},{17,1},{33,17},{49,33},{2,50}... | collective-permute-start | bytes 540680 | tf_op jit(solution)/shard_map/ppermute | solution.py:422
  22.5 0.0 collective-permute-start.5
  22.5 0.0 collective-permute-done.2.near
  22.6 0.0 collective-permute-done.3.far
  22.6 0.0 copy-start.1
  22.6 1.9 %shard_map.115 = (bf16[1024,512]{1,0:T(8,128)(2,1)S(1)}, bf16[88,1024]{1,0:T(8,128)(2,1)S(1)}) custom-call(f32[1024,512]{1,0:T(8,128)S(1)} %get-tuple-element.66.acc, bf16[256,512]{1,0:T(8,128)(2,1)S(1)} %collective-permute-done.2.near, bf16[256,512]{1,0:T(8,128)(2,1)S(1)} %collective-permute-done.3.far, bf16[1024,640]{1,0:T(8,128)(2,1)S(1)} %get-tuple-element.62.halo_w, ...), custom_call_target="tpu_custom_call" | custom-call | flops 100000000 | bytes 400000 | tf_op jit(solution)/shard_map/pallas_call | solution.py:425
  24.5 3.3 %collective-permute-start.4 = (bf16[88,1024]{1,0:T(8,128)(2,1)S(1)}, bf16[88,1024]{1,0:T(8,128)(2,1)S(1)}, u32[]{:S(2)}, u32[]{:S(2)}) collective-permute-start(bf16[88,1024]{1,0:T(8,128)(2,1)S(1)} %get-tuple-element.69.own1), channel_id=1, source_target_pairs={{0,48},{16,0},{32,16},{48,32},{1,49},{17,1},{33,17},{49,33},{2,50}... | collective-permute-start | bytes 540680 | tf_op jit(solution)/shard_map/ppermute | solution.py:422
  27.8 0.0 collective-permute-start.8
  27.8 0.0 collective-permute-done.6.o20
  27.8 1.8 %collective-permute-done.5.o10 = bf16[88,1024]{1,0:T(8,128)(2,1)S(1)} collective-permute-done((bf16[88,1024]{1,0:T(8,128)(2,1)S(1)}, bf16[88,1024]{1,0:T(8,128)(2,1)S(1)}, u32[]{:S(2)}, u32[]{:S(2)}) %collective-permute-start.5) | collective-permute-done | bytes 180256 | tf_op jit(solution)/shard_map/ppermute | solution.py:422
  29.6 0.0 collective-permute-start.9
  29.6 1.5 %shard_map.116 = (bf16[512,1024]{1,0:T(8,128)(2,1)S(1)}, bf16[512,1024]{1,0:T(8,128)(2,1)S(1)}) custom-call(bf16[1024,512]{1,0:T(8,128)(2,1)S(1)} %get-tuple-element.71.lat.lat0, bf16[512,512]{1,0:T(8,128)(2,1)S(1)} %get-tuple-element.63.w_in), custom_call_target="tpu_custom_call" | custom-call | flops 100000000 | bytes 400000 | tf_op jit(solution)/shard_map/pallas_call | solution.py:435
  31.1 0.0 collective-permute-done.4.o21
  31.1 3.5 %collective-permute-start.7 = (bf16[88,1024]{1,0:T(8,128)(2,1)S(1)}, bf16[88,1024]{1,0:T(8,128)(2,1)S(1)}, u32[]{:S(2)}, u32[]{:S(2)}) collective-permute-start(bf16[88,1024]{1,0:T(8,128)(2,1)S(1)} %collective-permute-done.4.o21), channel_id=1, source_target_pairs={{0,48},{16,0},{32,16},{48,32},{1,49},{17,1},{33,17},{49,33},{2,50}... | collective-permute-start | bytes 540680 | tf_op jit(solution)/shard_map/ppermute | solution.py:422
  34.6 1.5 %shard_map.117 = (bf16[512,1024]{1,0:T(8,128)(2,1)S(1)}, bf16[512,1024]{1,0:T(8,128)(2,1)S(1)}) custom-call(bf16[1024,512]{1,0:T(8,128)(2,1)S(1)} %get-tuple-element.78.lat.lat1, bf16[512,512]{1,0:T(8,128)(2,1)S(1)} %get-tuple-element.63.w_in), custom_call_target="tpu_custom_call" | custom-call | flops 100000000 | bytes 400000 | tf_op jit(solution)/shard_map/pallas_call | solution.py:435
  36.1 0.0 copy-done
  36.1 0.0 copy-done.2
  36.1 0.0 copy-done.3
  36.1 0.0 copy-done.4
  36.2 1.6 %shard_map.118 = (bf16[2688,1024]{1,0:T(8,128)(2,1)S(1)}, bf16[512,512]{1,0:T(8,128)(2,1)S(1)}, bf16[512,88]{1,0:T(8,128)(2,1)S(1)}, bf16[88,1024]{1,0:T(8,128)(2,1)S(1)}, f32[88,1]{1,0:T(8,128)S(1)}) custom-call(s32[4,8]{1,0:T(4,128)S(1)} %bitcast.11, s32[8]{0:T(128)S(1)} %copy-done.3, bf16[8,4,128,128]{3,2,1,0:T(8,128)(2,1)S(1)} %get-tuple-element.76.weight, ...), custom_call_target="tpu_custom_call" | custom-call | flops 100000000 | bytes 400000 | tf_op jit(solution)/shard_map/pallas_call | solution.py:461
  37.7 0.0 collective-permute-done.8.o11
  37.7 0.0 collective-permute-done.9.far0
  37.7 1.1 %shard_map.119 = (f32[88,1024]{1,0:T(8,128)S(1)}, f32[88,1024]{1,0:T(8,128)S(1)}) custom-call(bf16[88,1024]{1,0:T(8,128)(2,1)S(1)} %get-tuple-element.65.own0, bf16[88,1024]{1,0:T(8,128)(2,1)S(1)} %get-tuple-element.69.own1, bf16[88,1024]{1,0:T(8,128)(2,1)S(1)} %collective-permute-done.5.o10, bf16[88,1024]{1,0:T(8,128)(2,1)S(1)} %collective-permute-done.8.o11, ...), custom_call_target="tpu_custom_call" | custom-call | flops 100000000 | bytes 400000 | tf_op jit(solution)/shard_map/pallas_call | solution.py:480
  38.9 0.0 collective-permute-done.7.far1
  38.9 0.0 copy-done.1
  38.9 2.7 %shard_map.120 = (bf16[512,1024]{1,0:T(8,128)(2,1)S(1)}, bf16[512,1024]{1,0:T(8,128)(2,1)S(1)}, f32[256,640]{1,0:T(8,128)S(1)}, bf16[256,640]{1,0:T(8,128)(2,1)S(1)}) custom-call(bf16[88,1024]{1,0:T(8,128)(2,1)S(1)} %get-tuple-element.65.own0, bf16[88,1024]{1,0:T(8,128)(2,1)S(1)} %get-tuple-element.69.own1, ...), custom_call_target="tpu_custom_call" | custom-call | flops 2000000000 | bytes 8000000 | tf_op jit(solution)/shard_map/pallas_call | solution.py:491
  41.5 0.1 collective-permute-start.10
  41.6 2.3 %shard_map.121 = (bf16[512,1024]{1,0:T(8,128)(2,1)S(1)}, bf16[512,1024]{1,0:T(8,128)(2,1)S(1)}, bf16[2,256,512]{2,1,0:T(8,128)(2,1)S(1)}, bf16[2,256,512]{2,1,0:T(8,128)(2,1)S(1)}) custom-call(bf16[512,1024]{1,0:T(8,128)(2,1)S(1)} %get-tuple-element.87.grad_pre0, bf16[512,1024]{1,0:T(8,128)(2,1)S(1)} %get-tuple-element.88.grad_pre1, ...), custom_call_target="tpu_custom_call" | custom-call | flops 2000000000 | bytes 8000000 | tf_op jit(solution)/shard_map/pallas_call | solution.py:515
  44.0 0.0 collective-permute-done.10.got
  44.0 0.1 shard_map.122
  44.1 2.5 %collective-permute-start.11 = (bf16[128,640]{1,0:T(8,128)(2,1)S(1)}, bf16[128,640]{1,0:T(8,128)(2,1)S(1)}, u32[]{:S(2)}, u32[]{:S(2)}) collective-permute-start(bf16[128,640]{1,0:T(8,128)(2,1)S(1)} %get-tuple-element.97), channel_id=1, source_target_pairs={{0,48},{16,32},{32,16},{48,0},{1,49},{17,33},{33,17},{49,1},{2,50}... | collective-permute-start | bytes 491528 | tf_op jit(solution)/shard_map/ppermute | solution.py:548
  46.6 3.2 %collective-permute-start.12 = (bf16[2,256,512]{2,1,0:T(8,128)(2,1)S(1)}, bf16[2,256,512]{2,1,0:T(8,128)(2,1)S(1)}, u32[]{:S(2)}, u32[]{:S(2)}) collective-permute-start(bf16[2,256,512]{2,1,0:T(8,128)(2,1)S(1)} %get-tuple-element.108), channel_id=1, source_target_pairs={{0,15},{1,2},{2,1},{3,4},{4,3},{5,6},{6,5},{7,8},{8,7},{9,10},{10,... | collective-permute-start | bytes 1572872 | tf_op jit(solution)/shard_map/ppermute | solution.py:553
  49.9 0.0 collective-permute-start.13
  49.9 2.8 %shard_map.123 = (f32[2,2048,512]{2,1,0:T(8,128)}, f32[2,256,512]{2,1,0:T(8,128)S(1)}) custom-call(bf16[512,1024]{1,0:T(8,128)(2,1)S(1)} %get-tuple-element.100.grad_grid.base, bf16[2688,1024]{1,0:T(8,128)(2,1)S(1)} %get-tuple-element.89.turned, bf16[512,1024]{1,0:T(8,128)(2,1)S(1)} %get-tuple-element.100.grad_grid.base), custom_call_target="tpu_custom_call" | custom-call | flops 2000000000 | bytes 8000000 | tf_op jit(solution)/shard_map/pallas_call | solution.py:532
  52.7 0.0 collective-permute-done.11.got
  52.7 0.1 shard_map.124
  52.8 0.1 collective-permute-start.14
  52.9 2.8 %shard_map.125 = (f32[2,2048,512]{2,1,0:T(8,128)}, f32[2,256,512]{2,1,0:T(8,128)S(1)}) custom-call(bf16[512,1024]{1,0:T(8,128)(2,1)S(1)} %get-tuple-element.104.grad_grid, bf16[2688,1024]{1,0:T(8,128)(2,1)S(1)} %get-tuple-element.89.turned, f32[2,2048,512]{2,1,0:T(8,128)} %get-tuple-element.105.base), custom_call_target="tpu_custom_call", output_to_operand_aliasing={{0}: (2, {})} | custom-call | flops 2000000000 | bytes 8000000 | tf_op jit(solution)/shard_map/pallas_call | solution.py:532
  55.7 1.6 %collective-permute-done.14.got = bf16[64,640]{1,0:T(8,128)(2,1)S(1)} collective-permute-done((bf16[64,640]{1,0:T(8,128)(2,1)S(1)}, bf16[64,640]{1,0:T(8,128)(2,1)S(1)}, u32[]{:S(2)}, u32[]{:S(2)}) %collective-permute-start.14) | collective-permute-done | bytes 81952 | tf_op jit(solution)/shard_map/ppermute | solution.py:557
  57.3 12.5 %all_to_all.5.got = bf16[16,4,640]{2,1,0:T(4,128)(2,1)S(1)} all-to-all(bf16[16,4,640]{2,1,0:T(4,128)(2,1)S(1)} %shard_map.126), channel_id=1, replica_groups=mesh['dp'=2,'member'=4,'space'=16] {'space'}, dimensions={0} | all-to-all | bytes 163840 | tf_op jit(solution)/shard_map/all_to_all | solution.py:570
  69.8 0.0 collective-permute-done.12.near
  69.8 0.0 collective-permute-done.13.far
  69.8 2.0 %shard_map.127 = (f32[2,2048,512]{2,1,0:T(8,128)}, f32[4,512]{1,0:T(4,128)}, f32[4,83]{1,0:T(4,128)}) custom-call(f32[2,2048,512]{2,1,0:T(8,128)} %get-tuple-element.106.base, f32[2,256,512]{2,1,0:T(8,128)S(1)} %get-tuple-element.101.edge0, f32[2,256,512]{2,1,0:T(8,128)S(1)} %get-tuple-element.107.edge1, ...), custom_call_target="tpu_custom_call", output_to_operand_aliasing={{0}: (0, {})} | custom-call | tf_op jit(solution)/shard_map/pallas_call | solution.py:571
  (1 shorter events, 0.0 us)
Async XLA Ops:
  1.9 13.8 %collective-permute-start = (bf16[256,512]{1,0:T(8,128)(2,1)S(1)}, bf16[256,512]{1,0:T(8,128)(2,1)S(1)}, u32[]{:S(2)}, u32[]{:S(2)}) collective-permute-start(bf16[256,512]{1,0:T(8,128)(2,1)S(1)} %get-tuple-element.60), channel_id=1, source_target_pairs={{0,15},{1,2},{2,1},{3,4},{4,3},{5,6},{6,5},{7,8},{8,7},{9,10},{10,... | collective-permute-start | bytes 786440 | tf_op jit(solution)/shard_map/ppermute | solution.py:391
  8.5 9.2 %collective-permute-start.1 = (bf16[256,512]{1,0:T(8,128)(2,1)S(1)}, bf16[256,512]{1,0:T(8,128)(2,1)S(1)}, u32[]{:S(2)}, u32[]{:S(2)}) collective-permute-start(bf16[256,512]{1,0:T(8,128)(2,1)S(1)} %get-tuple-element.61), channel_id=1, source_target_pairs={{0,1},{1,0},{2,3},{3,2},{4,5},{5,4},{6,7},{7,6},{8,9},{9,8},{10,11... | collective-permute-start | bytes 786440 | tf_op jit(solution)/shard_map/ppermute | solution.py:390
  8.5 14.0 %collective-permute-start.2 = (bf16[256,512]{1,0:T(8,128)(2,1)S(1)}, bf16[256,512]{1,0:T(8,128)(2,1)S(1)}, u32[]{:S(2)}, u32[]{:S(2)}) collective-permute-start(bf16[256,512]{1,0:T(8,128)(2,1)S(1)} %get-tuple-element.67), channel_id=1, source_target_pairs={{0,15},{1,2},{2,1},{3,4},{4,3},{5,6},{6,5},{7,8},{8,7},{9,10},{10,... | collective-permute-start | bytes 786440 | tf_op jit(solution)/shard_map/ppermute | solution.py:391
  9.0 13.5 %collective-permute-start.3 = (bf16[256,512]{1,0:T(8,128)(2,1)S(1)}, bf16[256,512]{1,0:T(8,128)(2,1)S(1)}, u32[]{:S(2)}, u32[]{:S(2)}) collective-permute-start(bf16[256,512]{1,0:T(8,128)(2,1)S(1)} %get-tuple-element.68), channel_id=1, source_target_pairs={{0,1},{1,0},{2,3},{3,2},{4,5},{5,4},{6,7},{7,6},{8,9},{9,8},{10,11... | collective-permute-start | bytes 786440 | tf_op jit(solution)/shard_map/ppermute | solution.py:390
  17.8 18.4 %copy-start = (bf16[1,83,1024]{2,1,0:T(8,128)(2,1)S(1)}, bf16[1,83,1024]{2,1,0:T(8,128)(2,1)}, u32[]{:S(2)}) copy-start(bf16[1,83,1024]{2,1,0:T(8,128)(2,1)} %param.15) | copy-start | bytes 509956
  17.8 18.4 %copy-start.2 = (s32[8,4]{0,1:T(4,128)S(1)}, s32[8,4]{0,1:T(4,128)}, u32[]{:S(2)}) copy-start(s32[8,4]{0,1:T(4,128)} %param.11) | copy-start | bytes 388
  17.8 18.4 %copy-start.3 = (s32[8]{0:T(128)S(1)}, s32[8]{0:T(128)}, u32[]{:S(2)}) copy-start(s32[8]{0:T(128)} %count.1) | copy-start | bytes 100
  17.8 18.4 %copy-start.4 = (f32[83]{0:T(128)S(1)}, f32[83]{0:T(128)}, u32[]{:S(2)}) copy-start(f32[83]{0:T(128)} %param.17) | copy-start | bytes 1000
  19.7 8.1 %collective-permute-start.6 = (bf16[88,1024]{1,0:T(8,128)(2,1)S(1)}, bf16[88,1024]{1,0:T(8,128)(2,1)S(1)}, u32[]{:S(2)}, u32[]{:S(2)}) collective-permute-start(bf16[88,1024]{1,0:T(8,128)(2,1)S(1)} %get-tuple-element.65.own0), channel_id=1, source_target_pairs={{0,48},{16,0},{32,16},{48,32},{1,49},{17,1},{33,17},{49,33},{2,50}... | collective-permute-start | bytes 540680 | tf_op jit(solution)/shard_map/ppermute | solution.py:422
  22.5 7.0 %collective-permute-start.5 = (bf16[88,1024]{1,0:T(8,128)(2,1)S(1)}, bf16[88,1024]{1,0:T(8,128)(2,1)S(1)}, u32[]{:S(2)}, u32[]{:S(2)}) collective-permute-start(bf16[88,1024]{1,0:T(8,128)(2,1)S(1)} %get-tuple-element.65.own0), channel_id=1, source_target_pairs={{0,16},{16,32},{32,48},{48,0},{1,17},{17,33},{33,49},{49,1},{2,18}... | collective-permute-start | bytes 540680 | tf_op jit(solution)/shard_map/ppermute | solution.py:422
  22.6 16.3 %copy-start.1 = (f32[1024]{0:T(1024)S(1)}, f32[1024]{0:T(1024)}, u32[]{:S(2)}) copy-start(f32[1024]{0:T(1024)} %param.16) | copy-start | bytes 12292
  24.5 6.6 %collective-permute-start.4 = (bf16[88,1024]{1,0:T(8,128)(2,1)S(1)}, bf16[88,1024]{1,0:T(8,128)(2,1)S(1)}, u32[]{:S(2)}, u32[]{:S(2)}) collective-permute-start(bf16[88,1024]{1,0:T(8,128)(2,1)S(1)} %get-tuple-element.69.own1), channel_id=1, source_target_pairs={{0,48},{16,0},{32,16},{48,32},{1,49},{17,1},{33,17},{49,33},{2,50}... | collective-permute-start | bytes 540680 | tf_op jit(solution)/shard_map/ppermute | solution.py:422
  27.8 9.9 %collective-permute-start.8 = (bf16[88,1024]{1,0:T(8,128)(2,1)S(1)}, bf16[88,1024]{1,0:T(8,128)(2,1)S(1)}, u32[]{:S(2)}, u32[]{:S(2)}) collective-permute-start(bf16[88,1024]{1,0:T(8,128)(2,1)S(1)} %get-tuple-element.69.own1), channel_id=1, source_target_pairs={{0,16},{16,32},{32,48},{48,0},{1,17},{17,33},{33,49},{49,1},{2,18}... | collective-permute-start | bytes 540680 | tf_op jit(solution)/shard_map/ppermute | solution.py:422
  29.6 8.1 %collective-permute-start.9 = (bf16[88,1024]{1,0:T(8,128)(2,1)S(1)}, bf16[88,1024]{1,0:T(8,128)(2,1)S(1)}, u32[]{:S(2)}, u32[]{:S(2)}) collective-permute-start(bf16[88,1024]{1,0:T(8,128)(2,1)S(1)} %collective-permute-done.5.o10), channel_id=1, source_target_pairs={{0,16},{16,32},{32,48},{48,0},{1,17},{17,33},{33,49},{49,1},{2,18}... | collective-permute-start | bytes 540680 | tf_op jit(solution)/shard_map/ppermute | solution.py:422
  31.1 7.8 %collective-permute-start.7 = (bf16[88,1024]{1,0:T(8,128)(2,1)S(1)}, bf16[88,1024]{1,0:T(8,128)(2,1)S(1)}, u32[]{:S(2)}, u32[]{:S(2)}) collective-permute-start(bf16[88,1024]{1,0:T(8,128)(2,1)S(1)} %collective-permute-done.4.o21), channel_id=1, source_target_pairs={{0,48},{16,0},{32,16},{48,32},{1,49},{17,1},{33,17},{49,33},{2,50}... | collective-permute-start | bytes 540680 | tf_op jit(solution)/shard_map/ppermute | solution.py:422
  41.5 2.4 %collective-permute-start.10 = (bf16[256,640]{1,0:T(8,128)(2,1)S(1)}, bf16[256,640]{1,0:T(8,128)(2,1)S(1)}, u32[]{:S(2)}, u32[]{:S(2)}) collective-permute-start(bf16[256,640]{1,0:T(8,128)(2,1)S(1)} %get-tuple-element.93), channel_id=1, source_target_pairs={{0,64},{64,0},{1,65},{65,1},{2,66},{66,2},{3,67},{67,3},{4,68},{68... | collective-permute-start | bytes 983048 | tf_op jit(solution)/shard_map/ppermute | solution.py:513
  44.1 8.6 %collective-permute-start.11 = (bf16[128,640]{1,0:T(8,128)(2,1)S(1)}, bf16[128,640]{1,0:T(8,128)(2,1)S(1)}, u32[]{:S(2)}, u32[]{:S(2)}) collective-permute-start(bf16[128,640]{1,0:T(8,128)(2,1)S(1)} %get-tuple-element.97), channel_id=1, source_target_pairs={{0,48},{16,32},{32,16},{48,0},{1,49},{17,33},{33,17},{49,1},{2,50}... | collective-permute-start | bytes 491528 | tf_op jit(solution)/shard_map/ppermute | solution.py:548
  46.6 23.1 %collective-permute-start.12 = (bf16[2,256,512]{2,1,0:T(8,128)(2,1)S(1)}, bf16[2,256,512]{2,1,0:T(8,128)(2,1)S(1)}, u32[]{:S(2)}, u32[]{:S(2)}) collective-permute-start(bf16[2,256,512]{2,1,0:T(8,128)(2,1)S(1)} %get-tuple-element.108), channel_id=1, source_target_pairs={{0,15},{1,2},{2,1},{3,4},{4,3},{5,6},{6,5},{7,8},{8,7},{9,10},{10,... | collective-permute-start | bytes 1572872 | tf_op jit(solution)/shard_map/ppermute | solution.py:553
  49.9 19.9 %collective-permute-start.13 = (bf16[2,256,512]{2,1,0:T(8,128)(2,1)S(1)}, bf16[2,256,512]{2,1,0:T(8,128)(2,1)S(1)}, u32[]{:S(2)}, u32[]{:S(2)}) collective-permute-start(bf16[2,256,512]{2,1,0:T(8,128)(2,1)S(1)} %get-tuple-element.109), channel_id=1, source_target_pairs={{0,1},{1,0},{2,3},{3,2},{4,5},{5,4},{6,7},{7,6},{8,9},{9,8},{10,11... | collective-permute-start | bytes 1572872 | tf_op jit(solution)/shard_map/ppermute | solution.py:552
  52.8 4.5 %collective-permute-start.14 = (bf16[64,640]{1,0:T(8,128)(2,1)S(1)}, bf16[64,640]{1,0:T(8,128)(2,1)S(1)}, u32[]{:S(2)}, u32[]{:S(2)}) collective-permute-start(bf16[64,640]{1,0:T(8,128)(2,1)S(1)} %get-tuple-element.103), channel_id=1, source_target_pairs={{0,16},{16,0},{32,48},{48,32},{1,17},{17,1},{33,49},{49,33},{2,18}... | collective-permute-start | bytes 245768 | tf_op jit(solution)/shard_map/ppermute | solution.py:557

commit v7 on v6

--- a/solution.py
+++ b/solution.py
@@ -181,8 +181,8 @@
 def fields_kernel(acc, near, far, halo_w, w_in, w_out, lat_out, fields):
     count = acc.shape[0]
     half_k = near.shape[0]
-    for start in range(0, count, 2 * CHUNK):
-        at = slice(start, start + 2 * CHUNK)
+    for start in range(0, count, 4 * CHUNK):
+        at = slice(start, start + 4 * CHUNK)
         total = acc[at] + dot(halo_w[at, :half_k], near[...])
         total = total + dot(halo_w[at, half_k : 2 * half_k], far[...])
         rounded = total.astype(bf16)
@@ -272,13 +272,13 @@
     grad_pre0, grad_pre1, turned, w_in_t, grad_grid0, grad_grid1, near, far, *, own_rows,
 ):
     half_k = near.shape[1]
-    middle = own_rows + half_k
     for m, (grad_pre, grad_grid) in enumerate(
         ((grad_pre0, grad_grid0), (grad_pre1, grad_grid1))
     ):
         grad_grid[...] = dot(w_in_t[...], grad_pre[...]).astype(bf16)
-        near[m] = dot(turned[own_rows:middle], grad_grid[...], NT).astype(bf16)
-        far[m] = dot(turned[middle : middle + half_k], grad_grid[...], NT).astype(bf16)
+        rims = dot(turned[own_rows : own_rows + 2 * half_k], grad_grid[...], NT).astype(bf16)
+        near[m] = rims[:half_k]
+        far[m] = rims[half_k:]
 
 
 def owned_kernel(grad_grid, turned, base, out, edge, parts, sems, *, member, own_rows):
@@ -301,7 +301,7 @@
 
 
 def finish_kernel(
-    base, edge0, edge1, near, far, got, out, grad_in, grad_out, parts, sems,
+    base, edge0, edge1, far, near, got, out, grad_in, grad_out, parts, sems,
 ):
     step = edge0.shape[1]
     last = out.shape[1] - step
@@ -583,7 +583,7 @@
         ],
         input_output_aliases={0: 0},
         compiler_params=params(8),
-    )(owned, *in_vmem(edge0, edge1), got_near, got_far, spread)
+    )(owned, *in_vmem(edge0, edge1), got_far, got_near, spread)
     return grad_latent[None], grad_w_in, grad_w_out.T
 
 

time: 72.1 us -> 70.5 us (0.978)
  blocking collectives: 12.5 us -> 11.4 us
    all_to_all x1, blocking collectives: 12.5 us -> 11.4 us  [local(): spread = lax.all_to_all(spread, 'space', 0, 0, tiled=True)]
  transfers between devices with their start and end apart: 15 -> 15, of which waited for: 4 -> 4; matrix products, arithmetic and copies ran while one was open for 0% -> 0% of each run, Pallas kernels for 31% -> 30%
where the time goes in v7:
time: 70.5 us; the launch traced here: 70.3 us
  Pallas kernels  27.4 us (39%)
  starting transfers between devices  23.9 us (34%)
  blocking collectives  11.4 us (16%)
  waiting for transfers between devices  6.56 us (9%)
  between operations  1.02 us (1%)
    all_to_all x1, blocking collectives, local(): spread = lax.all_to_all(spread, 'space', 0, 0, tiled=True)  11.4 us
    ppermute x6, starting transfers between devices, along(): return lax.ppermute(x, 'member', ring(chips, distance))  9.6 us
    ppermute x2, starting transfers between devices, local(): near = lax.ppermute(edges[2 * m], 'space', first)  7.16 us
    pallas_call x2, Pallas kernels, owned_of(): pl.pallas_call(functools.partial(owned_kernel, member=member, own_rows=ow...  5.65 us
    pallas_call x1, Pallas kernels, local(): pl.pallas_call(functools.partial(prepare_kernel, spaces=spaces), in_specs...  4.32 us
    pallas_call x2, Pallas kernels, fields_of(): pl.pallas_call(fields_kernel, in_specs=[vmem()] * 6, out_specs=[vmem()] *...  3.27 us
    pallas_call x2, Pallas kernels, slopes_of(): pl.pallas_call(slopes_kernel, in_specs=[vmem()] * 2, out_specs=[vmem()] *...  3.02 us
    ppermute x1, starting transfers between devices, local(): got_near = lax.ppermute(rim_near, 'space', first)  2.99 us
  transfers between devices with their start and end apart: 15, of which 4 were waited for; matrix products, arithmetic and copies ran while one was open for 0% of the time, Pallas kernels for 30%

profile of v7, /device:TPU:0, one launch (start us, length us, event | category | flops | bytes accessed | tf_op | source)
XLA Modules:
  0.0 70.3 jit_solution(13229405153799219362)
XLA Ops:
  0.6 1.2 %shard_map.113 = (bf16[256,512]{1,0:T(8,128)(2,1)S(1)}, bf16[256,512]{1,0:T(8,128)(2,1)S(1)}, bf16[256,512]{1,0:T(8,128)(2,1)S(1)}, bf16[256,512]{1,0:T(8,128)(2,1)S(1)}) custom-call(bf16[2,2048,512]{2,1,0:T(8,128)(2,1)} %bitcast.14), custom_call_target="tpu_custom_call" | custom-call | tf_op jit(solution)/shard_map/pallas_call | solution.py:380
  1.9 6.7 %collective-permute-start = (bf16[256,512]{1,0:T(8,128)(2,1)S(1)}, bf16[256,512]{1,0:T(8,128)(2,1)S(1)}, u32[]{:S(2)}, u32[]{:S(2)}) collective-permute-start(bf16[256,512]{1,0:T(8,128)(2,1)S(1)} %get-tuple-element.60), channel_id=1, source_target_pairs={{0,15},{1,2},{2,1},{3,4},{4,3},{5,6},{6,5},{7,8},{8,7},{9,10},{10,... | collective-permute-start | bytes 786440 | tf_op jit(solution)/shard_map/ppermute | solution.py:391
  8.5 0.0 collective-permute-start.1
  8.5 0.5 collective-permute-start.2
  9.0 1.5 %collective-permute-start.3 = (bf16[256,512]{1,0:T(8,128)(2,1)S(1)}, bf16[256,512]{1,0:T(8,128)(2,1)S(1)}, u32[]{:S(2)}, u32[]{:S(2)}) collective-permute-start(bf16[256,512]{1,0:T(8,128)(2,1)S(1)} %get-tuple-element.68), channel_id=1, source_target_pairs={{0,1},{1,0},{2,3},{3,2},{4,5},{5,4},{6,7},{7,6},{8,9},{9,8},{10,11... | collective-permute-start | bytes 786440 | tf_op jit(solution)/shard_map/ppermute | solution.py:390
  10.6 4.3 %shard_map.112 = (f32[1024,512]{1,0:T(8,128)S(1)}, f32[1024,512]{1,0:T(8,128)S(1)}, bf16[1024,640]{1,0:T(8,128)(2,1)S(1)}, bf16[512,512]{1,0:T(8,128)(2,1)S(1)},...) custom-call(s32[4,8]{1,0:T(4,128)} %bitcast.10, s32[8]{0:T(128)} %count.1, ...), custom_call_target="tpu_custom_call" | custom-call | flops 2000000000 | bytes 8000000 | tf_op jit(solution)/shard_map/pallas_call | solution.py:396
  14.9 0.8 %collective-permute-done.near = bf16[256,512]{1,0:T(8,128)(2,1)S(1)} collective-permute-done((bf16[256,512]{1,0:T(8,128)(2,1)S(1)}, bf16[256,512]{1,0:T(8,128)(2,1)S(1)}, u32[]{:S(2)}, u32[]{:S(2)}) %collective-permute-start) | collective-permute-done | bytes 262176 | tf_op jit(solution)/shard_map/ppermute | solution.py:391
  15.7 2.1 %collective-permute-done.1.far = bf16[256,512]{1,0:T(8,128)(2,1)S(1)} collective-permute-done((bf16[256,512]{1,0:T(8,128)(2,1)S(1)}, bf16[256,512]{1,0:T(8,128)(2,1)S(1)}, u32[]{:S(2)}, u32[]{:S(2)}) %collective-permute-start.1) | collective-permute-done | bytes 262176 | tf_op jit(solution)/shard_map/ppermute | solution.py:390
  17.8 0.0 copy-start
  17.8 0.0 copy-start.2
  17.8 0.0 copy-start.3
  17.8 0.0 copy-start.4
  17.8 1.6 %shard_map.114 = (bf16[1024,512]{1,0:T(8,128)(2,1)S(1)}, bf16[88,1024]{1,0:T(8,128)(2,1)S(1)}) custom-call(f32[1024,512]{1,0:T(8,128)S(1)} %get-tuple-element.59.acc, bf16[256,512]{1,0:T(8,128)(2,1)S(1)} %collective-permute-done.near, bf16[256,512]{1,0:T(8,128)(2,1)S(1)} %collective-permute-done.1.far, bf16[1024,640]{1,0:T(8,128)(2,1)S(1)} %get-tuple-element.62.halo_w, ...), custom_call_target="tpu_custom_call" | custom-call | flops 100000000 | bytes 400000 | tf_op jit(solution)/shard_map/pallas_call | solution.py:425
  19.4 2.8 %collective-permute-start.6 = (bf16[88,1024]{1,0:T(8,128)(2,1)S(1)}, bf16[88,1024]{1,0:T(8,128)(2,1)S(1)}, u32[]{:S(2)}, u32[]{:S(2)}) collective-permute-start(bf16[88,1024]{1,0:T(8,128)(2,1)S(1)} %get-tuple-element.65.own0), channel_id=1, source_target_pairs={{0,48},{16,0},{32,16},{48,32},{1,49},{17,1},{33,17},{49,33},{2,50}... | collective-permute-start | bytes 540680 | tf_op jit(solution)/shard_map/ppermute | solution.py:422
  22.2 0.0 collective-permute-start.5
  22.2 0.0 collective-permute-done.2.near
  22.2 0.0 collective-permute-done.3.far
  22.2 0.0 copy-start.1
  22.3 1.6 %shard_map.115 = (bf16[1024,512]{1,0:T(8,128)(2,1)S(1)}, bf16[88,1024]{1,0:T(8,128)(2,1)S(1)}) custom-call(f32[1024,512]{1,0:T(8,128)S(1)} %get-tuple-element.66.acc, bf16[256,512]{1,0:T(8,128)(2,1)S(1)} %collective-permute-done.2.near, bf16[256,512]{1,0:T(8,128)(2,1)S(1)} %collective-permute-done.3.far, bf16[1024,640]{1,0:T(8,128)(2,1)S(1)} %get-tuple-element.62.halo_w, ...), custom_call_target="tpu_custom_call" | custom-call | flops 100000000 | bytes 400000 | tf_op jit(solution)/shard_map/pallas_call | solution.py:425
  23.9 3.3 %collective-permute-start.4 = (bf16[88,1024]{1,0:T(8,128)(2,1)S(1)}, bf16[88,1024]{1,0:T(8,128)(2,1)S(1)}, u32[]{:S(2)}, u32[]{:S(2)}) collective-permute-start(bf16[88,1024]{1,0:T(8,128)(2,1)S(1)} %get-tuple-element.69.own1), channel_id=1, source_target_pairs={{0,48},{16,0},{32,16},{48,32},{1,49},{17,1},{33,17},{49,33},{2,50}... | collective-permute-start | bytes 540680 | tf_op jit(solution)/shard_map/ppermute | solution.py:422
  27.2 0.0 collective-permute-start.8
  27.2 0.0 collective-permute-done.6.o20
  27.2 2.1 %collective-permute-done.5.o10 = bf16[88,1024]{1,0:T(8,128)(2,1)S(1)} collective-permute-done((bf16[88,1024]{1,0:T(8,128)(2,1)S(1)}, bf16[88,1024]{1,0:T(8,128)(2,1)S(1)}, u32[]{:S(2)}, u32[]{:S(2)}) %collective-permute-start.5) | collective-permute-done | bytes 180256 | tf_op jit(solution)/shard_map/ppermute | solution.py:422
  29.3 0.0 collective-permute-start.9
  29.3 1.5 %shard_map.116 = (bf16[512,1024]{1,0:T(8,128)(2,1)S(1)}, bf16[512,1024]{1,0:T(8,128)(2,1)S(1)}) custom-call(bf16[1024,512]{1,0:T(8,128)(2,1)S(1)} %get-tuple-element.71.lat.lat0, bf16[512,512]{1,0:T(8,128)(2,1)S(1)} %get-tuple-element.63.w_in), custom_call_target="tpu_custom_call" | custom-call | flops 100000000 | bytes 400000 | tf_op jit(solution)/shard_map/pallas_call | solution.py:435
  30.8 0.0 collective-permute-done.4.o21
  30.8 3.5 %collective-permute-start.7 = (bf16[88,1024]{1,0:T(8,128)(2,1)S(1)}, bf16[88,1024]{1,0:T(8,128)(2,1)S(1)}, u32[]{:S(2)}, u32[]{:S(2)}) collective-permute-start(bf16[88,1024]{1,0:T(8,128)(2,1)S(1)} %collective-permute-done.4.o21), channel_id=1, source_target_pairs={{0,48},{16,0},{32,16},{48,32},{1,49},{17,1},{33,17},{49,33},{2,50}... | collective-permute-start | bytes 540680 | tf_op jit(solution)/shard_map/ppermute | solution.py:422
  34.3 1.5 %shard_map.117 = (bf16[512,1024]{1,0:T(8,128)(2,1)S(1)}, bf16[512,1024]{1,0:T(8,128)(2,1)S(1)}) custom-call(bf16[1024,512]{1,0:T(8,128)(2,1)S(1)} %get-tuple-element.78.lat.lat1, bf16[512,512]{1,0:T(8,128)(2,1)S(1)} %get-tuple-element.63.w_in), custom_call_target="tpu_custom_call" | custom-call | flops 100000000 | bytes 400000 | tf_op jit(solution)/shard_map/pallas_call | solution.py:435
  35.8 0.0 copy-done
  35.8 0.0 copy-done.2
  35.8 0.0 copy-done.3
  35.8 0.0 copy-done.4
  35.8 1.6 %shard_map.118 = (bf16[2688,1024]{1,0:T(8,128)(2,1)S(1)}, bf16[512,512]{1,0:T(8,128)(2,1)S(1)}, bf16[512,88]{1,0:T(8,128)(2,1)S(1)}, bf16[88,1024]{1,0:T(8,128)(2,1)S(1)}, f32[88,1]{1,0:T(8,128)S(1)}) custom-call(s32[4,8]{1,0:T(4,128)S(1)} %bitcast.11, s32[8]{0:T(128)S(1)} %copy-done.3, bf16[8,4,128,128]{3,2,1,0:T(8,128)(2,1)S(1)} %get-tuple-element.76.weight, ...), custom_call_target="tpu_custom_call" | custom-call | flops 100000000 | bytes 400000 | tf_op jit(solution)/shard_map/pallas_call | solution.py:461
  37.4 0.0 collective-permute-done.8.o11
  37.4 0.0 collective-permute-done.9.far0
  37.4 1.1 %shard_map.119 = (f32[88,1024]{1,0:T(8,128)S(1)}, f32[88,1024]{1,0:T(8,128)S(1)}) custom-call(bf16[88,1024]{1,0:T(8,128)(2,1)S(1)} %get-tuple-element.65.own0, bf16[88,1024]{1,0:T(8,128)(2,1)S(1)} %get-tuple-element.69.own1, bf16[88,1024]{1,0:T(8,128)(2,1)S(1)} %collective-permute-done.5.o10, bf16[88,1024]{1,0:T(8,128)(2,1)S(1)} %collective-permute-done.8.o11, ...), custom_call_target="tpu_custom_call" | custom-call | flops 100000000 | bytes 400000 | tf_op jit(solution)/shard_map/pallas_call | solution.py:480
  38.5 0.0 collective-permute-done.7.far1
  38.5 0.0 copy-done.1
  38.6 2.7 %shard_map.120 = (bf16[512,1024]{1,0:T(8,128)(2,1)S(1)}, bf16[512,1024]{1,0:T(8,128)(2,1)S(1)}, f32[256,640]{1,0:T(8,128)S(1)}, bf16[256,640]{1,0:T(8,128)(2,1)S(1)}) custom-call(bf16[88,1024]{1,0:T(8,128)(2,1)S(1)} %get-tuple-element.65.own0, bf16[88,1024]{1,0:T(8,128)(2,1)S(1)} %get-tuple-element.69.own1, ...), custom_call_target="tpu_custom_call" | custom-call | flops 2000000000 | bytes 8000000 | tf_op jit(solution)/shard_map/pallas_call | solution.py:491
  41.2 0.1 collective-permute-start.10
  41.3 2.3 %shard_map.121 = (bf16[512,1024]{1,0:T(8,128)(2,1)S(1)}, bf16[512,1024]{1,0:T(8,128)(2,1)S(1)}, bf16[2,256,512]{2,1,0:T(8,128)(2,1)S(1)}, bf16[2,256,512]{2,1,0:T(8,128)(2,1)S(1)}) custom-call(bf16[512,1024]{1,0:T(8,128)(2,1)S(1)} %get-tuple-element.87.grad_pre0, bf16[512,1024]{1,0:T(8,128)(2,1)S(1)} %get-tuple-element.88.grad_pre1, ...), custom_call_target="tpu_custom_call" | custom-call | flops 2000000000 | bytes 8000000 | tf_op jit(solution)/shard_map/pallas_call | solution.py:515
  43.7 0.0 collective-permute-done.10.got
  43.7 0.1 shard_map.122
  43.8 2.5 %collective-permute-start.11 = (bf16[128,640]{1,0:T(8,128)(2,1)S(1)}, bf16[128,640]{1,0:T(8,128)(2,1)S(1)}, u32[]{:S(2)}, u32[]{:S(2)}) collective-permute-start(bf16[128,640]{1,0:T(8,128)(2,1)S(1)} %get-tuple-element.97), channel_id=1, source_target_pairs={{0,48},{16,32},{32,16},{48,0},{1,49},{17,33},{33,17},{49,1},{2,50}... | collective-permute-start | bytes 491528 | tf_op jit(solution)/shard_map/ppermute | solution.py:548
  46.3 0.0 collective-permute-start.12
  46.3 3.0 %collective-permute-start.13 = (bf16[2,256,512]{2,1,0:T(8,128)(2,1)S(1)}, bf16[2,256,512]{2,1,0:T(8,128)(2,1)S(1)}, u32[]{:S(2)}, u32[]{:S(2)}) collective-permute-start(bf16[2,256,512]{2,1,0:T(8,128)(2,1)S(1)} %get-tuple-element.109), channel_id=1, source_target_pairs={{0,15},{1,2},{2,1},{3,4},{4,3},{5,6},{6,5},{7,8},{8,7},{9,10},{10,... | collective-permute-start | bytes 1572872 | tf_op jit(solution)/shard_map/ppermute | solution.py:553
  49.3 2.8 %shard_map.123 = (f32[2,2048,512]{2,1,0:T(8,128)}, f32[2,256,512]{2,1,0:T(8,128)S(1)}) custom-call(bf16[512,1024]{1,0:T(8,128)(2,1)S(1)} %get-tuple-element.100.grad_grid.base, bf16[2688,1024]{1,0:T(8,128)(2,1)S(1)} %get-tuple-element.89.turned, bf16[512,1024]{1,0:T(8,128)(2,1)S(1)} %get-tuple-element.100.grad_grid.base), custom_call_target="tpu_custom_call" | custom-call | flops 2000000000 | bytes 8000000 | tf_op jit(solution)/shard_map/pallas_call | solution.py:532
  52.1 0.0 collective-permute-done.11.got
  52.1 0.1 shard_map.124
  52.2 0.1 collective-permute-start.14
  52.3 2.8 %shard_map.125 = (f32[2,2048,512]{2,1,0:T(8,128)}, f32[2,256,512]{2,1,0:T(8,128)S(1)}) custom-call(bf16[512,1024]{1,0:T(8,128)(2,1)S(1)} %get-tuple-element.104.grad_grid, bf16[2688,1024]{1,0:T(8,128)(2,1)S(1)} %get-tuple-element.89.turned, f32[2,2048,512]{2,1,0:T(8,128)} %get-tuple-element.105.base), custom_call_target="tpu_custom_call", output_to_operand_aliasing={{0}: (2, {})} | custom-call | flops 2000000000 | bytes 8000000 | tf_op jit(solution)/shard_map/pallas_call | solution.py:532
  55.1 1.6 %collective-permute-done.14.got = bf16[64,640]{1,0:T(8,128)(2,1)S(1)} collective-permute-done((bf16[64,640]{1,0:T(8,128)(2,1)S(1)}, bf16[64,640]{1,0:T(8,128)(2,1)S(1)}, u32[]{:S(2)}, u32[]{:S(2)}) %collective-permute-start.14) | collective-permute-done | bytes 81952 | tf_op jit(solution)/shard_map/ppermute | solution.py:557
  56.8 11.4 %all_to_all.5.got = bf16[16,4,640]{2,1,0:T(4,128)(2,1)S(1)} all-to-all(bf16[16,4,640]{2,1,0:T(4,128)(2,1)S(1)} %shard_map.126), channel_id=1, replica_groups=mesh['dp'=2,'member'=4,'space'=16] {'space'}, dimensions={0} | all-to-all | bytes 163840 | tf_op jit(solution)/shard_map/all_to_all | solution.py:570
  68.2 0.0 collective-permute-done.12.far
  68.2 0.0 collective-permute-done.13.near
  68.2 2.0 %shard_map.127 = (f32[2,2048,512]{2,1,0:T(8,128)}, f32[4,512]{1,0:T(4,128)}, f32[4,83]{1,0:T(4,128)}) custom-call(f32[2,2048,512]{2,1,0:T(8,128)} %get-tuple-element.106.base, f32[2,256,512]{2,1,0:T(8,128)S(1)} %get-tuple-element.101.edge0, f32[2,256,512]{2,1,0:T(8,128)S(1)} %get-tuple-element.107.edge1, ...), custom_call_target="tpu_custom_call", output_to_operand_aliasing={{0}: (0, {})} | custom-call | tf_op jit(solution)/shard_map/pallas_call | solution.py:571
  (1 shorter events, 0.0 us)
Async XLA Ops:
  1.9 13.8 %collective-permute-start = (bf16[256,512]{1,0:T(8,128)(2,1)S(1)}, bf16[256,512]{1,0:T(8,128)(2,1)S(1)}, u32[]{:S(2)}, u32[]{:S(2)}) collective-permute-start(bf16[256,512]{1,0:T(8,128)(2,1)S(1)} %get-tuple-element.60), channel_id=1, source_target_pairs={{0,15},{1,2},{2,1},{3,4},{4,3},{5,6},{6,5},{7,8},{8,7},{9,10},{10,... | collective-permute-start | bytes 786440 | tf_op jit(solution)/shard_map/ppermute | solution.py:391
  8.5 9.2 %collective-permute-start.1 = (bf16[256,512]{1,0:T(8,128)(2,1)S(1)}, bf16[256,512]{1,0:T(8,128)(2,1)S(1)}, u32[]{:S(2)}, u32[]{:S(2)}) collective-permute-start(bf16[256,512]{1,0:T(8,128)(2,1)S(1)} %get-tuple-element.61), channel_id=1, source_target_pairs={{0,1},{1,0},{2,3},{3,2},{4,5},{5,4},{6,7},{7,6},{8,9},{9,8},{10,11... | collective-permute-start | bytes 786440 | tf_op jit(solution)/shard_map/ppermute | solution.py:390
  8.5 13.7 %collective-permute-start.2 = (bf16[256,512]{1,0:T(8,128)(2,1)S(1)}, bf16[256,512]{1,0:T(8,128)(2,1)S(1)}, u32[]{:S(2)}, u32[]{:S(2)}) collective-permute-start(bf16[256,512]{1,0:T(8,128)(2,1)S(1)} %get-tuple-element.67), channel_id=1, source_target_pairs={{0,15},{1,2},{2,1},{3,4},{4,3},{5,6},{6,5},{7,8},{8,7},{9,10},{10,... | collective-permute-start | bytes 786440 | tf_op jit(solution)/shard_map/ppermute | solution.py:391
  9.0 13.2 %collective-permute-start.3 = (bf16[256,512]{1,0:T(8,128)(2,1)S(1)}, bf16[256,512]{1,0:T(8,128)(2,1)S(1)}, u32[]{:S(2)}, u32[]{:S(2)}) collective-permute-start(bf16[256,512]{1,0:T(8,128)(2,1)S(1)} %get-tuple-element.68), channel_id=1, source_target_pairs={{0,1},{1,0},{2,3},{3,2},{4,5},{5,4},{6,7},{7,6},{8,9},{9,8},{10,11... | collective-permute-start | bytes 786440 | tf_op jit(solution)/shard_map/ppermute | solution.py:390
  17.8 18.0 %copy-start = (bf16[1,83,1024]{2,1,0:T(8,128)(2,1)S(1)}, bf16[1,83,1024]{2,1,0:T(8,128)(2,1)}, u32[]{:S(2)}) copy-start(bf16[1,83,1024]{2,1,0:T(8,128)(2,1)} %param.15) | copy-start | bytes 509956
  17.8 18.0 %copy-start.2 = (s32[8,4]{0,1:T(4,128)S(1)}, s32[8,4]{0,1:T(4,128)}, u32[]{:S(2)}) copy-start(s32[8,4]{0,1:T(4,128)} %param.11) | copy-start | bytes 388
  17.8 18.0 %copy-start.3 = (s32[8]{0:T(128)S(1)}, s32[8]{0:T(128)}, u32[]{:S(2)}) copy-start(s32[8]{0:T(128)} %count.1) | copy-start | bytes 100
  17.8 18.1 %copy-start.4 = (f32[83]{0:T(128)S(1)}, f32[83]{0:T(128)}, u32[]{:S(2)}) copy-start(f32[83]{0:T(128)} %param.17) | copy-start | bytes 1000
  19.4 7.8 %collective-permute-start.6 = (bf16[88,1024]{1,0:T(8,128)(2,1)S(1)}, bf16[88,1024]{1,0:T(8,128)(2,1)S(1)}, u32[]{:S(2)}, u32[]{:S(2)}) collective-permute-start(bf16[88,1024]{1,0:T(8,128)(2,1)S(1)} %get-tuple-element.65.own0), channel_id=1, source_target_pairs={{0,48},{16,0},{32,16},{48,32},{1,49},{17,1},{33,17},{49,33},{2,50}... | collective-permute-start | bytes 540680 | tf_op jit(solution)/shard_map/ppermute | solution.py:422
  22.2 7.0 %collective-permute-start.5 = (bf16[88,1024]{1,0:T(8,128)(2,1)S(1)}, bf16[88,1024]{1,0:T(8,128)(2,1)S(1)}, u32[]{:S(2)}, u32[]{:S(2)}) collective-permute-start(bf16[88,1024]{1,0:T(8,128)(2,1)S(1)} %get-tuple-element.65.own0), channel_id=1, source_target_pairs={{0,16},{16,32},{32,48},{48,0},{1,17},{17,33},{33,49},{49,1},{2,18}... | collective-permute-start | bytes 540680 | tf_op jit(solution)/shard_map/ppermute | solution.py:422
  22.2 16.3 %copy-start.1 = (f32[1024]{0:T(1024)S(1)}, f32[1024]{0:T(1024)}, u32[]{:S(2)}) copy-start(f32[1024]{0:T(1024)} %param.16) | copy-start | bytes 12292
  23.9 6.9 %collective-permute-start.4 = (bf16[88,1024]{1,0:T(8,128)(2,1)S(1)}, bf16[88,1024]{1,0:T(8,128)(2,1)S(1)}, u32[]{:S(2)}, u32[]{:S(2)}) collective-permute-start(bf16[88,1024]{1,0:T(8,128)(2,1)S(1)} %get-tuple-element.69.own1), channel_id=1, source_target_pairs={{0,48},{16,0},{32,16},{48,32},{1,49},{17,1},{33,17},{49,33},{2,50}... | collective-permute-start | bytes 540680 | tf_op jit(solution)/shard_map/ppermute | solution.py:422
  27.2 10.2 %collective-permute-start.8 = (bf16[88,1024]{1,0:T(8,128)(2,1)S(1)}, bf16[88,1024]{1,0:T(8,128)(2,1)S(1)}, u32[]{:S(2)}, u32[]{:S(2)}) collective-permute-start(bf16[88,1024]{1,0:T(8,128)(2,1)S(1)} %get-tuple-element.69.own1), channel_id=1, source_target_pairs={{0,16},{16,32},{32,48},{48,0},{1,17},{17,33},{33,49},{49,1},{2,18}... | collective-permute-start | bytes 540680 | tf_op jit(solution)/shard_map/ppermute | solution.py:422
  29.3 8.1 %collective-permute-start.9 = (bf16[88,1024]{1,0:T(8,128)(2,1)S(1)}, bf16[88,1024]{1,0:T(8,128)(2,1)S(1)}, u32[]{:S(2)}, u32[]{:S(2)}) collective-permute-start(bf16[88,1024]{1,0:T(8,128)(2,1)S(1)} %collective-permute-done.5.o10), channel_id=1, source_target_pairs={{0,16},{16,32},{32,48},{48,0},{1,17},{17,33},{33,49},{49,1},{2,18}... | collective-permute-start | bytes 540680 | tf_op jit(solution)/shard_map/ppermute | solution.py:422
  30.8 7.8 %collective-permute-start.7 = (bf16[88,1024]{1,0:T(8,128)(2,1)S(1)}, bf16[88,1024]{1,0:T(8,128)(2,1)S(1)}, u32[]{:S(2)}, u32[]{:S(2)}) collective-permute-start(bf16[88,1024]{1,0:T(8,128)(2,1)S(1)} %collective-permute-done.4.o21), channel_id=1, source_target_pairs={{0,48},{16,0},{32,16},{48,32},{1,49},{17,1},{33,17},{49,33},{2,50}... | collective-permute-start | bytes 540680 | tf_op jit(solution)/shard_map/ppermute | solution.py:422
  41.2 2.5 %collective-permute-start.10 = (bf16[256,640]{1,0:T(8,128)(2,1)S(1)}, bf16[256,640]{1,0:T(8,128)(2,1)S(1)}, u32[]{:S(2)}, u32[]{:S(2)}) collective-permute-start(bf16[256,640]{1,0:T(8,128)(2,1)S(1)} %get-tuple-element.93), channel_id=1, source_target_pairs={{0,64},{64,0},{1,65},{65,1},{2,66},{66,2},{3,67},{67,3},{4,68},{68... | collective-permute-start | bytes 983048 | tf_op jit(solution)/shard_map/ppermute | solution.py:513
  43.8 8.3 %collective-permute-start.11 = (bf16[128,640]{1,0:T(8,128)(2,1)S(1)}, bf16[128,640]{1,0:T(8,128)(2,1)S(1)}, u32[]{:S(2)}, u32[]{:S(2)}) collective-permute-start(bf16[128,640]{1,0:T(8,128)(2,1)S(1)} %get-tuple-element.97), channel_id=1, source_target_pairs={{0,48},{16,32},{32,16},{48,0},{1,49},{17,33},{33,17},{49,1},{2,50}... | collective-permute-start | bytes 491528 | tf_op jit(solution)/shard_map/ppermute | solution.py:548
  46.3 21.9 %collective-permute-start.12 = (bf16[2,256,512]{2,1,0:T(8,128)(2,1)S(1)}, bf16[2,256,512]{2,1,0:T(8,128)(2,1)S(1)}, u32[]{:S(2)}, u32[]{:S(2)}) collective-permute-start(bf16[2,256,512]{2,1,0:T(8,128)(2,1)S(1)} %get-tuple-element.108), channel_id=1, source_target_pairs={{0,1},{1,0},{2,3},{3,2},{4,5},{5,4},{6,7},{7,6},{8,9},{9,8},{10,11... | collective-permute-start | bytes 1572872 | tf_op jit(solution)/shard_map/ppermute | solution.py:552
  46.3 21.9 %collective-permute-start.13 = (bf16[2,256,512]{2,1,0:T(8,128)(2,1)S(1)}, bf16[2,256,512]{2,1,0:T(8,128)(2,1)S(1)}, u32[]{:S(2)}, u32[]{:S(2)}) collective-permute-start(bf16[2,256,512]{2,1,0:T(8,128)(2,1)S(1)} %get-tuple-element.109), channel_id=1, source_target_pairs={{0,15},{1,2},{2,1},{3,4},{4,3},{5,6},{6,5},{7,8},{8,7},{9,10},{10,... | collective-permute-start | bytes 1572872 | tf_op jit(solution)/shard_map/ppermute | solution.py:553
  52.2 4.5 %collective-permute-start.14 = (bf16[64,640]{1,0:T(8,128)(2,1)S(1)}, bf16[64,640]{1,0:T(8,128)(2,1)S(1)}, u32[]{:S(2)}, u32[]{:S(2)}) collective-permute-start(bf16[64,640]{1,0:T(8,128)(2,1)S(1)} %get-tuple-element.103), channel_id=1, source_target_pairs={{0,16},{16,0},{32,48},{48,32},{1,17},{17,1},{33,49},{49,33},{2,18}... | collective-permute-start | bytes 245768 | tf_op jit(solution)/shard_map/ppermute | solution.py:557

commit v8 on v7

--- a/solution.py
+++ b/solution.py
@@ -188,8 +188,9 @@
         rounded = total.astype(bf16)
         lat_out[at] = rounded
         pre = dot(w_in[...], rounded, NT)
-        _, half = gelu_parts(pre)
-        fields[:, at] = dot(w_out[...], (pre * half).astype(bf16)).astype(bf16)
+        inner = pre * (gelu_scale + (gelu_scale * gelu_cubic) * (pre * pre))
+        half = 0.5 + 0.5 * jnp.tanh(inner.astype(bf16))
+        fields[:, at] = dot(w_out[...], pre.astype(bf16) * half).astype(bf16)
 
 
 def slopes_kernel(lat, w_in, act_t, slope_t):

time: 70.5 us -> 70.5 us (level)
  no operation moved by 1% of the time
where the time goes in v8:
time: 70.5 us; the launch traced here: 70.3 us
  Pallas kernels  27.3 us (39%)
  starting transfers between devices  23.9 us (34%)
  blocking collectives  11.4 us (16%)
  waiting for transfers between devices  6.61 us (9%)
  between operations  1.02 us (1%)
    all_to_all x1, blocking collectives, local(): spread = lax.all_to_all(spread, 'space', 0, 0, tiled=True)  11.4 us
    ppermute x6, starting transfers between devices, along(): return lax.ppermute(x, 'member', ring(chips, distance))  9.61 us
    ppermute x2, starting transfers between devices, local(): near = lax.ppermute(edges[2 * m], 'space', first)  7.16 us
    pallas_call x2, Pallas kernels, owned_of(): pl.pallas_call(functools.partial(owned_kernel, member=member, own_rows=ow...  5.65 us
    pallas_call x1, Pallas kernels, local(): pl.pallas_call(functools.partial(prepare_kernel, spaces=spaces), in_specs...  4.32 us
    pallas_call x2, Pallas kernels, fields_of(): pl.pallas_call(fields_kernel, in_specs=[vmem()] * 6, out_specs=[vmem()] *...  3.17 us
    pallas_call x2, Pallas kernels, slopes_of(): pl.pallas_call(slopes_kernel, in_specs=[vmem()] * 2, out_specs=[vmem()] *...  3.02 us
    ppermute x1, starting transfers between devices, local(): got_near = lax.ppermute(rim_near, 'space', first)  2.98 us
  transfers between devices with their start and end apart: 15, of which 4 were waited for; matrix products, arithmetic and copies ran while one was open for 0% of the time, Pallas kernels for 30%

profile of v8, /device:TPU:0, one launch (start us, length us, event | category | flops | bytes accessed | tf_op | source)
XLA Modules:
  0.0 70.3 jit_solution(7451774939120183915)
XLA Ops:
  0.6 1.2 %shard_map.113 = (bf16[256,512]{1,0:T(8,128)(2,1)S(1)}, bf16[256,512]{1,0:T(8,128)(2,1)S(1)}, bf16[256,512]{1,0:T(8,128)(2,1)S(1)}, bf16[256,512]{1,0:T(8,128)(2,1)S(1)}) custom-call(bf16[2,2048,512]{2,1,0:T(8,128)(2,1)} %bitcast.14), custom_call_target="tpu_custom_call" | custom-call | tf_op jit(solution)/shard_map/pallas_call | solution.py:381
  1.9 6.7 %collective-permute-start = (bf16[256,512]{1,0:T(8,128)(2,1)S(1)}, bf16[256,512]{1,0:T(8,128)(2,1)S(1)}, u32[]{:S(2)}, u32[]{:S(2)}) collective-permute-start(bf16[256,512]{1,0:T(8,128)(2,1)S(1)} %get-tuple-element.60), channel_id=1, source_target_pairs={{0,15},{1,2},{2,1},{3,4},{4,3},{5,6},{6,5},{7,8},{8,7},{9,10},{10,... | collective-permute-start | bytes 786440 | tf_op jit(solution)/shard_map/ppermute | solution.py:392
  8.5 0.0 collective-permute-start.1
  8.5 0.5 collective-permute-start.2
  9.0 1.5 %collective-permute-start.3 = (bf16[256,512]{1,0:T(8,128)(2,1)S(1)}, bf16[256,512]{1,0:T(8,128)(2,1)S(1)}, u32[]{:S(2)}, u32[]{:S(2)}) collective-permute-start(bf16[256,512]{1,0:T(8,128)(2,1)S(1)} %get-tuple-element.68), channel_id=1, source_target_pairs={{0,1},{1,0},{2,3},{3,2},{4,5},{5,4},{6,7},{7,6},{8,9},{9,8},{10,11... | collective-permute-start | bytes 786440 | tf_op jit(solution)/shard_map/ppermute | solution.py:391
  10.6 4.3 %shard_map.112 = (f32[1024,512]{1,0:T(8,128)S(1)}, f32[1024,512]{1,0:T(8,128)S(1)}, bf16[1024,640]{1,0:T(8,128)(2,1)S(1)}, bf16[512,512]{1,0:T(8,128)(2,1)S(1)},...) custom-call(s32[4,8]{1,0:T(4,128)} %bitcast.10, s32[8]{0:T(128)} %count.1, ...), custom_call_target="tpu_custom_call" | custom-call | flops 2000000000 | bytes 8000000 | tf_op jit(solution)/shard_map/pallas_call | solution.py:397
  14.9 0.8 %collective-permute-done.near = bf16[256,512]{1,0:T(8,128)(2,1)S(1)} collective-permute-done((bf16[256,512]{1,0:T(8,128)(2,1)S(1)}, bf16[256,512]{1,0:T(8,128)(2,1)S(1)}, u32[]{:S(2)}, u32[]{:S(2)}) %collective-permute-start) | collective-permute-done | bytes 262176 | tf_op jit(solution)/shard_map/ppermute | solution.py:392
  15.7 2.1 %collective-permute-done.1.far = bf16[256,512]{1,0:T(8,128)(2,1)S(1)} collective-permute-done((bf16[256,512]{1,0:T(8,128)(2,1)S(1)}, bf16[256,512]{1,0:T(8,128)(2,1)S(1)}, u32[]{:S(2)}, u32[]{:S(2)}) %collective-permute-start.1) | collective-permute-done | bytes 262176 | tf_op jit(solution)/shard_map/ppermute | solution.py:391
  17.8 0.0 copy-start
  17.8 0.0 copy-start.2
  17.8 0.0 copy-start.3
  17.8 0.0 copy-start.4
  17.8 1.6 %shard_map.114 = (bf16[1024,512]{1,0:T(8,128)(2,1)S(1)}, bf16[88,1024]{1,0:T(8,128)(2,1)S(1)}) custom-call(f32[1024,512]{1,0:T(8,128)S(1)} %get-tuple-element.59.acc, bf16[256,512]{1,0:T(8,128)(2,1)S(1)} %collective-permute-done.near, bf16[256,512]{1,0:T(8,128)(2,1)S(1)} %collective-permute-done.1.far, bf16[1024,640]{1,0:T(8,128)(2,1)S(1)} %get-tuple-element.62.halo_w, ...), custom_call_target="tpu_custom_call" | custom-call | flops 100000000 | bytes 400000 | tf_op jit(solution)/shard_map/pallas_call | solution.py:426
  19.4 2.8 %collective-permute-start.6 = (bf16[88,1024]{1,0:T(8,128)(2,1)S(1)}, bf16[88,1024]{1,0:T(8,128)(2,1)S(1)}, u32[]{:S(2)}, u32[]{:S(2)}) collective-permute-start(bf16[88,1024]{1,0:T(8,128)(2,1)S(1)} %get-tuple-element.65.own0), channel_id=1, source_target_pairs={{0,48},{16,0},{32,16},{48,32},{1,49},{17,1},{33,17},{49,33},{2,50}... | collective-permute-start | bytes 540680 | tf_op jit(solution)/shard_map/ppermute | solution.py:423
  22.2 0.0 collective-permute-start.5
  22.2 0.0 collective-permute-done.2.near
  22.2 0.0 collective-permute-done.3.far
  22.2 0.0 copy-start.1
  22.2 1.6 %shard_map.115 = (bf16[1024,512]{1,0:T(8,128)(2,1)S(1)}, bf16[88,1024]{1,0:T(8,128)(2,1)S(1)}) custom-call(f32[1024,512]{1,0:T(8,128)S(1)} %get-tuple-element.66.acc, bf16[256,512]{1,0:T(8,128)(2,1)S(1)} %collective-permute-done.2.near, bf16[256,512]{1,0:T(8,128)(2,1)S(1)} %collective-permute-done.3.far, bf16[1024,640]{1,0:T(8,128)(2,1)S(1)} %get-tuple-element.62.halo_w, ...), custom_call_target="tpu_custom_call" | custom-call | flops 100000000 | bytes 400000 | tf_op jit(solution)/shard_map/pallas_call | solution.py:426
  23.8 3.3 %collective-permute-start.4 = (bf16[88,1024]{1,0:T(8,128)(2,1)S(1)}, bf16[88,1024]{1,0:T(8,128)(2,1)S(1)}, u32[]{:S(2)}, u32[]{:S(2)}) collective-permute-start(bf16[88,1024]{1,0:T(8,128)(2,1)S(1)} %get-tuple-element.69.own1), channel_id=1, source_target_pairs={{0,48},{16,0},{32,16},{48,32},{1,49},{17,1},{33,17},{49,33},{2,50}... | collective-permute-start | bytes 540680 | tf_op jit(solution)/shard_map/ppermute | solution.py:423
  27.1 0.0 collective-permute-start.8
  27.1 0.0 collective-permute-done.6.o20
  27.1 2.1 %collective-permute-done.5.o10 = bf16[88,1024]{1,0:T(8,128)(2,1)S(1)} collective-permute-done((bf16[88,1024]{1,0:T(8,128)(2,1)S(1)}, bf16[88,1024]{1,0:T(8,128)(2,1)S(1)}, u32[]{:S(2)}, u32[]{:S(2)}) %collective-permute-start.5) | collective-permute-done | bytes 180256 | tf_op jit(solution)/shard_map/ppermute | solution.py:423
  29.2 0.0 collective-permute-start.9
  29.2 1.5 %shard_map.116 = (bf16[512,1024]{1,0:T(8,128)(2,1)S(1)}, bf16[512,1024]{1,0:T(8,128)(2,1)S(1)}) custom-call(bf16[1024,512]{1,0:T(8,128)(2,1)S(1)} %get-tuple-element.71.lat.lat0, bf16[512,512]{1,0:T(8,128)(2,1)S(1)} %get-tuple-element.63.w_in), custom_call_target="tpu_custom_call" | custom-call | flops 100000000 | bytes 400000 | tf_op jit(solution)/shard_map/pallas_call | solution.py:436
  30.7 0.0 collective-permute-done.4.o21
  30.7 3.5 %collective-permute-start.7 = (bf16[88,1024]{1,0:T(8,128)(2,1)S(1)}, bf16[88,1024]{1,0:T(8,128)(2,1)S(1)}, u32[]{:S(2)}, u32[]{:S(2)}) collective-permute-start(bf16[88,1024]{1,0:T(8,128)(2,1)S(1)} %collective-permute-done.4.o21), channel_id=1, source_target_pairs={{0,48},{16,0},{32,16},{48,32},{1,49},{17,1},{33,17},{49,33},{2,50}... | collective-permute-start | bytes 540680 | tf_op jit(solution)/shard_map/ppermute | solution.py:423
  34.2 1.5 %shard_map.117 = (bf16[512,1024]{1,0:T(8,128)(2,1)S(1)}, bf16[512,1024]{1,0:T(8,128)(2,1)S(1)}) custom-call(bf16[1024,512]{1,0:T(8,128)(2,1)S(1)} %get-tuple-element.78.lat.lat1, bf16[512,512]{1,0:T(8,128)(2,1)S(1)} %get-tuple-element.63.w_in), custom_call_target="tpu_custom_call" | custom-call | flops 100000000 | bytes 400000 | tf_op jit(solution)/shard_map/pallas_call | solution.py:436
  35.7 0.0 copy-done
  35.7 0.0 copy-done.2
  35.8 0.0 copy-done.3
  35.8 0.0 copy-done.4
  35.8 1.6 %shard_map.118 = (bf16[2688,1024]{1,0:T(8,128)(2,1)S(1)}, bf16[512,512]{1,0:T(8,128)(2,1)S(1)}, bf16[512,88]{1,0:T(8,128)(2,1)S(1)}, bf16[88,1024]{1,0:T(8,128)(2,1)S(1)}, f32[88,1]{1,0:T(8,128)S(1)}) custom-call(s32[4,8]{1,0:T(4,128)S(1)} %bitcast.11, s32[8]{0:T(128)S(1)} %copy-done.3, bf16[8,4,128,128]{3,2,1,0:T(8,128)(2,1)S(1)} %get-tuple-element.76.weight, ...), custom_call_target="tpu_custom_call" | custom-call | flops 100000000 | bytes 400000 | tf_op jit(solution)/shard_map/pallas_call | solution.py:462
  37.3 0.0 collective-permute-done.8.o11
  37.4 0.0 collective-permute-done.9.far0
  37.4 1.1 %shard_map.119 = (f32[88,1024]{1,0:T(8,128)S(1)}, f32[88,1024]{1,0:T(8,128)S(1)}) custom-call(bf16[88,1024]{1,0:T(8,128)(2,1)S(1)} %get-tuple-element.65.own0, bf16[88,1024]{1,0:T(8,128)(2,1)S(1)} %get-tuple-element.69.own1, bf16[88,1024]{1,0:T(8,128)(2,1)S(1)} %collective-permute-done.5.o10, bf16[88,1024]{1,0:T(8,128)(2,1)S(1)} %collective-permute-done.8.o11, ...), custom_call_target="tpu_custom_call" | custom-call | flops 100000000 | bytes 400000 | tf_op jit(solution)/shard_map/pallas_call | solution.py:481
  38.5 0.0 collective-permute-done.7.far1
  38.5 0.0 copy-done.1
  38.5 2.7 %shard_map.120 = (bf16[512,1024]{1,0:T(8,128)(2,1)S(1)}, bf16[512,1024]{1,0:T(8,128)(2,1)S(1)}, f32[256,640]{1,0:T(8,128)S(1)}, bf16[256,640]{1,0:T(8,128)(2,1)S(1)}) custom-call(bf16[88,1024]{1,0:T(8,128)(2,1)S(1)} %get-tuple-element.65.own0, bf16[88,1024]{1,0:T(8,128)(2,1)S(1)} %get-tuple-element.69.own1, ...), custom_call_target="tpu_custom_call" | custom-call | flops 2000000000 | bytes 8000000 | tf_op jit(solution)/shard_map/pallas_call | solution.py:492
  41.2 0.1 collective-permute-start.10
  41.3 2.3 %shard_map.121 = (bf16[512,1024]{1,0:T(8,128)(2,1)S(1)}, bf16[512,1024]{1,0:T(8,128)(2,1)S(1)}, bf16[2,256,512]{2,1,0:T(8,128)(2,1)S(1)}, bf16[2,256,512]{2,1,0:T(8,128)(2,1)S(1)}) custom-call(bf16[512,1024]{1,0:T(8,128)(2,1)S(1)} %get-tuple-element.87.grad_pre0, bf16[512,1024]{1,0:T(8,128)(2,1)S(1)} %get-tuple-element.88.grad_pre1, ...), custom_call_target="tpu_custom_call" | custom-call | flops 2000000000 | bytes 8000000 | tf_op jit(solution)/shard_map/pallas_call | solution.py:516
  43.6 0.0 collective-permute-done.10.got
  43.6 0.1 shard_map.122
  43.8 2.5 %collective-permute-start.11 = (bf16[128,640]{1,0:T(8,128)(2,1)S(1)}, bf16[128,640]{1,0:T(8,128)(2,1)S(1)}, u32[]{:S(2)}, u32[]{:S(2)}) collective-permute-start(bf16[128,640]{1,0:T(8,128)(2,1)S(1)} %get-tuple-element.97), channel_id=1, source_target_pairs={{0,48},{16,32},{32,16},{48,0},{1,49},{17,33},{33,17},{49,1},{2,50}... | collective-permute-start | bytes 491528 | tf_op jit(solution)/shard_map/ppermute | solution.py:549
  46.3 0.0 collective-permute-start.12
  46.3 3.0 %collective-permute-start.13 = (bf16[2,256,512]{2,1,0:T(8,128)(2,1)S(1)}, bf16[2,256,512]{2,1,0:T(8,128)(2,1)S(1)}, u32[]{:S(2)}, u32[]{:S(2)}) collective-permute-start(bf16[2,256,512]{2,1,0:T(8,128)(2,1)S(1)} %get-tuple-element.109), channel_id=1, source_target_pairs={{0,15},{1,2},{2,1},{3,4},{4,3},{5,6},{6,5},{7,8},{8,7},{9,10},{10,... | collective-permute-start | bytes 1572872 | tf_op jit(solution)/shard_map/ppermute | solution.py:554
  49.2 2.8 %shard_map.123 = (f32[2,2048,512]{2,1,0:T(8,128)}, f32[2,256,512]{2,1,0:T(8,128)S(1)}) custom-call(bf16[512,1024]{1,0:T(8,128)(2,1)S(1)} %get-tuple-element.100.grad_grid.base, bf16[2688,1024]{1,0:T(8,128)(2,1)S(1)} %get-tuple-element.89.turned, bf16[512,1024]{1,0:T(8,128)(2,1)S(1)} %get-tuple-element.100.grad_grid.base), custom_call_target="tpu_custom_call" | custom-call | flops 2000000000 | bytes 8000000 | tf_op jit(solution)/shard_map/pallas_call | solution.py:533
  52.1 0.0 collective-permute-done.11.got
  52.1 0.1 shard_map.124
  52.2 0.1 collective-permute-start.14
  52.2 2.8 %shard_map.125 = (f32[2,2048,512]{2,1,0:T(8,128)}, f32[2,256,512]{2,1,0:T(8,128)S(1)}) custom-call(bf16[512,1024]{1,0:T(8,128)(2,1)S(1)} %get-tuple-element.104.grad_grid, bf16[2688,1024]{1,0:T(8,128)(2,1)S(1)} %get-tuple-element.89.turned, f32[2,2048,512]{2,1,0:T(8,128)} %get-tuple-element.105.base), custom_call_target="tpu_custom_call", output_to_operand_aliasing={{0}: (2, {})} | custom-call | flops 2000000000 | bytes 8000000 | tf_op jit(solution)/shard_map/pallas_call | solution.py:533
  55.1 1.6 %collective-permute-done.14.got = bf16[64,640]{1,0:T(8,128)(2,1)S(1)} collective-permute-done((bf16[64,640]{1,0:T(8,128)(2,1)S(1)}, bf16[64,640]{1,0:T(8,128)(2,1)S(1)}, u32[]{:S(2)}, u32[]{:S(2)}) %collective-permute-start.14) | collective-permute-done | bytes 81952 | tf_op jit(solution)/shard_map/ppermute | solution.py:558
  56.7 11.4 %all_to_all.5.got = bf16[16,4,640]{2,1,0:T(4,128)(2,1)S(1)} all-to-all(bf16[16,4,640]{2,1,0:T(4,128)(2,1)S(1)} %shard_map.126), channel_id=1, replica_groups=mesh['dp'=2,'member'=4,'space'=16] {'space'}, dimensions={0} | all-to-all | bytes 163840 | tf_op jit(solution)/shard_map/all_to_all | solution.py:571
  68.1 0.0 collective-permute-done.12.far
  68.1 0.0 collective-permute-done.13.near
  68.1 2.0 %shard_map.127 = (f32[2,2048,512]{2,1,0:T(8,128)}, f32[4,512]{1,0:T(4,128)}, f32[4,83]{1,0:T(4,128)}) custom-call(f32[2,2048,512]{2,1,0:T(8,128)} %get-tuple-element.106.base, f32[2,256,512]{2,1,0:T(8,128)S(1)} %get-tuple-element.101.edge0, f32[2,256,512]{2,1,0:T(8,128)S(1)} %get-tuple-element.107.edge1, ...), custom_call_target="tpu_custom_call", output_to_operand_aliasing={{0}: (0, {})} | custom-call | tf_op jit(solution)/shard_map/pallas_call | solution.py:572
  (1 shorter events, 0.0 us)
Async XLA Ops:
  1.9 13.8 %collective-permute-start = (bf16[256,512]{1,0:T(8,128)(2,1)S(1)}, bf16[256,512]{1,0:T(8,128)(2,1)S(1)}, u32[]{:S(2)}, u32[]{:S(2)}) collective-permute-start(bf16[256,512]{1,0:T(8,128)(2,1)S(1)} %get-tuple-element.60), channel_id=1, source_target_pairs={{0,15},{1,2},{2,1},{3,4},{4,3},{5,6},{6,5},{7,8},{8,7},{9,10},{10,... | collective-permute-start | bytes 786440 | tf_op jit(solution)/shard_map/ppermute | solution.py:392
  8.5 9.2 %collective-permute-start.1 = (bf16[256,512]{1,0:T(8,128)(2,1)S(1)}, bf16[256,512]{1,0:T(8,128)(2,1)S(1)}, u32[]{:S(2)}, u32[]{:S(2)}) collective-permute-start(bf16[256,512]{1,0:T(8,128)(2,1)S(1)} %get-tuple-element.61), channel_id=1, source_target_pairs={{0,1},{1,0},{2,3},{3,2},{4,5},{5,4},{6,7},{7,6},{8,9},{9,8},{10,11... | collective-permute-start | bytes 786440 | tf_op jit(solution)/shard_map/ppermute | solution.py:391
  8.5 13.7 %collective-permute-start.2 = (bf16[256,512]{1,0:T(8,128)(2,1)S(1)}, bf16[256,512]{1,0:T(8,128)(2,1)S(1)}, u32[]{:S(2)}, u32[]{:S(2)}) collective-permute-start(bf16[256,512]{1,0:T(8,128)(2,1)S(1)} %get-tuple-element.67), channel_id=1, source_target_pairs={{0,15},{1,2},{2,1},{3,4},{4,3},{5,6},{6,5},{7,8},{8,7},{9,10},{10,... | collective-permute-start | bytes 786440 | tf_op jit(solution)/shard_map/ppermute | solution.py:392
  9.0 13.2 %collective-permute-start.3 = (bf16[256,512]{1,0:T(8,128)(2,1)S(1)}, bf16[256,512]{1,0:T(8,128)(2,1)S(1)}, u32[]{:S(2)}, u32[]{:S(2)}) collective-permute-start(bf16[256,512]{1,0:T(8,128)(2,1)S(1)} %get-tuple-element.68), channel_id=1, source_target_pairs={{0,1},{1,0},{2,3},{3,2},{4,5},{5,4},{6,7},{7,6},{8,9},{9,8},{10,11... | collective-permute-start | bytes 786440 | tf_op jit(solution)/shard_map/ppermute | solution.py:391
  17.8 18.0 %copy-start = (bf16[1,83,1024]{2,1,0:T(8,128)(2,1)S(1)}, bf16[1,83,1024]{2,1,0:T(8,128)(2,1)}, u32[]{:S(2)}) copy-start(bf16[1,83,1024]{2,1,0:T(8,128)(2,1)} %param.15) | copy-start | bytes 509956
  17.8 18.0 %copy-start.2 = (s32[8,4]{0,1:T(4,128)S(1)}, s32[8,4]{0,1:T(4,128)}, u32[]{:S(2)}) copy-start(s32[8,4]{0,1:T(4,128)} %param.11) | copy-start | bytes 388
  17.8 18.0 %copy-start.3 = (s32[8]{0:T(128)S(1)}, s32[8]{0:T(128)}, u32[]{:S(2)}) copy-start(s32[8]{0:T(128)} %count.1) | copy-start | bytes 100
  17.8 18.0 %copy-start.4 = (f32[83]{0:T(128)S(1)}, f32[83]{0:T(128)}, u32[]{:S(2)}) copy-start(f32[83]{0:T(128)} %param.17) | copy-start | bytes 1000
  19.4 7.7 %collective-permute-start.6 = (bf16[88,1024]{1,0:T(8,128)(2,1)S(1)}, bf16[88,1024]{1,0:T(8,128)(2,1)S(1)}, u32[]{:S(2)}, u32[]{:S(2)}) collective-permute-start(bf16[88,1024]{1,0:T(8,128)(2,1)S(1)} %get-tuple-element.65.own0), channel_id=1, source_target_pairs={{0,48},{16,0},{32,16},{48,32},{1,49},{17,1},{33,17},{49,33},{2,50}... | collective-permute-start | bytes 540680 | tf_op jit(solution)/shard_map/ppermute | solution.py:423
  22.2 7.0 %collective-permute-start.5 = (bf16[88,1024]{1,0:T(8,128)(2,1)S(1)}, bf16[88,1024]{1,0:T(8,128)(2,1)S(1)}, u32[]{:S(2)}, u32[]{:S(2)}) collective-permute-start(bf16[88,1024]{1,0:T(8,128)(2,1)S(1)} %get-tuple-element.65.own0), channel_id=1, source_target_pairs={{0,16},{16,32},{32,48},{48,0},{1,17},{17,33},{33,49},{49,1},{2,18}... | collective-permute-start | bytes 540680 | tf_op jit(solution)/shard_map/ppermute | solution.py:423
  22.2 16.3 %copy-start.1 = (f32[1024]{0:T(1024)S(1)}, f32[1024]{0:T(1024)}, u32[]{:S(2)}) copy-start(f32[1024]{0:T(1024)} %param.16) | copy-start | bytes 12292
  23.8 6.9 %collective-permute-start.4 = (bf16[88,1024]{1,0:T(8,128)(2,1)S(1)}, bf16[88,1024]{1,0:T(8,128)(2,1)S(1)}, u32[]{:S(2)}, u32[]{:S(2)}) collective-permute-start(bf16[88,1024]{1,0:T(8,128)(2,1)S(1)} %get-tuple-element.69.own1), channel_id=1, source_target_pairs={{0,48},{16,0},{32,16},{48,32},{1,49},{17,1},{33,17},{49,33},{2,50}... | collective-permute-start | bytes 540680 | tf_op jit(solution)/shard_map/ppermute | solution.py:423
  27.1 10.3 %collective-permute-start.8 = (bf16[88,1024]{1,0:T(8,128)(2,1)S(1)}, bf16[88,1024]{1,0:T(8,128)(2,1)S(1)}, u32[]{:S(2)}, u32[]{:S(2)}) collective-permute-start(bf16[88,1024]{1,0:T(8,128)(2,1)S(1)} %get-tuple-element.69.own1), channel_id=1, source_target_pairs={{0,16},{16,32},{32,48},{48,0},{1,17},{17,33},{33,49},{49,1},{2,18}... | collective-permute-start | bytes 540680 | tf_op jit(solution)/shard_map/ppermute | solution.py:423
  29.2 8.1 %collective-permute-start.9 = (bf16[88,1024]{1,0:T(8,128)(2,1)S(1)}, bf16[88,1024]{1,0:T(8,128)(2,1)S(1)}, u32[]{:S(2)}, u32[]{:S(2)}) collective-permute-start(bf16[88,1024]{1,0:T(8,128)(2,1)S(1)} %collective-permute-done.5.o10), channel_id=1, source_target_pairs={{0,16},{16,32},{32,48},{48,0},{1,17},{17,33},{33,49},{49,1},{2,18}... | collective-permute-start | bytes 540680 | tf_op jit(solution)/shard_map/ppermute | solution.py:423
  30.7 7.8 %collective-permute-start.7 = (bf16[88,1024]{1,0:T(8,128)(2,1)S(1)}, bf16[88,1024]{1,0:T(8,128)(2,1)S(1)}, u32[]{:S(2)}, u32[]{:S(2)}) collective-permute-start(bf16[88,1024]{1,0:T(8,128)(2,1)S(1)} %collective-permute-done.4.o21), channel_id=1, source_target_pairs={{0,48},{16,0},{32,16},{48,32},{1,49},{17,1},{33,17},{49,33},{2,50}... | collective-permute-start | bytes 540680 | tf_op jit(solution)/shard_map/ppermute | solution.py:423
  41.2 2.5 %collective-permute-start.10 = (bf16[256,640]{1,0:T(8,128)(2,1)S(1)}, bf16[256,640]{1,0:T(8,128)(2,1)S(1)}, u32[]{:S(2)}, u32[]{:S(2)}) collective-permute-start(bf16[256,640]{1,0:T(8,128)(2,1)S(1)} %get-tuple-element.93), channel_id=1, source_target_pairs={{0,64},{64,0},{1,65},{65,1},{2,66},{66,2},{3,67},{67,3},{4,68},{68... | collective-permute-start | bytes 983048 | tf_op jit(solution)/shard_map/ppermute | solution.py:514
  43.8 8.3 %collective-permute-start.11 = (bf16[128,640]{1,0:T(8,128)(2,1)S(1)}, bf16[128,640]{1,0:T(8,128)(2,1)S(1)}, u32[]{:S(2)}, u32[]{:S(2)}) collective-permute-start(bf16[128,640]{1,0:T(8,128)(2,1)S(1)} %get-tuple-element.97), channel_id=1, source_target_pairs={{0,48},{16,32},{32,16},{48,0},{1,49},{17,33},{33,17},{49,1},{2,50}... | collective-permute-start | bytes 491528 | tf_op jit(solution)/shard_map/ppermute | solution.py:549
  46.3 21.9 %collective-permute-start.12 = (bf16[2,256,512]{2,1,0:T(8,128)(2,1)S(1)}, bf16[2,256,512]{2,1,0:T(8,128)(2,1)S(1)}, u32[]{:S(2)}, u32[]{:S(2)}) collective-permute-start(bf16[2,256,512]{2,1,0:T(8,128)(2,1)S(1)} %get-tuple-element.108), channel_id=1, source_target_pairs={{0,1},{1,0},{2,3},{3,2},{4,5},{5,4},{6,7},{7,6},{8,9},{9,8},{10,11... | collective-permute-start | bytes 1572872 | tf_op jit(solution)/shard_map/ppermute | solution.py:553
  46.3 21.9 %collective-permute-start.13 = (bf16[2,256,512]{2,1,0:T(8,128)(2,1)S(1)}, bf16[2,256,512]{2,1,0:T(8,128)(2,1)S(1)}, u32[]{:S(2)}, u32[]{:S(2)}) collective-permute-start(bf16[2,256,512]{2,1,0:T(8,128)(2,1)S(1)} %get-tuple-element.109), channel_id=1, source_target_pairs={{0,15},{1,2},{2,1},{3,4},{4,3},{5,6},{6,5},{7,8},{8,7},{9,10},{10,... | collective-permute-start | bytes 1572872 | tf_op jit(solution)/shard_map/ppermute | solution.py:554
  52.2 4.5 %collective-permute-start.14 = (bf16[64,640]{1,0:T(8,128)(2,1)S(1)}, bf16[64,640]{1,0:T(8,128)(2,1)S(1)}, u32[]{:S(2)}, u32[]{:S(2)}) collective-permute-start(bf16[64,640]{1,0:T(8,128)(2,1)S(1)} %get-tuple-element.103), channel_id=1, source_target_pairs={{0,16},{16,0},{32,48},{48,32},{1,17},{17,1},{33,49},{49,33},{2,18}... | collective-permute-start | bytes 245768 | tf_op jit(solution)/shard_map/ppermute | solution.py:558
